TPU v7x, 256 devices: a whole 4x4x8 slice. The times are simulated.
256 devices in a mesh: gx: 32 (over z, x), gz: 8 (over y, core).
Axes of the slice: x: 4, y: 4, z: 8, core: 2. Of those that a mesh axis runs over, the one named last changes fastest.
Arguments:
- eta: float32 [1024, 512], P('gx'), may hold values from -0.6 to 0.6
- phis: float32 [1024, 512], P('gx'), may hold values from -3 to 3
- particles: float32 [8, 64, 4, 16, 128], P(None, 'gx', None, 'gz'), as said below
- cell_count: int32 [64, 4, 16], P('gx', None, 'gz'), may hold values from 16 to 128, as said below
- pair_cells: int32 [32, 8, 2, 96], P('gx', 'gz'), may hold values from 0 to 63, as said below
- pair_count: int32 [32, 8, 1], P('gx', 'gz'), may hold values from 24 to 96, as said below
Outputs:
- w_surface: float32 [1024, 512], P('gx')
- density_rate: float32 [64, 4, 16, 128], P('gx', None, 'gz')
Inputs may be any that keep to these rules, and one draw needn't show every extreme that they name: `particles`: positions lie inside their cell, cells being cubes of side 2 placed at 2 times their global index; densities lie in 0.8 to 1.2, masses in 0.05 to 0.09. `cell_count`: each device's first cell holds 128 live particles. `pair_cells`: entry 0 is an own cell index, entry 1 a neighbourhood cell index within one cell of it along every dimension; used pairs of one device are distinct. `pair_count`: the first device's list is full.
All inputs are finite; a program needn't handle non-finite values.
Results may differ from a plain program's by a relative error of at most 0.0003.
Values sent between devices are 32-bit elements; how exact they have to be, the bound alone decides.
No kernel may reach another device: no remote copies, remote signals or barrier semaphores. Data moves between devices by JAX's collectives and lax.ppermute only.
A program may use at most 64 MiB of HBM per device.

v0:
```python
import jax
import jax.numpy as jnp
from jax import lax
from jax.sharding import PartitionSpec as P

TWO_PI = 6.283185307179586
DELTA_COEF = 0.1
SOUND_SPEED = 10.0
KERNEL_COEF = -5.0 * 21.0 / (16.0 * 3.141592653589793)
EXACT = lax.Precision.HIGHEST
FIRST_KINDS = (("power", 1), ("power", 2), ("power", 3), ("slope_x", 1), ("slope_y", 1))
SECOND_KINDS = (("power", 1), ("power", 2))
THIRD_KINDS = (("power", 1),)


def passed_along(array, axis, by):
    length = lax.axis_size(axis)
    return lax.ppermute(array, axis, [(i, (i + by) % length) for i in range(length)])


def extended(array, sides, width):
    for axis, dim in sides:
        size, length = (lax.axis_size(axis), array.shape[dim])
        up = [(i, (i + 1) % size) for i in range(size - 1)]
        down = [(j, i) for i, j in up]
        last = lax.slice_in_dim(array, length - width, length, axis=dim)
        initial = lax.slice_in_dim(array, 0, width, axis=dim)
        before = lax.ppermute(last, axis, up)
        after = lax.ppermute(initial, axis, down)
        array = jnp.concatenate([before, array, after], axis=dim)
    return array


def phase_table(first_index, second_index, length):
    turn_count = first_index * second_index % length
    phase_angle = turn_count.astype(jnp.float32) * (TWO_PI / length)
    return (jnp.cos(phase_angle), jnp.sin(phase_angle))


def wave_number(position, length):
    signed = jnp.where(position < length // 2, position, position - length)
    return signed.astype(jnp.float32) * (TWO_PI / length)


def transform_rows(real_part, imag_part, direction):
    length, width = real_part.shape
    block_size = min(64, length)
    joined = jnp.concatenate([real_part, imag_part], axis=1)
    column_index = jnp.arange(length, dtype=jnp.int32)[None, :]

    def block_rows(first_row):
        row_index = first_row + jnp.arange(block_size, dtype=jnp.int32)[:, None]
        cosine_table, sine_table = phase_table(row_index, column_index, length)
        with_cos = jnp.dot(cosine_table, joined, precision=EXACT)
        with_sin = jnp.dot(sine_table, joined, precision=EXACT)
        return (
            with_cos[:, :width] + direction * with_sin[:, width:],
            with_cos[:, width:] - direction * with_sin[:, :width],
        )

    firsts = jnp.arange(length // block_size, dtype=jnp.int32) * block_size
    out_real, out_imag = lax.map(block_rows, firsts)
    return (out_real.reshape(length, width), out_imag.reshape(length, width))


def apply_filters(spec_real, spec_imag, wave_x, wave_y, kind_list):
    wave_abs = jnp.sqrt(wave_x * wave_x + wave_y * wave_y)
    real_terms = []
    imag_terms = []
    for kind_name, exponent in kind_list:
        if kind_name == "power":
            factor = wave_abs**exponent
            real_terms.append(factor * spec_real)
            imag_terms.append(factor * spec_imag)
        else:
            factor = wave_x if kind_name == "slope_x" else wave_y
            real_terms.append(-factor * spec_imag)
            imag_terms.append(factor * spec_real)
    return transform_rows(jnp.concatenate(real_terms, 1), jnp.concatenate(imag_terms, 1), -1.0)


def spectral_partial(field_rows, kind_list):
    row_count, col_total = field_rows.shape
    x_total = row_count * lax.axis_size("gx")
    col_share = col_total // lax.axis_size("gz")
    col_piece = col_share // lax.axis_size("gx")
    slab_index = lax.axis_index("gx")
    first_wave = lax.axis_index("gz") * col_share
    y_index = jnp.arange(col_total, dtype=jnp.int32)
    wave_index = first_wave + jnp.arange(col_share, dtype=jnp.int32)
    cos_forward, sin_forward = phase_table(y_index[:, None], wave_index[None, :], col_total)
    along_real = jnp.dot(field_rows, cos_forward, precision=EXACT)
    along_imag = -jnp.dot(field_rows, sin_forward, precision=EXACT)
    spread = lax.all_to_all(
        jnp.stack([along_real, along_imag], 0), "gx", split_axis=2, concat_axis=1, tiled=True
    )
    spec_real, spec_imag = transform_rows(spread[0], spread[1], 1.0)
    wave_x = wave_number(jnp.arange(x_total, dtype=jnp.int32), x_total)[:, None]
    my_waves = first_wave + slab_index * col_piece + jnp.arange(col_piece, dtype=jnp.int32)
    wave_y = wave_number(my_waves, col_total)[None, :]
    back_real, back_imag = apply_filters(spec_real, spec_imag, wave_x, wave_y, kind_list)
    count_out = len(kind_list)
    stacked = jnp.stack(
        [
            back_real.reshape(x_total, count_out, col_piece),
            back_imag.reshape(x_total, count_out, col_piece),
        ],
        0,
    )
    returned = lax.all_to_all(stacked, "gx", split_axis=1, concat_axis=3, tiled=True)
    cos_back, sin_back = phase_table(wave_index[:, None], y_index[None, :], col_total)
    flat_real = returned[0].reshape(row_count * count_out, col_share)
    flat_imag = returned[1].reshape(row_count * count_out, col_share)
    partial_sum = jnp.dot(flat_real, cos_back, precision=EXACT) - jnp.dot(
        flat_imag, sin_back, precision=EXACT
    )
    partial_sum = partial_sum * (1.0 / (x_total * col_total))
    return jnp.moveaxis(partial_sum.reshape(row_count, count_out, col_total), 1, 0)


def pair_terms(own_tiles, other_tiles):
    gap_x = own_tiles[0][:, :, None] - other_tiles[0][:, None, :]
    gap_y = own_tiles[1][:, :, None] - other_tiles[1][:, None, :]
    gap_z = own_tiles[2][:, :, None] - other_tiles[2][:, None, :]
    radius = jnp.sqrt(gap_x * gap_x + gap_y * gap_y + gap_z * gap_z)
    reach = jnp.maximum(1.0 - 0.5 * radius, 0.0)
    kernel_slope = KERNEL_COEF * reach * reach * reach
    approach = (own_tiles[3][:, :, None] - other_tiles[3][:, None, :]) * gap_x
    approach = approach + (own_tiles[4][:, :, None] - other_tiles[4][:, None, :]) * gap_y
    approach = approach + (own_tiles[5][:, :, None] - other_tiles[5][:, None, :]) * gap_z
    continuity = other_tiles[7][:, None, :] * approach
    diffusion = (
        -2.0
        * DELTA_COEF
        * SOUND_SPEED
        * (other_tiles[6][:, None, :] - own_tiles[6][:, :, None])
        * other_tiles[8][:, None, :]
    )
    return jnp.sum(kernel_slope * (continuity + diffusion), axis=2)


def per_device(eta, phis, particles, cell_count, pair_cells, pair_count):
    row_count, col_total = eta.shape

    def advance(field_rows, kind_list):
        return lax.psum(spectral_partial(field_rows, kind_list), "gz")

    first = advance(phis, FIRST_KINDS)
    phi_second = -eta * first[0]
    second = advance(phi_second, SECOND_KINDS)
    phi_third = -eta * second[0] - 0.5 * eta * eta * first[1]
    third = advance(phi_third, THIRD_KINDS)
    vertical = (
        first[0]
        + second[0]
        + eta * first[1]
        + third[0]
        + eta * second[1]
        + 0.5 * eta * eta * first[2]
    )
    surface = jnp.stack([first[3], first[4], vertical], 0)
    next_rows = passed_along(surface[:, :1, :], "gx", -1)
    table_flat = jnp.concatenate([surface, next_rows], 1).reshape(3 * (row_count + 1), col_total)
    channel_count, cells_x, cells_y, cells_z, tile_size = particles.shape
    cell_total = cells_x * cells_y * cells_z
    slab_index = lax.axis_index("gx")
    scale_x = row_count / (2.0 * cells_x)
    scale_y = col_total / (2.0 * cells_y)
    top_height = 2.0 * cells_z * lax.axis_size("gz")
    relax_reach = 4.0 * lax.axis_size("gx") * cells_x
    flat_parts = particles.reshape(channel_count, cell_total, tile_size)
    row_ids = jnp.arange(row_count + 1, dtype=jnp.int32).astype(jnp.float32)
    col_ids = jnp.arange(col_total, dtype=jnp.int32).astype(jnp.float32)
    row_offset = (slab_index * row_count).astype(jnp.float32)

    def sample_cell(cell_positions):
        local_x = cell_positions[0] * scale_x - row_offset
        hos_y = cell_positions[1] * scale_y
        gap_y = hos_y[:, None] - col_ids[None, :]
        gap_y = gap_y - col_total * jnp.floor(gap_y / col_total + 0.5)
        weight_y = jnp.maximum(0.0, 1.0 - jnp.abs(gap_y))
        along_y = jnp.dot(table_flat, weight_y.T, precision=EXACT).reshape(
            3, row_count + 1, tile_size
        )
        weight_x = jnp.maximum(0.0, 1.0 - jnp.abs(local_x[None, :] - row_ids[:, None]))
        return jnp.sum(along_y * weight_x[None], axis=1)

    targets = jnp.moveaxis(lax.map(sample_cell, jnp.moveaxis(flat_parts[:2], 1, 0)), 1, 0)
    depth_factor = jnp.exp((flat_parts[2] - top_height) / top_height)
    closeness = jnp.clip(1.0 - flat_parts[0] / relax_reach, 0.0, 1.0)
    relax_weight = closeness * closeness
    velocity = flat_parts[3:6] + relax_weight * (targets * depth_factor - flat_parts[3:6])
    slot_live = (jnp.arange(tile_size, dtype=jnp.int32) < cell_count[..., None]).reshape(
        cell_total, tile_size
    )
    mass_live = jnp.where(slot_live, flat_parts[7], 0.0)
    volume_live = jnp.where(slot_live, flat_parts[7] / flat_parts[6], 0.0)
    channels = jnp.concatenate(
        [flat_parts[0:3], velocity, flat_parts[6:7], mass_live[None], volume_live[None]], 0
    )
    channels = channels.reshape(9, cells_x, cells_y, cells_z, tile_size)
    haloed = extended(channels, (("gx", 1), ("gz", 3)), 1)
    halo_grid = haloed.reshape(9, (cells_x + 2) * cells_y * (cells_z + 2), tile_size)
    pair_list = pair_cells.reshape(2, -1)
    pair_total = pair_list.shape[1]
    used_count = pair_count.reshape(())
    own_cell = pair_list[0]
    other_cell = pair_list[1]
    own_x = own_cell // (cells_y * cells_z)
    own_y = own_cell // cells_z % cells_y
    own_z = own_cell % cells_z
    own_halo = (own_x + 1) * cells_y * (cells_z + 2) + own_y * (cells_z + 2) + own_z + 1
    group_size = pair_total // 24
    turn_total = (used_count + group_size - 1) // group_size

    def add_group(turn_index, rate_sum):
        first_pair = turn_index * group_size
        own_ids = lax.dynamic_slice_in_dim(own_cell, first_pair, group_size)
        own_halo_ids = lax.dynamic_slice_in_dim(own_halo, first_pair, group_size)
        other_ids = lax.dynamic_slice_in_dim(other_cell, first_pair, group_size)
        pair_used = first_pair + jnp.arange(group_size, dtype=jnp.int32) < used_count
        own_tiles = jnp.take(halo_grid, own_halo_ids, axis=1)
        other_tiles = jnp.take(halo_grid, other_ids, axis=1)
        terms = pair_terms(own_tiles, other_tiles) * pair_used[:, None]
        return rate_sum.at[own_ids].add(terms)

    rate_sum = lax.fori_loop(
        0, turn_total, add_group, jnp.zeros((cell_total, tile_size), jnp.float32)
    )
    density_rate = jnp.where(slot_live, rate_sum, 0.0).reshape(cells_x, cells_y, cells_z, tile_size)
    return (surface[2], density_rate)


def solution(mesh):
    in_specs = (
        P("gx", None),
        P("gx", None),
        P(None, "gx", None, "gz", None),
        P("gx", None, "gz"),
        P("gx", "gz", None, None),
        P("gx", "gz", None),
    )
    out_specs = (P("gx", None), P("gx", None, "gz", None))
    return jax.shard_map(
        per_device, mesh=mesh, in_specs=in_specs, out_specs=out_specs, check_vma=False
    )
```

profile of v0, /device:TPU:14, one launch (start us, length us, event | category | flops | bytes accessed | tf_op | source)
XLA Modules:
  0.0 848.8 jit_solution(14299295052082979115)
XLA Ops:
  11.3 11.6 %all-to-all-start = ((f32[32,1,128]{2,1,0:T(1,128)}), f32[32,1,128]{2,1,0:T(1,128)S(1)}, u32[]{:S(2)}, u32[]{:S(2)}) async-start(f32[32,1,128]{2,1,0:T(1,128)} %reshape.358), calls=%async_computation | async-start | bytes 32768 | tf_op jit(solution)/shard_map/all_to_all | solution.py:94
  23.0 7.7 all-to-all-done
  32.4 64.6 %while.112 = (s32[]{:T(128)}, f32[16,64,2]{1,0,2:T(8,128)S(1)}, f32[16,64,2]{1,0,2:T(8,128)S(1)}, s32[16]{0:T(128)S(1)}, f32[1024,4]{0,1:T(4,128)S(1)}, /*index=5*/s32[]{:T(128)}, s32[]{:T(128)}) while((s32[]{:T(128)}, f32[16,64,2]{1,0,2:T(8,128)S(1)}, f32[16,64,2]{1,0,2:T(8,128)S(1)}, s32[16]{0:T(128)S(1)}, ...), condition=%wide.region_1.2_spmd.clone, body=%wide.region_0.1_spmd.clone.sunk | while | flops 8126786 | bytes 40805 | solution.py:62
  97.4 65.9 %while.113 = (s32[]{:T(128)}, f32[16,64,10]{1,0,2:T(8,128)S(1)}, f32[16,64,10]{1,0,2:T(8,128)S(1)}, s32[16]{0:T(128)S(1)}, f32[1024,20]{0,1:T(8,128)S(1)}, /*index=5*/s32[]{:T(128)}, s32[]{:T(128)}) while((s32[]{:T(128)}, f32[16,64,10]{1,0,2:T(8,128)S(1)}, f32[16,64,10]{1,0,2:T(8,128)S(1)}, s32[16]{0:T(128)S(1)}, ...), condition=%wide.region_3.4_spmd.clone, body=%wide.region_2.3_spmd.clone.sunk | while | flops 33294912 | bytes 210789 | solution.py:62
  99.9 1.4 fusion.386
  104.0 1.4 fusion.386
  112.3 1.4 fusion.386
  116.4 1.4 fusion.386
  120.5 1.4 fusion.386
  124.6 1.4 fusion.386
  132.9 1.4 fusion.386
  137.0 1.4 fusion.386
  163.5 1.4 copy.169
  164.9 3.0 reshape.360
  167.9 13.5 %all_to_all.90 = f32[32,1,640]{2,1,0:T(1,128)S(1)} all-to-all(f32[32,1,640]{2,1,0:T(1,128)S(1)} %reshape.360), channel_id=1, replica_groups=mesh['gx'=32,'gz'=8] {'gx'}, dimensions={0} | all-to-all | bytes 163840 | tf_op jit(solution)/shard_map/all_to_all | solution.py:110
  182.2 3.1 reshape.361
  190.0 59.4 %all-reduce.4.cloned.1.call-done = f32[5,32,512]{2,1,0:T(8,128)} async-done(((f32[5,32,512]{2,1,0:T(8,128)}), f32[5,32,512]{2,1,0:T(8,128)}) %all-reduce.4.cloned.1.call-update) | async-done | bytes 327696 | tf_op jit(solution)/shard_map/psum | solution.py:146
  249.4 2.1 convolution_bitcast_fusion.2
  251.5 2.1 fusion.178
  254.4 10.1 %all-to-all-start.2 = ((f32[32,1,128]{2,1,0:T(1,128)}), f32[32,1,128]{2,1,0:T(1,128)S(1)}, u32[]{:S(2)}, u32[]{:S(2)}) async-start(f32[32,1,128]{2,1,0:T(1,128)} %reshape.362), calls=%async_computation.2 | async-start | bytes 32768 | tf_op jit(solution)/shard_map/all_to_all | solution.py:94
  265.0 7.4 all-to-all-done.2
  273.4 64.6 %while.114 = (s32[]{:T(128)}, f32[16,64,2]{1,0,2:T(8,128)S(1)}, f32[16,64,2]{1,0,2:T(8,128)S(1)}, s32[16]{0:T(128)S(1)}, f32[1024,4]{0,1:T(4,128)S(1)}, /*index=5*/s32[]{:T(128)}, s32[]{:T(128)}) while((s32[]{:T(128)}, f32[16,64,2]{1,0,2:T(8,128)S(1)}, f32[16,64,2]{1,0,2:T(8,128)S(1)}, s32[16]{0:T(128)S(1)}, ...), condition=%wide.region_6.7_spmd.clone, body=%wide.region_5.6_spmd.clone.sunk | while | flops 8126786 | bytes 40805 | solution.py:62
  338.3 64.8 %while.115 = (s32[]{:T(128)}, f32[16,64,4]{1,0,2:T(8,128)S(1)}, f32[16,64,4]{1,0,2:T(8,128)S(1)}, s32[16]{0:T(128)S(1)}, f32[1024,8]{0,1:T(8,128)S(1)}, /*index=5*/s32[]{:T(128)}, s32[]{:T(128)}) while((s32[]{:T(128)}, f32[16,64,4]{1,0,2:T(8,128)S(1)}, f32[16,64,4]{1,0,2:T(8,128)S(1)}, s32[16]{0:T(128)S(1)}, ...), condition=%wide.region_8.9_spmd.clone, body=%wide.region_7.8_spmd.clone.sunk | while | flops 14419010 | bytes 80741 | solution.py:62
  403.3 1.4 copy.180
  404.7 2.9 reshape.364
  407.6 13.1 %all_to_all.91 = f32[32,1,256]{2,1,0:T(1,128)S(1)} all-to-all(f32[32,1,256]{2,1,0:T(1,128)S(1)} %reshape.364), channel_id=1, replica_groups=mesh['gx'=32,'gz'=8] {'gx'}, dimensions={0} | all-to-all | bytes 65536 | tf_op jit(solution)/shard_map/all_to_all | solution.py:110
  421.4 3.2 reshape.365
  429.8 58.1 %all-reduce.6.cloned.1.call-done = f32[2,32,512]{2,1,0:T(8,128)} async-done(((f32[2,32,512]{2,1,0:T(8,128)}), f32[2,32,512]{2,1,0:T(8,128)}) %all-reduce.6.cloned.1.call-update) | async-done | bytes 131088 | tf_op jit(solution)/shard_map/psum | solution.py:146
  487.9 2.1 convolution_bitcast_fusion.1
  489.9 2.1 fusion.177
  492.8 10.1 %all-to-all-start.4 = ((f32[32,1,128]{2,1,0:T(1,128)}), f32[32,1,128]{2,1,0:T(1,128)S(1)}, u32[]{:S(2)}, u32[]{:S(2)}) async-start(f32[32,1,128]{2,1,0:T(1,128)} %reshape.366), calls=%async_computation.4 | async-start | bytes 32768 | tf_op jit(solution)/shard_map/all_to_all | solution.py:94
  503.2 7.6 all-to-all-done.4
  511.9 64.6 %while.116 = (s32[]{:T(128)}, f32[16,64,2]{1,0,2:T(8,128)S(1)}, f32[16,64,2]{1,0,2:T(8,128)S(1)}, s32[16]{0:T(128)S(1)}, f32[1024,4]{0,1:T(4,128)S(1)}, /*index=5*/s32[]{:T(128)}, s32[]{:T(128)}) while((s32[]{:T(128)}, f32[16,64,2]{1,0,2:T(8,128)S(1)}, f32[16,64,2]{1,0,2:T(8,128)S(1)}, s32[16]{0:T(128)S(1)}, ...), condition=%wide.region_11.12_spmd.clone, body=%wide.region_10.11_spmd.clone.sunk | while | flops 8126786 | bytes 40805 | solution.py:62
  576.8 64.7 %while.117 = (s32[]{:T(128)}, f32[16,64,2]{1,0,2:T(8,128)S(1)}, f32[16,64,2]{1,0,2:T(8,128)S(1)}, s32[16]{0:T(128)S(1)}, f32[1024,4]{0,1:T(4,128)S(1)}, /*index=5*/s32[]{:T(128)}, s32[]{:T(128)}) while((s32[]{:T(128)}, f32[16,64,2]{1,0,2:T(8,128)S(1)}, f32[16,64,2]{1,0,2:T(8,128)S(1)}, s32[16]{0:T(128)S(1)}, ...), condition=%wide.region_13.14_spmd.clone, body=%wide.region_12.13_spmd.clone.sunk | while | flops 8127042 | bytes 40805 | solution.py:62
  642.5 4.3 reduce.5
  646.8 1.4 reshape.368
  648.3 13.2 %all_to_all.92 = f32[32,1,128]{2,1,0:T(1,128)S(1)} all-to-all(f32[32,1,128]{2,1,0:T(1,128)S(1)} %reshape.368), channel_id=1, replica_groups=mesh['gx'=32,'gz'=8] {'gx'}, dimensions={0} | all-to-all | bytes 32768 | tf_op jit(solution)/shard_map/all_to_all | solution.py:110
  662.1 1.7 reshape.369
  665.3 1.4 fusion.176
  666.7 57.5 %all-reduce.8.cloned.1.call-done = f32[32,512]{1,0:T(8,128)} async-done(((f32[32,512]{1,0:T(8,128)}), f32[32,512]{1,0:T(8,128)}) %all-reduce.8.cloned.1.call-update) | async-done | bytes 65552 | tf_op jit(solution)/shard_map/psum | solution.py:146
  726.2 4.7 collective-permute-done
  731.0 11.4 %while.118 = (s32[]{:T(128)}, f32[16,3,128]{2,1,0:T(4,128)S(1)}, f32[16,2,128]{2,1,0:T(2,128)S(1)}, f32[99,512]{1,0:T(8,128)S(1)}, f32[]{:T(128)}, /*index=5*/s32[]{:T(128)}) while((s32[]{:T(128)}, f32[16,3,128]{2,1,0:T(4,128)S(1)}, f32[16,2,128]{2,1,0:T(2,128)S(1)}, f32[99,512]{1,0:T(8,128)S(1)}, f32[]{:T(128)}, ...), condition=%wide.region_17.18_spmd.clone, body=%wide.region_15.17_spmd.clone.sunk | while | flops 78489376 | bytes 454489 | solution.py:188
  742.6 1.9 collective-permute-start.1
  744.5 3.9 collective-permute-start.2
  748.5 4.0 collective-permute-done.2
  752.7 1.9 collective-permute-start.3
  754.6 3.6 collective-permute-start.4
  760.7 80.5 %while.111 = (s32[]{:T(128)}, f32[16,128]{1,0:T(8,128)S(1)}, s32[]{:T(128)}, s32[96]{0:T(128)S(1)}, s32[96]{0:T(128)S(1)}, /*index=5*/f32[9,64,128]{2,0,1:T(8,12...) while((s32[]{:T(128)}, f32[16,128]{1,0:T(8,128)S(1)}, ...), condition=%wide.region_21.23_spmd, body=%wide.region_18.22_spmd.sunk | while | flops 1847374 | bytes 267123 | solution.py:227
  (1294 shorter events, 492.0 us)
Async XLA Ops:
  7.2 0.8 copy-start
  11.3 19.4 %all-to-all-start = ((f32[32,1,128]{2,1,0:T(1,128)}), f32[32,1,128]{2,1,0:T(1,128)S(1)}, u32[]{:S(2)}, u32[]{:S(2)}) async-start(f32[32,1,128]{2,1,0:T(1,128)} %reshape.358), calls=%async_computation | async-start | bytes 32768 | tf_op jit(solution)/shard_map/all_to_all | solution.py:94
  22.9 226.5 %all-reduce.4.cloned.1.call-start = ((), (), s32[]{:S(2)}) async-start(), calls=%async_computation.6 | async-start | bytes 655360 | tf_op jit(solution)/shard_map/psum | solution.py:146
  186.4 63.0 %copy-start.5 = (f32[32,512]{1,0:T(8,128)S(1)}, f32[32,512]{1,0:T(8,128)}, u32[]{:S(2)}) copy-start(f32[32,512]{1,0:T(8,128)} %param.24) | copy-start | bytes 196612
  254.4 18.0 %all-to-all-start.2 = ((f32[32,1,128]{2,1,0:T(1,128)}), f32[32,1,128]{2,1,0:T(1,128)S(1)}, u32[]{:S(2)}, u32[]{:S(2)}) async-start(f32[32,1,128]{2,1,0:T(1,128)} %reshape.362), calls=%async_computation.2 | async-start | bytes 32768 | tf_op jit(solution)/shard_map/all_to_all | solution.py:94
  264.5 223.4 %all-reduce.6.cloned.1.call-start = ((), (), s32[]{:S(2)}) async-start(), calls=%async_computation.7 | async-start | bytes 262144 | tf_op jit(solution)/shard_map/psum | solution.py:146
  426.1 61.8 %copy-start.2 = (f32[5,32,512]{2,1,0:T(8,128)S(1)}, f32[5,32,512]{2,1,0:T(8,128)}, u32[]{:S(2)}) copy-start(f32[5,32,512]{2,1,0:T(8,128)} %all-reduce.4.cloned.1.call-done) | copy-start | bytes 983044
  492.8 18.0 %all-to-all-start.4 = ((f32[32,1,128]{2,1,0:T(1,128)}), f32[32,1,128]{2,1,0:T(1,128)S(1)}, u32[]{:S(2)}, u32[]{:S(2)}) async-start(f32[32,1,128]{2,1,0:T(1,128)} %reshape.366), calls=%async_computation.4 | async-start | bytes 32768 | tf_op jit(solution)/shard_map/all_to_all | solution.py:94
  503.0 221.2 %all-reduce.8.cloned.1.call-start = ((), (), s32[]{:S(2)}) async-start(), calls=%async_computation.8 | async-start | bytes 131072 | tf_op jit(solution)/shard_map/psum | solution.py:146
  646.8 19.9 %copy-start.3 = (f32[8,2,4,2,128]{4,3,2,1,0:T(2,128)S(1)}, f32[8,2,4,2,128]{4,3,2,1,0:T(2,128)}, u32[]{:S(2)}) copy-start(f32[8,2,4,2,128]{4,3,2,1,0:T(2,128)} %param.26) | copy-start | bytes 196612
  648.3 75.9 %copy-start.4 = (f32[2,32,512]{2,1,0:T(8,128)S(1)}, f32[2,32,512]{2,1,0:T(8,128)}, u32[]{:S(2)}) copy-start(f32[2,32,512]{2,1,0:T(8,128)} %all-reduce.6.cloned.1.call-done) | copy-start | bytes 393220
  662.1 64.0 %slice-start = ((f32[8,2,4,2,128]{4,3,2,1,0:T(2,128)}), f32[2,2,4,2,128]{4,3,2,1,0:T(2,128)S(1)}, s32[]{:S(2)}) async-start(f32[8,2,4,2,128]{4,3,2,1,0:T(2,128)} %param.26), calls=%async_computation.9 | async-start | bytes 32768 | tf_op jit(solution)/shard_map/slice | solution.py:188
  663.8 62.3 %copy-start.6 = (s32[2,4,2]{1,2,0:T(2,128)S(1)}, s32[2,4,2]{1,2,0:T(2,128)}, u32[]{:S(2)}) copy-start(s32[2,4,2]{1,2,0:T(2,128)} %param.27) | copy-start | bytes 196
  725.1 5.9 copy-start.1
  725.1 5.8 collective-permute-start
  731.0 17.5 %copy-start.7 = (s32[1,1,2,96]{3,2,1,0:T(2,128)S(1)}, s32[1,1,2,96]{3,2,1,0:T(2,128)}, u32[]{:S(2)}) copy-start(s32[1,1,2,96]{3,2,1,0:T(2,128)} %param.28) | copy-start | bytes 2308
  742.6 5.9 collective-permute-start.1
  744.5 8.0 collective-permute-start.2
  752.7 6.3 collective-permute-start.3
  754.6 5.6 collective-permute-start.4
Sparse Core Ops, SparseCore 0:
  190.1 59.2 all-reduce.3
  429.9 57.9 all-reduce.5
  666.8 57.3 all-reduce.7
where the time goes:
time: 863 us; the launch traced here: 849 us
  matrix products  279 us (32%)
  waiting for transfers between devices  208 us (24%)
  other arithmetic  131 us (15%)
  local copies, waits for them, and re-layouts  122 us (14%)
  starting transfers between devices  44.9 us (5%)
  blocking collectives  39.7 us (5%)
  between operations  15.9 us (2%)
  loops' own time  8.66 us (1%)
    psum x3, waiting for transfers between devices, advance(): return lax.psum(spectral_partial(field_rows, kind_list), 'gz')  175 us
    dot_general x96, matrix products, block_rows(): with_cos = jnp.dot(cosine_table, joined, precision=EXACT)  129 us
    dot_general x96, matrix products, block_rows(): with_sin = jnp.dot(sine_table, joined, precision=EXACT)  125 us
    add x96, other arithmetic, block_rows(): row_index = first_row + jnp.arange(block_size, dtype=jnp.int32)[:, None]  62.1 us
    dynamic_slice x96, local copies, waits for them, and re-layouts, transform_rows(): out_real, out_imag = lax.map(block_rows, firsts)  56.3 us
    all_to_all x3, blocking collectives, spectral_partial(): lax.all_to_all(stacked, 'gx', split_axis=1, concat_axis=3, tiled=True)  39.7 us
    all_to_all x3, starting transfers between devices, spectral_partial(): lax.all_to_all(jnp.stack([along_real, along_imag], 0), 'gx', split_axis=2...  31.8 us
    all_to_all x3, waiting for transfers between devices, spectral_partial(): lax.all_to_all(jnp.stack([along_real, along_imag], 0), 'gx', split_axis=2...  22.8 us
  transfers between devices with their start and end apart: 11, of which 9 were waited for; matrix products, arithmetic and copies ran while one was open for 0% of the time, Pallas kernels for 0%

commit v1 on v0

v1 whole, which is shorter than its diff:
```python
import functools

import jax
import jax.numpy as jnp
import ml_dtypes
import numpy as np
from jax import lax
from jax.experimental import pallas as pl
from jax.experimental.pallas import tpu as pltpu
from jax.sharding import PartitionSpec as P

TWO_PI = 6.283185307179586
KERNEL_COEF = -5.0 * 21.0 / (16.0 * 3.141592653589793)
NX = 1024
NY = 512
HALF = 512
ROWS = 72
F32 = jnp.float32
BF16 = jnp.bfloat16
NN = (((1,), (0,)), ((), ()))
NT = (((1,), (1,)), ((), ()))
VM = pl.BlockSpec(memory_space=pltpu.VMEM)
SM = pl.BlockSpec(memory_space=pltpu.SMEM)


def parts_of(table):
    high = table.astype(ml_dtypes.bfloat16)
    low = (table - high.astype(np.float64)).astype(ml_dtypes.bfloat16)
    return high, low


@functools.cache
def tables():
    c = np.arange(NY)
    wave = 32 * (c // 64) + c % 32
    is_sine = (c % 64) >= 32
    wave[32] = NY // 2
    is_sine[32] = False
    angle = TWO_PI / NY * ((wave[:, None] * np.arange(NY)[None, :]) % NY)
    norm = np.where((wave == 0) | (wave == NY // 2), 1.0 / NY, 2.0 / NY) ** 0.5
    basis_y = np.where(is_sine[:, None], np.sin(angle), np.cos(angle)) * norm[:, None]
    r = np.arange(HALF)
    m = r % 256
    even = 2 * m
    even[256] = NX // 2
    odd = 2 * m + 1
    wave = np.concatenate([even, odd])
    is_sine = np.concatenate([r > 256, r >= 256])
    angle = TWO_PI / NX * ((np.arange(NX)[:, None] * wave[None, :]) % NX)
    norm = np.where((wave == 0) | (wave == NX // 2), 1.0 / NX, 2.0 / NX) ** 0.5
    basis_x = np.where(is_sine[None, :], np.sin(angle), np.cos(angle)) * norm[None, :]
    n = np.arange(HALF)
    order_gz = 32 * (n % 16) + 4 * (n // 64) + n // 16 % 4
    order_gx = 32 * (n // 16 % 16) + 16 * (n // 256) + n % 16
    rows = (np.arange(NX + ROWS) - 16) % NX
    return dict(
        y=parts_of(basis_y),
        yt=parts_of(np.ascontiguousarray(basis_y.T)),
        gz=parts_of(basis_x[order_gz]),
        gx=parts_of(basis_x[order_gx]),
        own=np.concatenate(parts_of(basis_x[rows]), axis=1),
    )


def split(value):
    high = value.astype(BF16)
    return high, (value - high.astype(F32)).astype(BF16)


def dot(lhs, rhs, dims):
    return lax.dot_general(lhs, rhs, dims, preferred_element_type=F32)


def data_by_table(value, high, low, dims):
    count = value.shape[0]
    vh, vl = split(value)
    both = dot(jnp.concatenate([vh, vl], 0), high, dims)
    return both[:count] + both[count:] + dot(vh, low, dims)


def table_by_data(high, low, value):
    count = value.shape[1]
    vh, vl = split(value)
    both = dot(high, jnp.concatenate([vh, vl], 1), NN)
    return both[:, :count] + both[:, count:] + dot(low, vh, NN)


def wave_squares(ids_ref):
    share = ids_ref[1]
    c = lax.broadcasted_iota(jnp.int32, (64, NX), 0)
    r = lax.broadcasted_iota(jnp.int32, (64, NX), 1)
    ky = 32 * share + c % 32
    ky = jnp.where((share == 0) & (c == 32), NY // 2, ky)
    m = r % 256
    kx = jnp.where(r == 256, NX // 2, jnp.where(r < HALF, 2 * m, 2 * m + 1))
    kx = kx.astype(F32) * (TWO_PI / NX)
    ky = ky.astype(F32) * (TWO_PI / NY)
    return kx, ky, kx * kx + ky * ky


def to_waves(sums, gaps, high, low):
    even = data_by_table(sums, high[:, :HALF], low[:, :HALF], NN)
    odd = data_by_table(gaps, high[:, HALF:], low[:, HALF:], NN)
    return jnp.concatenate([even, odd], 1)


def low_lanes(shape):
    return lax.broadcasted_iota(jnp.int32, shape, 1) < 64


def folded_waves(got_ref, high, low):
    sums, gaps = [], []
    mask = low_lanes((64, 128))
    for j in range(4):
        first, second = got_ref[2 * j], got_ref[2 * j + 1]
        first_turned = pltpu.roll(first, 64, 1)
        second_turned = pltpu.roll(second, 64, 1)
        sums.append(jnp.where(mask, first + first_turned, second + second_turned))
        gaps.append(jnp.where(mask, first - first_turned, second_turned - second))
    return to_waves(jnp.concatenate(sums, 1), jnp.concatenate(gaps, 1), high, low)


def send_rows(waves, high, low, out_ref):
    even = data_by_table(waves[:, :HALF], high[:, :HALF], low[:, :HALF], NT)
    odd = data_by_table(waves[:, HALF:], high[:, HALF:], low[:, HALF:], NT)
    top, bottom = even + odd, even - odd
    mask = low_lanes((waves.shape[0], 128))
    for j in range(4):
        upper = top[:, 128 * j : 128 * j + 128]
        lower = bottom[:, 128 * j : 128 * j + 128]
        out_ref[2 * j] = jnp.where(mask, upper, pltpu.roll(lower, 64, 1))
        out_ref[2 * j + 1] = jnp.where(mask, pltpu.roll(upper, 64, 1), lower)


def start_kernel(ids_ref, phis_ref, eta_ref, yh_ref, yl_ref, out_ref):
    first = pl.multiple_of(64 * ids_ref[1], 64)
    high = yh_ref[pl.ds(first, 64), :]
    low = yl_ref[pl.ds(first, 64), :]
    coefs = data_by_table(phis_ref[...], high, low, NT)
    eta = eta_ref[...]
    pieces = [jnp.concatenate([coefs[:16], coefs[16:]], 1)]
    pieces += [eta[:, 128 * j : 128 * j + 128] for j in range(4)]
    block = jnp.concatenate(pieces, 0)
    out_ref[...] = jnp.broadcast_to(block[None], out_ref.shape)


def first_kernel(ids_ref, got_ref, gxh_ref, gxl_ref, gzh_ref, gzl_ref, out_ref, waves_ref):
    got = jnp.concatenate([got_ref[pl.ds(32 * a, 16), :] for a in range(32)], 0)
    turned = jnp.concatenate([got[128 * j : 128 * j + 128].T for j in range(4)], 1)
    sums = turned[:, :256] + turned[:, 256:]
    gaps = turned[:, :256] - turned[:, 256:]
    sums = jnp.concatenate([sums[:64], sums[64:]], 1)
    gaps = jnp.concatenate([gaps[:64], gaps[64:]], 1)
    waves = to_waves(sums, gaps, gxh_ref[...], gxl_ref[...])
    waves_ref[...] = waves
    kx, ky, squares = wave_squares(ids_ref)
    both = jnp.concatenate([jnp.sqrt(squares) * waves, squares * waves], 0)
    send_rows(both, gzh_ref[...], gzl_ref[...], out_ref)


def second_kernel(got_ref, eta_ref, yh_ref, yl_ref, th_ref, tl_ref, out_ref, turned_ref, curve_ref):
    turned = []
    for j in range(4):
        block = [
            eta_ref[pl.ds(512 * half + 16 + 4 * j + q, 16, stride=32), :]
            for half in range(2)
            for q in range(4)
        ]
        turned.append(jnp.concatenate(block, 0).T)
    eta = jnp.concatenate(turned, 0)
    turned_ref[...] = eta
    first = jnp.concatenate([got_ref[s, :64, :] for s in range(8)], 0)
    second = jnp.concatenate([got_ref[s, 64:, :] for s in range(8)], 0)
    fields = table_by_data(th_ref[...], tl_ref[...], jnp.concatenate([first, second], 1))
    curve_ref[...] = 0.5 * eta * fields[:, 128:]
    waves = table_by_data(yh_ref[...], yl_ref[...], -eta * fields[:, :128])
    for s in range(8):
        out_ref[s] = waves[64 * s : 64 * s + 64]


def third_kernel(ids_ref, got_ref, gzh_ref, gzl_ref, out_ref, waves_ref):
    waves = folded_waves(got_ref, gzh_ref[...], gzl_ref[...])
    waves_ref[...] = waves
    kx, ky, squares = wave_squares(ids_ref)
    send_rows(jnp.sqrt(squares) * waves, gzh_ref[...], gzl_ref[...], out_ref)


def fourth_kernel(got_ref, eta_ref, curve_ref, yh_ref, yl_ref, th_ref, tl_ref, out_ref):
    coefs = jnp.concatenate([got_ref[s] for s in range(8)], 0)
    field = table_by_data(th_ref[...], tl_ref[...], coefs)
    waves = table_by_data(yh_ref[...], yl_ref[...], -eta_ref[...] * (field + curve_ref[...]))
    for s in range(8):
        out_ref[s] = waves[64 * s : 64 * s + 64]


def fifth_kernel(ids_ref, got_ref, gzh_ref, gzl_ref, own_ref, first_ref, second_ref, out_ref):
    third = folded_waves(got_ref, gzh_ref[...], gzl_ref[...])
    first = first_ref[...]
    both = first + second_ref[...]
    kx, ky, squares = wave_squares(ids_ref)
    size = jnp.sqrt(squares)
    blocks = []
    for part in (0, HALF):
        speed = kx[:, part : part + 256]
        blocks.append(speed * first[:, part + 256 : part + HALF])
        blocks.append(-speed * first[:, part : part + 256])
    slope_x = jnp.concatenate(blocks, 1)
    speed = ky[:32]
    slope_y = jnp.concatenate([speed * first[32:], -speed * first[:32]], 0)
    fields = jnp.concatenate(
        [size * (both + third), squares * both, size * squares * first, slope_x, slope_y], 0
    )
    fh, fl = split(fields)
    oh, ol = own_ref[:, :NX], own_ref[:, NX:]
    rows = dot(oh, fh, NT) + dot(oh, fl, NT) + dot(ol, fh, NT)
    for s in range(8):
        out_ref[s] = rows


def last_kernel(
    ids_ref, pairs_ref, count_ref, got_ref, eta_ref, parts_ref, yh_ref, yl_ref,
    surface_ref, rate_ref, field_ref, target_ref, chan_ref, own_ref, sum_ref,
):
    slab = ids_ref[0]
    mask = low_lanes((ROWS, 128))
    fields = []
    for f in range(5):
        pieces = []
        lane = 128 * (f // 2)
        for j in range(4):
            first = got_ref[2 * j, :, lane : lane + 128] if f < 4 else got_ref[2 * j, :, 256:320]
            second = got_ref[2 * j + 1, :, lane : lane + 128] if f < 4 else got_ref[2 * j + 1, :, 256:320]
            if f == 4:
                pieces.append(jnp.concatenate([first, second], 1))
            elif f % 2 == 0:
                pieces.append(jnp.where(mask, first, pltpu.roll(second, 64, 1)))
            else:
                pieces.append(jnp.where(mask, pltpu.roll(first, 64, 1), second))
        fields.append(jnp.concatenate(pieces, 1))
    fields = data_by_table(jnp.concatenate(fields, 0), yh_ref[...], yl_ref[...], NN)
    eta = eta_ref[...]
    vertical = (
        fields[:ROWS]
        + eta * fields[ROWS : 2 * ROWS]
        + 0.5 * eta * eta * fields[2 * ROWS : 3 * ROWS]
    )
    surface_ref[...] = vertical[16:48]
    sampled = (fields[3 * ROWS : 4 * ROWS], fields[4 * ROWS :], vertical)
    for f in range(3):
        field_ref[2 * f] = sampled[f]
        field_ref[2 * f + 1] = pltpu.roll(sampled[f], NY - 1, 1) - sampled[f]
    row_ids = lax.broadcasted_iota(jnp.int32, (24, 128), 0).astype(F32)

    def sample(cx, carry):
        first_row = pl.multiple_of(16 * cx, 16)
        origin = (32 * slab - 16 + 16 * cx).astype(F32)
        found = [[], [], []]
        place_x = parts_ref[0, pl.ds(first_row, 16), :] * 8.0 - origin
        place_y = parts_ref[1, pl.ds(first_row, 16), :] * 64.0
        for cy in range(4):
            for cz in range(4):
                cell = 4 * cy + cz
                along = place_y[cell : cell + 1] - 128.0 * cy
                index = jnp.clip(along.astype(jnp.int32), 0, 127)
                part = along - index.astype(F32)
                index = jnp.broadcast_to(index, (24, 128))
                weight = jnp.maximum(0.0, 1.0 - jnp.abs(place_x[cell : cell + 1] - row_ids))
                weight_next = weight * part
                for f in range(3):
                    here = field_ref[2 * f, pl.ds(first_row, 24), 128 * cy : 128 * cy + 128]
                    step = field_ref[2 * f + 1, pl.ds(first_row, 24), 128 * cy : 128 * cy + 128]
                    here = jnp.take_along_axis(here, index, axis=1)
                    step = jnp.take_along_axis(step, index, axis=1)
                    found[f].append(
                        jnp.sum(weight * here + weight_next * step, axis=0, keepdims=True)
                    )
        for f in range(3):
            target_ref[f, pl.ds(first_row, 16), :] = jnp.concatenate(found[f], 0)
        return carry

    lax.fori_loop(0, 4, sample, 0)
    depth = jnp.exp((parts_ref[2] - 32.0) * (1.0 / 32.0))
    close = jnp.clip(1.0 - parts_ref[0] * (1.0 / 256.0), 0.0, 1.0)
    close = close * close
    for i in range(3):
        chan_ref[i] = parts_ref[i]
        speed = parts_ref[3 + i]
        chan_ref[3 + i] = speed + close * (target_ref[i] * depth - speed)
    chan_ref[6] = parts_ref[6]
    mass = parts_ref[7]
    chan_ref[7] = KERNEL_COEF * mass
    chan_ref[8] = (-2.0 * KERNEL_COEF) * (mass / parts_ref[6])

    def own_rows(values):
        pieces = []
        for cx in (1, 2):
            for cy in range(4):
                first = 16 * cx + 4 * cy + 1
                pieces.append(values[first : first + 2])
        return jnp.concatenate(pieces, 0)

    columns = jnp.concatenate([own_rows(chan_ref[i]) for i in range(8)], 0).T
    for i in range(7):
        for o in range(16):
            k = 16 * i + o
            own_ref[o, i] = jnp.broadcast_to(columns[:, k : k + 1], (128, 128))
    sum_ref[...] = jnp.zeros_like(sum_ref)

    def add_pair(t, carry):
        o = pairs_ref[0, t]
        cell = pairs_ref[1, t]
        other = [chan_ref[i, pl.ds(cell, 1), :] for i in range(9)]
        for piece in range(4):
            span = pl.ds(32 * piece, 32)
            gap_x = own_ref[o, 0, span, :] - other[0]
            gap_y = own_ref[o, 1, span, :] - other[1]
            gap_z = own_ref[o, 2, span, :] - other[2]
            radius = jnp.sqrt(gap_x * gap_x + gap_y * gap_y + gap_z * gap_z)
            reach = jnp.maximum(1.0 - 0.5 * radius, 0.0)
            approach = (own_ref[o, 3, span, :] - other[3]) * gap_x
            approach = approach + (own_ref[o, 4, span, :] - other[4]) * gap_y
            approach = approach + (own_ref[o, 5, span, :] - other[5]) * gap_z
            flow = other[7] * approach + (other[6] - own_ref[o, 6, span, :]) * other[8]
            sum_ref[o, span, :] += reach * reach * reach * flow
        return carry

    lax.fori_loop(0, count_ref[0], add_pair, 0)
    ones = jnp.ones((8, 384), BF16)
    rates = []
    for o in range(16):
        total = sum_ref[o]
        high, rest = split(total)
        middle, last = split(total - high.astype(F32))
        rates.append(dot(ones, jnp.concatenate([high, middle, last], 1), NT)[:1])
    rate_ref[...] = jnp.where(own_rows(mass) > 0.0, jnp.concatenate(rates, 0), 0.0)


def call(kernel, outs, in_specs, scratch=(), name=None):
    return pl.pallas_call(
        kernel,
        out_shape=[jax.ShapeDtypeStruct(s, F32) for s in outs],
        in_specs=in_specs,
        out_specs=[VM] * len(outs),
        scratch_shapes=list(scratch),
        compiler_params=pltpu.CompilerParams(vmem_limit_bytes=48 * 1024 * 1024),
        name=name,
    )


def passed(values, axis, by):
    size = lax.axis_size(axis)
    return lax.ppermute(values, axis, [(i, (i + by) % size) for i in range(size)])


def swap(block, axis):
    return lax.all_to_all(block, axis, split_axis=0, concat_axis=0, tiled=True)


def per_device(eta, phis, particles, cell_count, pair_cells, pair_count):
    slab = lax.axis_index("gx")
    layer = lax.axis_index("gz")
    ids = jnp.stack([slab, layer]).astype(jnp.int32)
    table = tables()
    yh, yl = (jnp.asarray(t) for t in table["y"])
    th, tl = (jnp.asarray(t) for t in table["yt"])
    gzh, gzl = (jnp.asarray(t) for t in table["gz"])
    gxh, gxl = (jnp.asarray(t) for t in table["gx"])
    own = lax.dynamic_slice(jnp.asarray(table["own"]), (32 * slab, 0), (ROWS, 2 * NX))

    live = jnp.arange(128, dtype=jnp.int32) < cell_count[..., None]
    mass = jnp.where(live, particles[7], 0.0)
    cells = jnp.concatenate([particles[:7], mass[None]], 0)
    eta_before = passed(eta[16:], "gx", 1)
    eta_after = passed(eta[:24], "gx", -1)
    cells_before = passed(cells[:, 1:], "gx", 1)
    cells_after = passed(cells[:, :1], "gx", -1)
    cells = jnp.concatenate([cells_before, cells, cells_after], 1)
    below = passed(cells[:, :, :, 1:], "gz", 1)
    above = passed(cells[:, :, :, :1], "gz", -1)
    cells = jnp.concatenate([below, cells, above], 3)
    at_x = 2 * slab - 1 + jnp.arange(4, dtype=jnp.int32)
    at_z = 2 * layer - 1 + jnp.arange(4, dtype=jnp.int32)
    inside_x = (at_x >= 0) & (at_x < 64)
    inside_z = (at_z >= 0) & (at_z < 16)
    inside = (inside_x[:, None] & inside_z[None, :])[:, None, :, None]
    inside = inside | (jnp.arange(8) < 7)[:, None, None, None, None]
    cells = jnp.where(inside, cells, 0.0).reshape(8, 64, 128)
    eta_rows = jnp.concatenate([eta_before, eta, eta_after], 0)

    eta_part = lax.dynamic_slice(eta, (4 * layer, 0), (4, NY))
    (block,) = call(start_kernel, [(32, 32, 128)], [SM, VM, VM, VM, VM], name="start")(
        ids, phis, eta_part, yh, yl
    )
    gathered = swap(block, "gx").reshape(1024, 128)
    block, first = call(
        first_kernel, [(8, 128, 128), (64, NX)], [SM] + [VM] * 5, name="first"
    )(ids, gathered, gxh, gxl, gzh, gzl)
    got = swap(block, "gz")
    block, eta_turned, curve = call(
        second_kernel, [(8, 64, 128), (NY, 128), (NY, 128)], [VM] * 6, name="second"
    )(got, gathered, yh, yl, th, tl)
    got = swap(block, "gz")
    block, second = call(
        third_kernel, [(8, 64, 128), (64, NX)], [SM] + [VM] * 3, name="third"
    )(ids, got, gzh, gzl)
    got = swap(block, "gz")
    (block,) = call(fourth_kernel, [(8, 64, 128)], [VM] * 7, name="fourth")(
        got, eta_turned, curve, yh, yl, th, tl
    )
    got = swap(block, "gz")
    (block,) = call(fifth_kernel, [(8, ROWS, 320)], [SM] + [VM] * 6, name="fifth")(
        ids, got, gzh, gzl, own, first, second
    )
    got = swap(block, "gz")
    surface, rate = call(
        last_kernel,
        [(32, NY), (16, 128)],
        [SM, SM, SM] + [VM] * 5,
        [
            pltpu.VMEM((6, ROWS, NY), F32),
            pltpu.VMEM((3, 64, 128), F32),
            pltpu.VMEM((9, 64, 128), F32),
            pltpu.VMEM((16, 7, 128, 128), F32),
            pltpu.VMEM((16, 128, 128), F32),
        ],
        name="last",
    )(ids, pair_cells.reshape(2, 96), pair_count.reshape(1), got, eta_rows, cells, yh, yl)
    return surface, rate.reshape(2, 4, 2, 128)


def solution(mesh):
    in_specs = (
        P("gx", None),
        P("gx", None),
        P(None, "gx", None, "gz", None),
        P("gx", None, "gz"),
        P("gx", "gz", None, None),
        P("gx", "gz", None),
    )
    out_specs = (P("gx", None), P("gx", None, "gz", None))
    return jax.shard_map(
        per_device, mesh=mesh, in_specs=in_specs, out_specs=out_specs, check_vma=False
    )
```

time: 863 us -> 149 us (0.17)
  the two profiles are of different devices: /device:TPU:14 before, /device:TPU:0 now
where the time goes in v1:
time: 149 us; the launch traced here: 147 us
  starting transfers between devices  30.6 us (21%)
  waiting for transfers between devices  28.9 us (19%)
  local copies, waits for them, and re-layouts  28.5 us (19%)
  blocking collectives  27.1 us (18%)
  Pallas kernels  26.3 us (18%)
  other arithmetic  4.39 us (3%)
  between operations  1.55 us (1%)
    all_to_all x1, blocking collectives, swap(): return lax.all_to_all(block, axis, split_axis=0, concat_axis=0, tiled=True)  27.1 us
    unnamed x71, local copies, waits for them, and re-layouts  23.8 us
    all_to_all x5, starting transfers between devices, swap(): return lax.all_to_all(block, axis, split_axis=0, concat_axis=0, tiled=True)  20.3 us
    all_to_all x5, waiting for transfers between devices, swap(): return lax.all_to_all(block, axis, split_axis=0, concat_axis=0, tiled=True)  19.6 us
    pallas_call x1, Pallas kernels, per_device(): call(last_kernel, [(32, NY), (16, 128)], [SM, SM, SM] + [VM] * 5, [pltpu....  15.3 us
    ppermute x6, starting transfers between devices, passed(): lax.ppermute(values, axis, [(i, (i + by) % size) for i in range(size)])  10.3 us
    ppermute x6, waiting for transfers between devices, passed(): lax.ppermute(values, axis, [(i, (i + by) % size) for i in range(size)])  9.31 us
  transfers between devices with their start and end apart: 11, of which 5 were waited for; matrix products, arithmetic and copies ran while one was open for 6% of the time, Pallas kernels for 6%

profile of v1, /device:TPU:0, one launch (start us, length us, event | category | flops | bytes accessed | tf_op | source)
XLA Modules:
  0.0 147.3 jit_solution(7958888196049118664)
XLA Ops:
  0.6 0.7 constant_dynamic-slice_fusion.1.eta_ref
  1.5 1.0 copy-done.4
  2.5 1.0 copy-done.6
  3.5 0.8 copy-done.29
  4.4 0.8 start.1
  5.2 27.1 %all_to_all.30 = f32[32,32,128]{2,1,0:T(8,128)S(1)} all-to-all(f32[32,32,128]{2,1,0:T(8,128)S(1)} %start.1), channel_id=1, replica_groups=mesh['gx'=32,'gz'=8] {'gx'}, dimensions={0} | all-to-all | bytes 1048576 | tf_op jit(solution)/shard_map/all_to_all | solution.py:356
  32.3 1.4 copy-done
  33.7 1.2 copy-done.2
  34.9 1.2 copy-done.15
  36.2 1.2 copy-done.16
  37.4 1.9 %first.1 = (f32[8,128,128]{2,1,0:T(8,128)S(1)}, f32[64,1024]{1,0:T(8,128)S(1)}) custom-call(s32[2]{0:T(128)S(1)} %pad_add_fusion.ids_ref, f32[1024,128]{1,0:T(8,128)S(1)} %bitcast.9, bf16[512,1024]{1,0:T(8,128)(2,1)S(1)} %copy-done.15, bf16[512,1024]{1,0:T(8,128)(2,1)S(1)} %copy-done.16, bf16[512,1024]{1,0:T(8,128)(2,1)S(1)} %copy-done, ...), custom_call_target="tpu_custom_call" | custom-call | tf_op jit(solution)/shard_map/first/pallas_call | solution.py:395
  39.4 0.8 copy-done.18
  40.8 4.5 %all-to-all-start.1 = ((f32[8,128,128]{2,1,0:T(8,128)}), f32[8,128,128]{2,1,0:T(8,128)}, u32[]{:S(2)}, u32[]{:S(2)}) async-start(f32[8,128,128]{2,1,0:T(8,128)} %copy-done.18), calls=%async_computation.1 | async-start | bytes 1048576 | tf_op jit(solution)/shard_map/all_to_all | solution.py:356
  46.2 0.9 collective-permute-start.2
  47.1 4.4 %collective-permute-start.3 = (f32[8,1,4,2,128]{4,3,2,1,0:T(2,128)}, f32[8,1,4,2,128]{4,3,2,1,0:T(2,128)}, u32[]{:S(2)}, u32[]{:S(2)}) collective-permute-start(f32[8,1,4,2,128]{4,3,2,1,0:T(2,128)} %get-tuple-element.23), channel_id=1, source_target_pairs={{0,248},{8,0},{16,8},{24,16},{32,24},{40,32},{48,40},{56,48},{64,5... | collective-permute-start | bytes 98312 | tf_op jit(solution)/shard_map/ppermute | solution.py:352
  52.8 2.0 %collective-permute-start = (f32[16,512]{1,0:T(8,128)}, f32[16,512]{1,0:T(8,128)}, u32[]{:S(2)}, u32[]{:S(2)}) collective-permute-start(f32[16,512]{1,0:T(8,128)} %slice.24), channel_id=1, source_target_pairs={{0,8},{8,16},{16,24},{24,32},{32,40},{40,48},{48,56},{56,64},{64,7... | collective-permute-start | bytes 98312 | tf_op jit(solution)/shard_map/ppermute | solution.py:352
  54.8 1.0 all-to-all-done.1.got_ref
  55.8 1.0 copy-done.9
  56.8 1.0 copy-done.11
  57.9 1.0 copy-done.13
  58.9 2.5 %second.1 = (f32[8,64,128]{2,1,0:T(8,128)S(1)}, f32[512,128]{1,0:T(8,128)S(1)}, f32[512,128]{1,0:T(8,128)S(1)}) custom-call(f32[8,128,128]{2,1,0:T(8,128)} %all-to-all-done.1.got_ref, f32[1024,128]{1,0:T(8,128)S(1)} %bitcast.10, bf16[512,512]{1,0:T(8,128)(2,1)S(1)} %copy-done.5, bf16[512,512]{1,0:T(8,128)(2,1)S(1)} %copy-done.7, ...), custom_call_target="tpu_custom_call" | custom-call | tf_op jit(solution)/shard_map/second/pallas_call | solution.py:399
  61.4 0.7 copy-done.23
  63.5 3.8 %all-to-all-start.2 = ((f32[8,64,128]{2,1,0:T(8,128)}), f32[8,64,128]{2,1,0:T(8,128)S(1)}, u32[]{:S(2)}, u32[]{:S(2)}) async-start(f32[8,64,128]{2,1,0:T(8,128)} %copy-done.27), calls=%async_computation.2 | async-start | bytes 524288 | tf_op jit(solution)/shard_map/all_to_all | solution.py:356
  67.4 7.5 %all-to-all-done.2.got_ref = f32[8,64,128]{2,1,0:T(8,128)S(1)} async-done(((f32[8,64,128]{2,1,0:T(8,128)}), f32[8,64,128]{2,1,0:T(8,128)S(1)}, u32[]{:S(2)}, u32[]{:S(2)}) %all-to-all-start.2) | async-done | bytes 262176 | tf_op jit(solution)/shard_map/all_to_all | solution.py:356
  74.8 1.9 %third.1 = (f32[8,64,128]{2,1,0:T(8,128)S(1)}, f32[64,1024]{1,0:T(8,128)S(1)}) custom-call(s32[2]{0:T(128)S(1)} %pad_add_fusion.ids_ref, f32[8,64,128]{2,1,0:T(8,128)S(1)} %all-to-all-done.2.got_ref, bf16[512,1024]{1,0:T(8,128)(2,1)S(1)} %copy-done.1, bf16[512,1024]{1,0:T(8,128)(2,1)S(1)} %copy-done.3), custom_call_target="tpu_custom_call" | custom-call | tf_op jit(solution)/shard_map/third/pallas_call | solution.py:403
  77.4 0.7 copy-done.28
  78.1 4.0 %all-to-all-start.3 = ((f32[8,64,128]{2,1,0:T(8,128)}), f32[8,64,128]{2,1,0:T(8,128)}, u32[]{:S(2)}, u32[]{:S(2)}) async-start(f32[8,64,128]{2,1,0:T(8,128)} %copy-done.28), calls=%async_computation.3 | async-start | bytes 524288 | tf_op jit(solution)/shard_map/all_to_all | solution.py:356
  82.2 1.0 constant_dynamic-slice_fusion.own_ref
  83.2 6.5 %all-to-all-done.3.got_ref = f32[8,64,128]{2,1,0:T(8,128)} async-done(((f32[8,64,128]{2,1,0:T(8,128)}), f32[8,64,128]{2,1,0:T(8,128)}, u32[]{:S(2)}, u32[]{:S(2)}) %all-to-all-start.3) | async-done | bytes 262176 | tf_op jit(solution)/shard_map/all_to_all | solution.py:356
  89.7 1.0 copy-done.12
  90.8 1.0 copy-done.14
  91.8 0.9 copy-done.24
  92.7 0.9 copy-done.26
  93.7 1.7 %fourth.1 = f32[8,64,128]{2,1,0:T(8,128)S(1)} custom-call(f32[8,64,128]{2,1,0:T(8,128)} %all-to-all-done.3.got_ref, f32[512,128]{1,0:T(8,128)S(1)} %copy-done.24, f32[512,128]{1,0:T(8,128)S(1)} %copy-done.26, bf16[512,512]{1,0:T(8,128)(2,1)S(1)} %copy-done.5, bf16[512,512]{1,0:T(8,128)(2,1)S(1)} %copy-done.7, bf16[512,512]{1,0:T(8,128)(2,1)S(1)} %copy-done.12, ...), custom_call_target="tpu_custom_call" | custom-call | tf_op jit(solution)/shard_map/fourth/pallas_call | solution.py:407
  96.1 4.2 %all-to-all-start.4 = ((f32[8,64,128]{2,1,0:T(8,128)}), f32[8,64,128]{2,1,0:T(8,128)}, u32[]{:S(2)}, u32[]{:S(2)}) async-start(f32[8,64,128]{2,1,0:T(8,128)} %copy-done.17), calls=%async_computation.4 | async-start | bytes 524288 | tf_op jit(solution)/shard_map/all_to_all | solution.py:356
  101.7 1.5 pad_maximum_fusion.2
  103.2 4.6 %all-to-all-done.4.got_ref = f32[8,64,128]{2,1,0:T(8,128)} async-done(((f32[8,64,128]{2,1,0:T(8,128)}), f32[8,64,128]{2,1,0:T(8,128)}, u32[]{:S(2)}, u32[]{:S(2)}) %all-to-all-start.4) | async-done | bytes 262176 | tf_op jit(solution)/shard_map/all_to_all | solution.py:356
  107.9 0.9 copy-done.20
  108.8 0.9 copy-done.22
  109.8 2.2 %fifth.1 = f32[8,72,320]{2,1,0:T(8,128)S(1)} custom-call(s32[2]{0:T(128)S(1)} %pad_add_fusion.ids_ref, f32[8,64,128]{2,1,0:T(8,128)} %all-to-all-done.4.got_ref, bf16[512,1024]{1,0:T(8,128)(2,1)S(1)} %copy-done.1, bf16[512,1024]{1,0:T(8,128)(2,1)S(1)} %copy-done.3, bf16[72,2048]{1,0:T(8,128)(2,1)S(1)} %constant_dynamic-slice_fusion.own_ref, ...), custom_call_target="tpu_custom_call" | custom-call | tf_op jit(solution)/shard_map/fifth/pallas_call | solution.py:411
  111.9 0.9 copy-done.10
  112.9 3.7 %all-to-all-start.5 = ((f32[8,72,320]{2,1,0:T(8,128)}), f32[8,72,320]{2,1,0:T(8,128)S(1)}, u32[]{:S(2)}, u32[]{:S(2)}) async-start(f32[8,72,320]{2,1,0:T(8,128)} %copy-done.10), calls=%async_computation.5 | async-start | bytes 1769472 | tf_op jit(solution)/shard_map/all_to_all | solution.py:356
  116.6 1.1 fusion.1
  118.0 2.7 %collective-permute-start.5 = (f32[8,4,4,1,128]{4,3,2,1,0:T(1,128)S(1)}, f32[8,4,4,1,128]{4,3,2,1,0:T(1,128)S(1)}, u32[]{:S(2)}, u32[]{:S(2)}) collective-permute-start(f32[8,4,4,1,128]{4,3,2,1,0:T(1,128)S(1)} %get-tuple-element.21), channel_id=1, source_target_pairs={{0,7},{1,0},{2,1},{3,2},{4,3},{5,4},{6,5},{7,6},{8,15},{9,8},{10,9... | collective-permute-start | bytes 196616 | tf_op jit(solution)/shard_map/ppermute | solution.py:352
  120.7 0.9 pad_maximum_fusion.1.eta_ref
  121.6 9.3 %collective-permute-done.4 = f32[8,4,4,1,128]{4,3,2,1,0:T(1,128)S(1)} collective-permute-done((f32[8,4,4,1,128]{4,3,2,1,0:T(1,128)S(1)}, f32[8,4,4,1,128]{4,3,2,1,0:T(1,128)S(1)}, u32[]{:S(2)}, u32[]{:S(2)}) %collective-permute-start.4) | collective-permute-done | bytes 65568 | tf_op jit(solution)/shard_map/ppermute | solution.py:352
  130.9 0.9 pad_maximum_fusion
  132.0 15.3 %last.1 = (f32[32,512]{1,0:T(8,128)}, f32[16,128]{1,0:T(8,128)}) custom-call(s32[2]{0:T(128)S(1)} %pad_add_fusion.ids_ref, s32[2,96]{1,0:T(2,128)S(1)} %bitcast.11, s32[1]{0:T(128)} %bitcast.8.count_ref, f32[8,72,320]{2,1,0:T(8,128)S(1)} %all-to-all-done.5.got_ref, f32[72,512]{1,0:T(8,128)S(1)} %pad_maximum_fusion.1.eta_ref, ...), custom_call_target="tpu_custom_call" | custom-call | tf_op jit(solution)/shard_map/last/pallas_call | solution.py:415
  (72 shorter events, 6.9 us)
Async XLA Ops:
  0.6 44.7 %copy-start.34 = (s32[2,4,2]{1,2,0:T(2,128)S(1)}, s32[2,4,2]{1,2,0:T(2,128)}, u32[]{:S(2)}) copy-start(s32[2,4,2]{1,2,0:T(2,128)} %param.18) | copy-start | bytes 196
  1.4 1.0 copy-start.4
  2.5 1.0 copy-start.6
  3.5 0.8 copy-start.29
  4.4 40.9 %copy-start.32 = (f32[8,2,4,2,128]{4,3,2,1,0:T(2,128)S(1)}, f32[8,2,4,2,128]{4,3,2,1,0:T(2,128)}, u32[]{:S(2)}) copy-start(f32[8,2,4,2,128]{4,3,2,1,0:T(2,128)} %param.17) | copy-start | bytes 196612
  4.4 47.1 %copy-start.31 = (f32[32,512]{1,0:T(8,128)S(1)}, f32[32,512]{1,0:T(8,128)}, u32[]{:S(2)}) copy-start(f32[32,512]{1,0:T(8,128)} %param.15) | copy-start | bytes 196612
  4.4 51.4 %copy-start.5 = (bf16[512,512]{1,0:T(8,128)(2,1)S(1)}, bf16[512,512]{1,0:T(8,128)(2,1)}, u32[]{:S(2)}) copy-start(bf16[512,512]{1,0:T(8,128)(2,1)} %constant.50.clone.yh_ref) | copy-start | bytes 1572868
  4.4 51.4 %copy-start.7 = (bf16[512,512]{1,0:T(8,128)(2,1)S(1)}, bf16[512,512]{1,0:T(8,128)(2,1)}, u32[]{:S(2)}) copy-start(bf16[512,512]{1,0:T(8,128)(2,1)} %constant.51.clone.yl_ref) | copy-start | bytes 1572868
  32.3 7.0 %copy-start.8 = (f32[32,32,128]{2,1,0:T(8,128)}, f32[32,32,128]{2,1,0:T(8,128)S(1)}, u32[]{:S(2)}) copy-start(f32[32,32,128]{2,1,0:T(8,128)S(1)} %all_to_all.30) | copy-start | bytes 1572868
  32.3 1.4 copy-start
  33.7 1.2 copy-start.2
  34.9 1.2 copy-start.15
  36.2 1.2 copy-start.16
  37.4 37.5 %copy-start.1 = (bf16[512,1024]{1,0:T(8,128)(2,1)S(1)}, bf16[512,1024]{1,0:T(8,128)(2,1)}, u32[]{:S(2)}) copy-start(bf16[512,1024]{1,0:T(8,128)(2,1)} %constant.54.clone.gzh_ref) | copy-start | bytes 3145732
  37.4 37.5 %copy-start.3 = (bf16[512,1024]{1,0:T(8,128)(2,1)S(1)}, bf16[512,1024]{1,0:T(8,128)(2,1)}, u32[]{:S(2)}) copy-start(bf16[512,1024]{1,0:T(8,128)(2,1)} %constant.55.clone.gzl_ref) | copy-start | bytes 3145732
  39.4 0.8 copy-start.18
  40.1 0.7 copy-start.19
  40.8 14.9 %all-to-all-start.1 = ((f32[8,128,128]{2,1,0:T(8,128)}), f32[8,128,128]{2,1,0:T(8,128)}, u32[]{:S(2)}, u32[]{:S(2)}) async-start(f32[8,128,128]{2,1,0:T(8,128)} %copy-done.18), calls=%async_computation.1 | async-start | bytes 1048576 | tf_op jit(solution)/shard_map/all_to_all | solution.py:356
  46.2 55.6 %collective-permute-start.2 = (f32[8,1,4,2,128]{4,3,2,1,0:T(2,128)}, f32[8,1,4,2,128]{4,3,2,1,0:T(2,128)S(1)}, u32[]{:S(2)}, u32[]{:S(2)}) collective-permute-start(f32[8,1,4,2,128]{4,3,2,1,0:T(2,128)} %get-tuple-element.22), channel_id=1, source_target_pairs={{0,8},{8,16},{16,24},{24,32},{32,40},{40,48},{48,56},{56,64},{64,7... | collective-permute-start | bytes 98312 | tf_op jit(solution)/shard_map/ppermute | solution.py:352
  47.1 54.7 %collective-permute-start.3 = (f32[8,1,4,2,128]{4,3,2,1,0:T(2,128)}, f32[8,1,4,2,128]{4,3,2,1,0:T(2,128)}, u32[]{:S(2)}, u32[]{:S(2)}) collective-permute-start(f32[8,1,4,2,128]{4,3,2,1,0:T(2,128)} %get-tuple-element.23), channel_id=1, source_target_pairs={{0,248},{8,0},{16,8},{24,16},{32,24},{40,32},{48,40},{56,48},{64,5... | collective-permute-start | bytes 98312 | tf_op jit(solution)/shard_map/ppermute | solution.py:352
  52.1 68.6 %collective-permute-start.1 = (f32[24,512]{1,0:T(8,128)}, f32[24,512]{1,0:T(8,128)}, u32[]{:S(2)}, u32[]{:S(2)}) collective-permute-start(f32[24,512]{1,0:T(8,128)} %slice.25), channel_id=1, source_target_pairs={{0,248},{8,0},{16,8},{24,16},{32,24},{40,32},{48,40},{56,48},{64,5... | collective-permute-start | bytes 147464 | tf_op jit(solution)/shard_map/ppermute | solution.py:352
  52.8 67.9 %collective-permute-start = (f32[16,512]{1,0:T(8,128)}, f32[16,512]{1,0:T(8,128)}, u32[]{:S(2)}, u32[]{:S(2)}) collective-permute-start(f32[16,512]{1,0:T(8,128)} %slice.24), channel_id=1, source_target_pairs={{0,8},{8,16},{16,24},{24,32},{32,40},{40,48},{48,56},{56,64},{64,7... | collective-permute-start | bytes 98312 | tf_op jit(solution)/shard_map/ppermute | solution.py:352
  55.8 1.0 copy-start.9
  56.8 1.0 copy-start.11
  57.9 1.0 copy-start.13
  61.4 0.7 copy-start.23
  62.1 0.7 copy-start.25
  62.8 0.7 copy-start.27
  63.5 11.4 %all-to-all-start.2 = ((f32[8,64,128]{2,1,0:T(8,128)}), f32[8,64,128]{2,1,0:T(8,128)S(1)}, u32[]{:S(2)}, u32[]{:S(2)}) async-start(f32[8,64,128]{2,1,0:T(8,128)} %copy-done.27), calls=%async_computation.2 | async-start | bytes 524288 | tf_op jit(solution)/shard_map/all_to_all | solution.py:356
  76.7 0.7 copy-start.21
  77.4 0.7 copy-start.28
  78.1 11.6 %all-to-all-start.3 = ((f32[8,64,128]{2,1,0:T(8,128)}), f32[8,64,128]{2,1,0:T(8,128)}, u32[]{:S(2)}, u32[]{:S(2)}) async-start(f32[8,64,128]{2,1,0:T(8,128)} %copy-done.28), calls=%async_computation.3 | async-start | bytes 524288 | tf_op jit(solution)/shard_map/all_to_all | solution.py:356
  89.7 1.0 copy-start.12
  90.8 1.0 copy-start.14
  91.8 0.9 copy-start.24
  92.7 0.9 copy-start.26
  95.4 0.7 copy-start.17
  96.1 35.9 %copy-start.30 = (s32[1,1,2,96]{3,2,1,0:T(2,128)S(1)}, s32[1,1,2,96]{3,2,1,0:T(2,128)}, u32[]{:S(2)}) copy-start(s32[1,1,2,96]{3,2,1,0:T(2,128)} %param.19) | copy-start | bytes 2308
  96.1 11.7 %all-to-all-start.4 = ((f32[8,64,128]{2,1,0:T(8,128)}), f32[8,64,128]{2,1,0:T(8,128)}, u32[]{:S(2)}, u32[]{:S(2)}) async-start(f32[8,64,128]{2,1,0:T(8,128)} %copy-done.17), calls=%async_computation.4 | async-start | bytes 524288 | tf_op jit(solution)/shard_map/all_to_all | solution.py:356
  101.1 30.8 %copy-start.33 = (pred[8,64]{1,0:T(8,128)(4,1)S(1)}, pred[8,64]{1,0:T(8,128)(4,1)}, u32[]{:S(2)}) copy-start(pred[8,64]{1,0:T(8,128)(4,1)} %copy.18) | copy-start | bytes 1540
  107.9 1.0 copy-start.20
  108.8 0.9 copy-start.22
  111.9 1.0 copy-start.10
  112.9 19.1 %all-to-all-start.5 = ((f32[8,72,320]{2,1,0:T(8,128)}), f32[8,72,320]{2,1,0:T(8,128)S(1)}, u32[]{:S(2)}, u32[]{:S(2)}) async-start(f32[8,72,320]{2,1,0:T(8,128)} %copy-done.10), calls=%async_computation.5 | async-start | bytes 1769472 | tf_op jit(solution)/shard_map/all_to_all | solution.py:356
  117.7 13.2 %collective-permute-start.4 = (f32[8,4,4,1,128]{4,3,2,1,0:T(1,128)S(1)}, f32[8,4,4,1,128]{4,3,2,1,0:T(1,128)S(1)}, u32[]{:S(2)}, u32[]{:S(2)}) collective-permute-start(f32[8,4,4,1,128]{4,3,2,1,0:T(1,128)S(1)} %get-tuple-element.20), channel_id=1, source_target_pairs={{0,1},{1,2},{2,3},{3,4},{4,5},{5,6},{6,7},{7,0},{8,9},{9,10},{10,1... | collective-permute-start | bytes 196616 | tf_op jit(solution)/shard_map/ppermute | solution.py:352
  118.0 12.9 %collective-permute-start.5 = (f32[8,4,4,1,128]{4,3,2,1,0:T(1,128)S(1)}, f32[8,4,4,1,128]{4,3,2,1,0:T(1,128)S(1)}, u32[]{:S(2)}, u32[]{:S(2)}) collective-permute-start(f32[8,4,4,1,128]{4,3,2,1,0:T(1,128)S(1)} %get-tuple-element.21), channel_id=1, source_target_pairs={{0,7},{1,0},{2,1},{3,2},{4,3},{5,4},{6,5},{7,6},{8,15},{9,8},{10,9... | collective-permute-start | bytes 196616 | tf_op jit(solution)/shard_map/ppermute | solution.py:352

commit v2 on v1

v2 whole, which is shorter than its diff:
```python
import functools

import jax
import jax.numpy as jnp
import ml_dtypes
import numpy as np
from jax import lax
from jax.experimental import pallas as pl
from jax.experimental.pallas import tpu as pltpu
from jax.sharding import PartitionSpec as P

TWO_PI = 6.283185307179586
KERNEL_COEF = -5.0 * 21.0 / (16.0 * 3.141592653589793)
NX = 1024
NY = 512
HALF = 512
ROWS = 72
F32 = jnp.float32
BF16 = jnp.bfloat16
NN = (((1,), (0,)), ((), ()))
NT = (((1,), (1,)), ((), ()))
VM = pl.BlockSpec(memory_space=pltpu.VMEM)
SM = pl.BlockSpec(memory_space=pltpu.SMEM)
HB = pl.BlockSpec(memory_space=pltpu.HBM)
GROUP = 8


def parts_of(table):
    high = table.astype(ml_dtypes.bfloat16)
    low = (table - high.astype(np.float64)).astype(ml_dtypes.bfloat16)
    return high, low


@functools.cache
def tables():
    c = np.arange(NY)
    wave = 32 * (c // 64) + c % 32
    is_sine = (c % 64) >= 32
    wave[32] = NY // 2
    is_sine[32] = False
    angle = TWO_PI / NY * ((wave[:, None] * np.arange(NY)[None, :]) % NY)
    norm = np.where((wave == 0) | (wave == NY // 2), 1.0 / NY, 2.0 / NY) ** 0.5
    basis_y = np.where(is_sine[:, None], np.sin(angle), np.cos(angle)) * norm[:, None]
    r = np.arange(HALF)
    m = r % 256
    even = 2 * m
    even[256] = NX // 2
    odd = 2 * m + 1
    wave = np.concatenate([even, odd])
    is_sine = np.concatenate([r > 256, r >= 256])
    angle = TWO_PI / NX * ((np.arange(NX)[:, None] * wave[None, :]) % NX)
    norm = np.where((wave == 0) | (wave == NX // 2), 1.0 / NX, 2.0 / NX) ** 0.5
    basis_x = np.where(is_sine[None, :], np.sin(angle), np.cos(angle)) * norm[None, :]
    n = np.arange(HALF)
    order_gz = 32 * (n % 16) + 4 * (n // 64) + n // 16 % 4
    rows = (np.arange(NX + ROWS) - 16) % NX
    yh, yl = parts_of(basis_y)
    xh, xl = parts_of(basis_x[order_gz])
    return dict(
        y=np.stack([yh, yl]),
        x=np.stack([xh[:, :HALF], xh[:, HALF:], xl[:, :HALF], xl[:, HALF:]]),
        own=np.concatenate(parts_of(basis_x[rows]), axis=1),
    )


def split(value):
    high = value.astype(BF16)
    return high, (value - high.astype(F32)).astype(BF16)


def dot(lhs, rhs, dims):
    return lax.dot_general(lhs, rhs, dims, preferred_element_type=F32)


def data_by_table(value, high, low, dims):
    count = value.shape[0]
    vh, vl = split(value)
    both = dot(jnp.concatenate([vh, vl], 0), high, dims)
    return both[:count] + both[count:] + dot(vh, low, dims)


def table_by_data(high, low, value):
    count = value.shape[0]
    vh, vl = split(value)
    both = dot(high, jnp.concatenate([vh, vl], 0), NT)
    return both[:, :count] + both[:, count:] + dot(low, vh, NT)


def wave_squares(ids_ref):
    share = ids_ref[1]
    c = lax.broadcasted_iota(jnp.int32, (64, NX), 0)
    r = lax.broadcasted_iota(jnp.int32, (64, NX), 1)
    ky = 32 * share + c % 32
    ky = jnp.where((share == 0) & (c == 32), NY // 2, ky)
    m = r % 256
    kx = jnp.where(r == 256, NX // 2, jnp.where(r < HALF, 2 * m, 2 * m + 1))
    kx = kx.astype(F32) * (TWO_PI / NX)
    ky = ky.astype(F32) * (TWO_PI / NY)
    return kx, ky, kx * kx + ky * ky


def to_waves(sums, gaps, x_ref):
    even = data_by_table(sums, x_ref[0], x_ref[2], NN)
    odd = data_by_table(gaps, x_ref[1], x_ref[3], NN)
    return jnp.concatenate([even, odd], 1)


def low_lanes(shape):
    return lax.broadcasted_iota(jnp.int32, shape, 1) < 64


def folded_waves(got_ref, x_ref):
    sums, gaps = [], []
    mask = low_lanes((64, 128))
    for j in range(4):
        first, second = got_ref[2 * j], got_ref[2 * j + 1]
        first_turned = pltpu.roll(first, 64, 1)
        second_turned = pltpu.roll(second, 64, 1)
        sums.append(jnp.where(mask, first + first_turned, second + second_turned))
        gaps.append(jnp.where(mask, first - first_turned, second_turned - second))
    return to_waves(jnp.concatenate(sums, 1), jnp.concatenate(gaps, 1), x_ref)


def from_waves(waves, x_ref):
    even = table_by_data(x_ref[0], x_ref[2], waves[:, :HALF])
    odd = table_by_data(x_ref[1], x_ref[3], waves[:, HALF:])
    return even + odd, even - odd


def by_share(first, second):
    mask = low_lanes(first.shape)
    return (
        jnp.where(mask, first, pltpu.roll(second, 64, 1)),
        jnp.where(mask, pltpu.roll(first, 64, 1), second),
    )


def fetch(source, buffer, sems, place):
    copy = pltpu.make_async_copy(source, buffer, sems.at[place])
    copy.start()
    return copy


def wait_all(copies):
    for copy in copies:
        copy.wait()


def send_block(block_ref, out_ref, sems):
    wait_all([fetch(block_ref, out_ref.at[s], sems, s) for s in range(out_ref.shape[0])])


def start_kernel(
    ids_ref, phis_hbm, eta_hbm, y_hbm, out_ref, phis_ref, eta_ref, table_ref, block_ref, sems, out_sems
):
    first = pl.multiple_of(64 * ids_ref[1], 64)
    rows = pl.multiple_of(8 * (ids_ref[1] // 2), 8)
    copies = [
        fetch(y_hbm.at[:, pl.ds(first, 64), :], table_ref, sems, 0),
        fetch(phis_hbm, phis_ref, sems, 1),
        fetch(eta_hbm.at[pl.ds(rows, 8), :], eta_ref, sems, 2),
    ]
    wait_all(copies)
    coefs = data_by_table(phis_ref[...], table_ref[0], table_ref[1], NT)
    eta = eta_ref[...]
    eta = jnp.where(ids_ref[1] % 2 == 0, eta[:4], eta[4:])
    block_ref[:16] = jnp.concatenate([coefs[:16], coefs[16:]], 1)
    for j in range(4):
        block_ref[16 + 4 * j : 20 + 4 * j] = eta[:, 128 * j : 128 * j + 128]
    send_block(block_ref, out_ref, out_sems)


def first_kernel(ids_ref, got_ref, x_ref, *refs):
    out_hbm, waves_hbm, out_ref, waves_ref, sems = refs[4:]
    kx, ky, squares = wave_squares(ids_ref)
    size = jnp.sqrt(squares)
    got = [
        got_ref[pl.ds(512 * half + r, 16, stride=32), :] for half in range(2) for r in range(16)
    ]
    turned = [jnp.concatenate(got[8 * j : 8 * j + 8], 0).T for j in range(4)]
    first, second = jnp.concatenate(turned[:2], 1), jnp.concatenate(turned[2:], 1)
    sums, gaps = first + second, first - second
    sums = jnp.concatenate([sums[:64], sums[64:]], 1)
    gaps = jnp.concatenate([gaps[:64], gaps[64:]], 1)
    waves = to_waves(sums, gaps, x_ref)
    waves_ref[...] = waves
    copies = [fetch(waves_ref, waves_hbm, sems, 8)]
    both = jnp.concatenate([size * waves, squares * waves], 0)
    top, bottom = from_waves(both, x_ref)
    for s in range(8):
        out_ref[s, :64] = top[64 * s : 64 * s + 64]
        out_ref[s, 64:] = bottom[64 * s : 64 * s + 64]
        copies.append(fetch(out_ref.at[s], out_hbm.at[s], sems, s))
    wait_all(copies)


def second_kernel(got_ref, gathered_ref, y_ref, *refs):
    out_hbm, eta_hbm, curve_hbm, token_ref, out_ref, eta_ref, curve_ref, sems = refs[2:]
    pairs = [by_share(got_ref[2 * j], got_ref[2 * j + 1]) for j in range(4)]
    first = jnp.concatenate([p[0] for p in pairs], 1)
    second = jnp.concatenate([p[1] for p in pairs], 1)
    fields = data_by_table(jnp.concatenate([first, second], 0), y_ref[0], y_ref[1], NN)
    columns = []
    for j in range(4):
        block = [
            gathered_ref[pl.ds(512 * half + 16 + 4 * j + q, 16, stride=32), :]
            for half in range(2)
            for q in range(4)
        ]
        columns.append(jnp.concatenate(block, 0))
    eta = jnp.concatenate(columns, 1)
    eta_ref[...] = eta
    curve_ref[...] = 0.5 * eta * fields[128:]
    copies = [fetch(eta_ref, eta_hbm, sems, 8), fetch(curve_ref, curve_hbm, sems, 9)]
    waves = table_by_data(y_ref[0], y_ref[1], -eta * fields[:128])
    token_ref[...] = waves[:8, :128]
    for s in range(8):
        out_ref[s] = waves[64 * s : 64 * s + 64]
        copies.append(fetch(out_ref.at[s], out_hbm.at[s], sems, s))
    wait_all(copies)


def third_kernel(ids_ref, got_ref, x_ref, token_ref, out_hbm, waves_hbm, out_ref, waves_ref, sems):
    kx, ky, squares = wave_squares(ids_ref)
    size = jnp.sqrt(squares)
    waves = folded_waves(got_ref, x_ref)
    waves_ref[...] = waves
    copies = [fetch(waves_ref, waves_hbm, sems, 8)]
    top, bottom = from_waves(size * waves, x_ref)
    both = jnp.concatenate([top, bottom], 1)
    for s in range(8):
        out_ref[s] = both[64 * s : 64 * s + 64]
        copies.append(fetch(out_ref.at[s], out_hbm.at[s], sems, s))
    wait_all(copies)


def fourth_kernel(
    got_ref, eta_hbm, curve_hbm, y_ref, out_hbm, out_ref, eta_ref, curve_ref, sems
):
    copies = [fetch(eta_hbm, eta_ref, sems, 8), fetch(curve_hbm, curve_ref, sems, 9)]
    pairs = [by_share(got_ref[2 * j], got_ref[2 * j + 1]) for j in range(4)]
    coefs = jnp.concatenate(
        [jnp.concatenate([p[half] for p in pairs], 1) for half in range(2)], 0
    )
    field = data_by_table(coefs, y_ref[0], y_ref[1], NN)
    wait_all(copies)
    waves = table_by_data(y_ref[0], y_ref[1], -eta_ref[...] * (field + curve_ref[...]))
    copies = []
    for s in range(8):
        out_ref[s] = waves[64 * s : 64 * s + 64]
        copies.append(fetch(out_ref.at[s], out_hbm.at[s], sems, s))
    wait_all(copies)


def fifth_kernel(
    ids_ref, got_ref, x_ref, own_hbm, first_hbm, second_hbm, out_hbm,
    own_ref, out_ref, first_ref, second_ref, sems, out_sems,
):
    start = pl.multiple_of(32 * ids_ref[0], 32)
    copies = [
        fetch(first_hbm, first_ref, sems, 1),
        fetch(second_hbm, second_ref, sems, 2),
        fetch(own_hbm.at[pl.ds(start, 80), :], own_ref, sems, 0),
    ]
    kx, ky, squares = wave_squares(ids_ref)
    size = jnp.sqrt(squares)
    third = folded_waves(got_ref, x_ref)
    wait_all(copies)
    first = first_ref[...]
    both = first + second_ref[...]
    blocks = []
    for part in (0, HALF):
        speed = kx[:, part : part + 256]
        blocks.append(speed * first[:, part + 256 : part + HALF])
        blocks.append(-speed * first[:, part : part + 256])
    slope_x = jnp.concatenate(blocks, 1)
    speed = ky[:32]
    slope_y = jnp.concatenate([speed * first[32:], -speed * first[:32]], 0)
    fields = jnp.concatenate(
        [size * (both + third), squares * both, size * squares * first, slope_x, slope_y], 0
    )
    fh, fl = split(fields)
    oh, ol = own_ref[:, :NX], own_ref[:, NX:]
    rows = dot(oh, fh, NT) + dot(oh, fl, NT) + dot(ol, fh, NT)
    out_ref[...] = rows[:ROWS]
    send_block(out_ref, out_hbm, out_sems)


def own_rows(values):
    pieces = []
    for cx in (1, 2):
        for cy in range(4):
            first = 16 * cx + 4 * cy + 1
            pieces.append(values[first : first + 2])
    return jnp.concatenate(pieces, 0)


def live_mass(ids_ref, parts_ref):
    cell = lax.broadcasted_iota(jnp.int32, (64, 128), 0)
    at_x = 2 * ids_ref[0] - 1 + cell // 16
    at_z = 2 * ids_ref[1] - 1 + cell % 4
    inside = (at_x >= 0) & (at_x < 64) & (at_z >= 0) & (at_z < 16)
    return jnp.where(inside, parts_ref[7], 0.0)


def spread_own(values, out_ref):
    columns = jnp.concatenate([own_rows(v) for v in values], 0)
    missing = 128 - columns.shape[0]
    if missing:
        columns = jnp.concatenate([columns, jnp.zeros((missing, 128), F32)], 0)
    columns = columns.T
    for i in range(len(values)):
        for o in range(16):
            k = 16 * i + o
            out_ref[o, i] = jnp.broadcast_to(columns[:, k : k + 1], (128, 128))


def reach_groups(count_ref):
    return (count_ref[0] + GROUP - 1) // GROUP


def reach_copy(source, target, sems, group):
    span = pl.ds(pl.multiple_of(group * GROUP, GROUP), GROUP)
    return pltpu.make_async_copy(source.at[span], target.at[span], sems.at[group])


def reach_kernel(
    ids_ref, pairs_ref, count_ref, parts_ref, token_ref,
    reach_hbm, place_hbm, sum_hbm, done_ref,
    reach_ref, place_ref, density_ref, sum_ref, chan_ref, sems, reach_sems,
):
    mass = live_mass(ids_ref, parts_ref)
    chan_ref[0] = parts_ref[6]
    chan_ref[1] = KERNEL_COEF * mass
    chan_ref[2] = (-2.0 * KERNEL_COEF) * (mass / parts_ref[6])
    spread_own([parts_ref[i] for i in range(3)], place_ref)
    copies = [fetch(place_ref, place_hbm, sems, 0)]
    spread_own([parts_ref[6]], density_ref)
    sum_ref[...] = jnp.zeros_like(sum_ref)
    done_ref[...] = token_ref[...]
    def add_pair(t, carry):
        o = pairs_ref[0, t]
        cell = pairs_ref[1, t]
        place = [parts_ref[i, pl.ds(cell, 1), :] for i in range(3)]
        density, weight, volume = [chan_ref[i, pl.ds(cell, 1), :] for i in range(3)]
        for piece in range(4):
            span = pl.ds(32 * piece, 32)
            gap_x = place_ref[o, 0, span, :] - place[0]
            gap_y = place_ref[o, 1, span, :] - place[1]
            gap_z = place_ref[o, 2, span, :] - place[2]
            radius = jnp.sqrt(gap_x * gap_x + gap_y * gap_y + gap_z * gap_z)
            reach = jnp.maximum(1.0 - 0.5 * radius, 0.0)
            reach = reach * reach * reach
            reach_ref[t, span, :] = reach * weight
            sum_ref[o, span, :] += reach * ((density - density_ref[o, 0, span, :]) * volume)
        return carry

    def add_group(g, carry):
        last = jnp.minimum(GROUP * g + GROUP, count_ref[0])
        lax.fori_loop(GROUP * g, last, add_pair, 0)
        reach_copy(reach_ref, reach_hbm, reach_sems, g).start()
        return carry

    def wait_group(g, carry):
        reach_copy(reach_ref, reach_hbm, reach_sems, g).wait()
        return carry

    groups = reach_groups(count_ref)
    lax.fori_loop(0, groups, add_group, 0)
    copies.append(fetch(sum_ref, sum_hbm, sems, 1))
    lax.fori_loop(0, groups, wait_group, 0)
    wait_all(copies)


def last_kernel(
    ids_ref, pairs_ref, count_ref, got_ref, before_hbm, eta_hbm, after_hbm, parts_hbm, y_ref,
    reach_hbm, place_hbm, sum_hbm, surface_ref, rate_ref,
    eta_ref, parts_ref, reach_ref, place_ref, sum_ref,
    field_ref, target_ref, speed_ref, own_ref, sems, reach_sems,
):
    copies = [
        fetch(before_hbm, eta_ref.at[:16], sems, 0),
        fetch(eta_hbm, eta_ref.at[16:48], sems, 1),
        fetch(after_hbm, eta_ref.at[48:], sems, 2),
        fetch(parts_hbm, parts_ref, sems, 3),
        fetch(place_hbm, place_ref, sems, 4),
        fetch(sum_hbm, sum_ref, sems, 5),
    ]

    def start_group(g, carry):
        reach_copy(reach_hbm, reach_ref, reach_sems, g).start()
        return carry

    def wait_group(g, carry):
        reach_copy(reach_hbm, reach_ref, reach_sems, g).wait()
        return carry

    groups = reach_groups(count_ref)
    lax.fori_loop(0, groups, start_group, 0)
    slab = ids_ref[0]
    mask = low_lanes((ROWS, 128))
    fields = []
    for f in range(5):
        pieces = []
        lane = 128 * (f // 2)
        for j in range(4):
            first = got_ref[2 * j, :, lane : lane + 128] if f < 4 else got_ref[2 * j, :, 256:320]
            second = got_ref[2 * j + 1, :, lane : lane + 128] if f < 4 else got_ref[2 * j + 1, :, 256:320]
            if f == 4:
                pieces.append(jnp.concatenate([first, second], 1))
            elif f % 2 == 0:
                pieces.append(jnp.where(mask, first, pltpu.roll(second, 64, 1)))
            else:
                pieces.append(jnp.where(mask, pltpu.roll(first, 64, 1), second))
        fields.append(jnp.concatenate(pieces, 1))
    fields = data_by_table(
        jnp.concatenate(fields, 0), y_ref[0], y_ref[1], NN
    )
    wait_all(copies[:4])
    eta = eta_ref[...]
    vertical = (
        fields[:ROWS]
        + eta * fields[ROWS : 2 * ROWS]
        + 0.5 * eta * eta * fields[2 * ROWS : 3 * ROWS]
    )
    surface_ref[...] = vertical[16:48]
    sampled = (fields[3 * ROWS : 4 * ROWS], fields[4 * ROWS :], vertical)
    for f in range(3):
        field_ref[2 * f] = sampled[f]
        field_ref[2 * f + 1] = pltpu.roll(sampled[f], NY - 1, 1) - sampled[f]
    row_ids = lax.broadcasted_iota(jnp.int32, (24, 128), 0).astype(F32)

    def sample(cx, carry):
        first_row = pl.multiple_of(16 * cx, 16)
        origin = (32 * slab - 16 + 16 * cx).astype(F32)
        found = [[], [], []]
        place_x = parts_ref[0, pl.ds(first_row, 16), :] * 8.0 - origin
        place_y = parts_ref[1, pl.ds(first_row, 16), :] * 64.0
        for cy in range(4):
            for cz in range(4):
                cell = 4 * cy + cz
                along = place_y[cell : cell + 1] - 128.0 * cy
                index = jnp.clip(along.astype(jnp.int32), 0, 127)
                part = along - index.astype(F32)
                index = jnp.broadcast_to(index, (24, 128))
                weight = jnp.maximum(0.0, 1.0 - jnp.abs(place_x[cell : cell + 1] - row_ids))
                weight_next = weight * part
                for f in range(3):
                    here = field_ref[2 * f, pl.ds(first_row, 24), 128 * cy : 128 * cy + 128]
                    step = field_ref[2 * f + 1, pl.ds(first_row, 24), 128 * cy : 128 * cy + 128]
                    here = jnp.take_along_axis(here, index, axis=1)
                    step = jnp.take_along_axis(step, index, axis=1)
                    found[f].append(
                        jnp.sum(weight * here + weight_next * step, axis=0, keepdims=True)
                    )
        for f in range(3):
            target_ref[f, pl.ds(first_row, 16), :] = jnp.concatenate(found[f], 0)
        return carry

    lax.fori_loop(0, 4, sample, 0)
    depth = jnp.exp((parts_ref[2] - 32.0) * (1.0 / 32.0))
    close = jnp.clip(1.0 - parts_ref[0] * (1.0 / 256.0), 0.0, 1.0)
    close = close * close
    for i in range(3):
        speed = parts_ref[3 + i]
        speed_ref[i] = speed + close * (target_ref[i] * depth - speed)
    spread_own([speed_ref[i] for i in range(3)], own_ref)
    wait_all(copies[4:])
    lax.fori_loop(0, groups, wait_group, 0)

    def add_pair(t, carry):
        o = pairs_ref[0, t]
        cell = pairs_ref[1, t]
        place = [parts_ref[i, pl.ds(cell, 1), :] for i in range(3)]
        speed = [speed_ref[i, pl.ds(cell, 1), :] for i in range(3)]
        for piece in range(4):
            span = pl.ds(32 * piece, 32)
            approach = 0.0
            for i in range(3):
                approach = approach + (own_ref[o, i, span, :] - speed[i]) * (
                    place_ref[o, i, span, :] - place[i]
                )
            sum_ref[o, span, :] += reach_ref[t, span, :] * approach
        return carry

    lax.fori_loop(0, count_ref[0], add_pair, 0)
    ones = jnp.ones((8, 384), BF16)
    rates = []
    for o in range(16):
        total = sum_ref[o]
        high, rest = split(total)
        middle, last = split(total - high.astype(F32))
        rates.append(dot(ones, jnp.concatenate([high, middle, last], 1), NT)[:1])
    mass = own_rows(parts_ref[7])
    rate_ref[...] = jnp.where(mass > 0.0, jnp.concatenate(rates, 0), 0.0)


def call(kernel, args, kinds, outs, name, vmem, scratch):
    specs = dict(S=SM, H=HB, V=VM)
    args = [
        pltpu.with_memory_space_constraint(a, pltpu.HBM) if k == "H" else a
        for a, k in zip(args, kinds, strict=True)
    ]
    return pl.pallas_call(
        kernel,
        out_shape=[
            pltpu.HBM(s, F32) if k == "H" else jax.ShapeDtypeStruct(s, F32) for s, k in outs
        ],
        in_specs=[specs[k] for k in kinds],
        out_specs=[specs[k] for _, k in outs],
        scratch_shapes=[pltpu.VMEM(s, F32) if isinstance(s, tuple) else s for s in scratch],
        compiler_params=pltpu.CompilerParams(vmem_limit_bytes=vmem * 1024 * 1024),
        name=name,
    )(*args)


def dma_sems(count):
    return pltpu.SemaphoreType.DMA((count,))


def passed(values, axis, by):
    size = lax.axis_size(axis)
    return lax.ppermute(values, axis, [(i, (i + by) % size) for i in range(size)])


def swap(block, axis):
    return lax.all_to_all(block, axis, split_axis=0, concat_axis=0, tiled=True)


def per_device(eta, phis, particles, cell_count, pair_cells, pair_count):
    slab = lax.axis_index("gx")
    layer = lax.axis_index("gz")
    ids = jnp.stack([slab, layer]).astype(jnp.int32)
    table = tables()
    y = jnp.asarray(table["y"])
    x = jnp.asarray(table["x"])
    own = jnp.asarray(table["own"])

    live = jnp.arange(128, dtype=jnp.int32) < cell_count[..., None]
    mass = jnp.where(live, particles[7], 0.0)
    cells = jnp.concatenate([particles[:7], mass[None]], 0)
    eta_before = passed(eta[16:], "gx", 1)
    eta_after = passed(eta[:24], "gx", -1)
    cells_before = passed(cells[:, 1:], "gx", 1)
    cells_after = passed(cells[:, :1], "gx", -1)
    cells = jnp.concatenate([cells_before, cells, cells_after], 1)
    below = passed(cells[:, :, :, 1:], "gz", 1)
    above = passed(cells[:, :, :, :1], "gz", -1)
    cells = jnp.concatenate([below, cells, above], 3)
    cells = cells.reshape(8, 64, 128)
    pairs = pair_cells.reshape(2, 96)
    count = pair_count.reshape(1)

    (block,) = call(
        start_kernel, (ids, phis, eta, y), "SHHH", [((32, 32, 128), "H")], "start", 4,
        [
            (32, NY),
            (8, NY),
            pltpu.VMEM((2, 64, NY), BF16),
            (32, 128),
            dma_sems(3),
            dma_sems(32),
        ],
    )
    gathered = swap(block, "gx").reshape(1024, 128)
    block, first = call(
        first_kernel,
        (ids, gathered, x, cells_before, cells_after, eta_before, eta_after),
        "SVVHHHH",
        [((8, 128, 128), "H"), ((64, NX), "H")],
        "first",
        8,
        [(8, 128, 128), (64, NX), dma_sems(9)],
    )
    got = swap(block, "gz")
    block, eta_part, curve, token = call(
        second_kernel,
        (got, gathered, y, below, above),
        "VVVHH",
        [((8, 64, 128), "H"), ((128, NY), "H"), ((128, NY), "H"), ((8, 128), "V")],
        "second",
        8,
        [(8, 64, 128), (128, NY), (128, NY), dma_sems(10)],
    )
    got = swap(block, "gz")
    reach, place, before, token = call(
        reach_kernel,
        (ids, pairs, count, cells, token),
        "SSSVV",
        [
            ((96, 128, 128), "H"),
            ((16, 3, 128, 128), "H"),
            ((16, 128, 128), "H"),
            ((8, 128), "V"),
        ],
        "reach",
        16,
        [
            (96, 128, 128),
            (16, 3, 128, 128),
            (16, 1, 128, 128),
            (16, 128, 128),
            (3, 64, 128),
            dma_sems(2),
            dma_sems(96 // GROUP),
        ],
    )
    block, second = call(
        third_kernel,
        (ids, got, x, token),
        "SVVV",
        [((8, 64, 128), "H"), ((64, NX), "H")],
        "third",
        8,
        [(8, 64, 128), (64, NX), dma_sems(9)],
    )
    got = swap(block, "gz")
    (block,) = call(
        fourth_kernel,
        (got, eta_part, curve, y),
        "VHHV",
        [((8, 64, 128), "H")],
        "fourth",
        8,
        [(8, 64, 128), (128, NY), (128, NY), dma_sems(10)],
    )
    got = swap(block, "gz")
    (block,) = call(
        fifth_kernel,
        (ids, got, x, own, first, second),
        "SVVHHH",
        [((8, ROWS, 320), "H")],
        "fifth",
        8,
        [
            pltpu.VMEM((80, 2 * NX), BF16),
            (ROWS, 320),
            (64, NX),
            (64, NX),
            dma_sems(3),
            dma_sems(8),
        ],
    )
    got = swap(block, "gz")
    surface, rate = call(
        last_kernel,
        (
            ids, pairs, count, got, eta_before, eta, eta_after, cells, y, reach, place, before
        ),
        "SSSVHHHHVHHH",
        [((32, NY), "V"), ((16, 128), "V")],
        "last",
        24,
        [
            (ROWS, NY),
            (8, 64, 128),
            (96, 128, 128),
            (16, 3, 128, 128),
            (16, 128, 128),
            (6, ROWS, NY),
            (3, 64, 128),
            (3, 64, 128),
            (16, 3, 128, 128),
            dma_sems(6),
            dma_sems(96 // GROUP),
        ],
    )
    return surface, rate.reshape(2, 4, 2, 128)


def solution(mesh):
    in_specs = (
        P("gx", None),
        P("gx", None),
        P(None, "gx", None, "gz", None),
        P("gx", None, "gz"),
        P("gx", "gz", None, None),
        P("gx", "gz", None),
    )
    out_specs = (P("gx", None), P("gx", None, "gz", None))
    return jax.shard_map(
        per_device, mesh=mesh, in_specs=in_specs, out_specs=out_specs, check_vma=False
    )
```

time: 149 us -> 132 us (0.89)
  the two profiles are of different devices: /device:TPU:0 before, /device:TPU:1 now
where the time goes in v2:
time: 132 us; the launch traced here: 131 us
  blocking collectives  40.1 us (30%)
  Pallas kernels  36.1 us (27%)
  starting transfers between devices  32.2 us (24%)
  waiting for transfers between devices  13.9 us (11%)
  local copies, waits for them, and re-layouts  4.18 us (3%)
  other arithmetic  2.81 us (2%)
  between operations  1.47 us (1%)
    all_to_all x3, blocking collectives, swap(): return lax.all_to_all(block, axis, split_axis=0, concat_axis=0, tiled=True)  40.1 us
    pallas_call x8, Pallas kernels, call(): pl.pallas_call(kernel, out_shape=[pltpu.HBM(s, F32) if k == 'H' else jax....  36.1 us
    all_to_all x3, starting transfers between devices, swap(): return lax.all_to_all(block, axis, split_axis=0, concat_axis=0, tiled=True)  24.1 us
    ppermute x6, waiting for transfers between devices, passed(): lax.ppermute(values, axis, [(i, (i + by) % size) for i in range(size)])  13.5 us
    ppermute x6, starting transfers between devices, passed(): lax.ppermute(values, axis, [(i, (i + by) % size) for i in range(size)])  8.08 us
  transfers between devices with their start and end apart: 9, of which 4 were waited for; matrix products, arithmetic and copies ran while one was open for 5% of the time, Pallas kernels for 7%

profile of v2, /device:TPU:1, one launch (start us, length us, event | category | flops | bytes accessed | tf_op | source)
XLA Modules:
  0.0 130.8 jit_solution(12544396831096357774)
XLA Ops:
  0.6 0.0 copy-start.1
  0.6 0.0 copy-start
  0.7 0.1 pad_add_fusion.ids_ref
  0.7 2.9 %start.1 = f32[32,32,128]{2,1,0:T(8,128)} custom-call(s32[2]{0:T(128)S(1)} %pad_add_fusion.ids_ref, f32[32,512]{1,0:T(8,128)} %phis_hbm.1, f32[32,512]{1,0:T(8,128)} %eta_hbm.3, bf16[2,512,512]{2,1,0:T(8,128)(2,1)} %constant.17.clone.y_hbm.y_ref), custom_call_target="tpu_custom_call" | custom-call | tf_op jit(solution)/shard_map/start/pallas_call | solution.py:504
  3.6 0.0 copy-start.3
  3.7 12.0 %all-to-all-start = ((f32[32,32,128]{2,1,0:T(8,128)}), f32[32,32,128]{2,1,0:T(8,128)}, u32[]{:S(2)}, u32[]{:S(2)}) async-start(f32[32,32,128]{2,1,0:T(8,128)} %start.1), calls=%async_computation | async-start | bytes 1048576 | tf_op jit(solution)/shard_map/all_to_all | solution.py:527
  15.7 0.8 slice.28
  16.4 1.2 collective-permute-start.2
  17.6 0.8 slice.29
  18.4 3.6 %collective-permute-start.3 = (f32[24,512]{1,0:T(8,128)S(1)}, f32[24,512]{1,0:T(8,128)S(1)}, u32[]{:S(2)}, u32[]{:S(2)}) collective-permute-start(f32[24,512]{1,0:T(8,128)S(1)} %slice.29), channel_id=1, source_target_pairs={{0,248},{8,0},{16,8},{24,16},{32,24},{40,32},{48,40},{56,48},{64,5... | collective-permute-start | bytes 147464 | tf_op jit(solution)/shard_map/ppermute | solution.py:523
  22.0 0.8 copy.11
  22.8 0.8 slice.24
  23.6 0.8 compare_select_fusion
  24.4 1.3 %collective-permute-start.1 = (f32[8,1,4,2,128]{4,3,2,1,0:T(2,128)S(1)}, f32[8,1,4,2,128]{4,3,2,1,0:T(2,128)S(1)}, u32[]{:S(2)}, u32[]{:S(2)}) collective-permute-start(f32[8,1,4,2,128]{4,3,2,1,0:T(2,128)S(1)} %get-tuple-element.32), channel_id=1, source_target_pairs={{0,248},{8,0},{16,8},{24,16},{32,24},{40,32},{48,40},{56,48},{64,5... | collective-permute-start | bytes 98312 | tf_op jit(solution)/shard_map/ppermute | solution.py:523
  25.8 0.2 collective-permute-start
  26.0 4.2 %collective-permute-done.2.refs_2_.before_hbm = f32[16,512]{1,0:T(8,128)S(1)} collective-permute-done((f32[16,512]{1,0:T(8,128)S(1)}, f32[16,512]{1,0:T(8,128)S(1)}, u32[]{:S(2)}, u32[]{:S(2)}) %collective-permute-start.2) | collective-permute-done | bytes 32800 | tf_op jit(solution)/shard_map/ppermute | solution.py:523
  30.2 0.0 collective-permute-done.1.refs_1_
  30.2 2.8 %collective-permute-done.refs_0_ = f32[8,1,4,2,128]{4,3,2,1,0:T(2,128)S(1)} collective-permute-done((f32[8,1,4,2,128]{4,3,2,1,0:T(2,128)S(1)}, f32[8,1,4,2,128]{4,3,2,1,0:T(2,128)S(1)}, u32[]{:S(2)}, u32[]{:S(2)}) %collective-permute-start) | collective-permute-done | bytes 32800 | tf_op jit(solution)/shard_map/ppermute | solution.py:523
  33.0 0.0 collective-permute-done.3.refs_3_.after_hbm
  33.0 0.0 all-to-all-done
  33.0 0.0 copy-done.9
  33.0 0.0 copy-done.4
  33.0 0.6 copy-done.5
  33.6 0.0 copy-done.8
  33.6 0.0 copy-done
  33.6 3.0 %first.1 = (f32[8,128,128]{2,1,0:T(8,128)}, f32[64,1024]{1,0:T(8,128)}) custom-call(s32[2]{0:T(128)S(1)} %pad_add_fusion.ids_ref, f32[1024,128]{1,0:T(8,128)} %bitcast.4.got_ref.gathered_ref, bf16[4,512,512]{2,1,0:T(8,128)(2,1)S(1)} %copy-done, f32[8,1,4,2,128]{4,3,2,1,0:T(2,128)} %copy-done.5, f32[8,1,4,2,128]{4,3,2,1,0:T(2,128)} %copy-done.4, ...), custom_call_target="tpu_custom_call" | custom-call | tf_op jit(solution)/shard_map/first/pallas_call | solution.py:504
  36.6 6.6 %all-to-all-start.1 = ((f32[8,128,128]{2,1,0:T(8,128)}), f32[8,128,128]{2,1,0:T(8,128)}, u32[]{:S(2)}, u32[]{:S(2)}) async-start(f32[8,128,128]{2,1,0:T(8,128)} %get-tuple-element.16), calls=%async_computation.1 | async-start | bytes 1048576 | tf_op jit(solution)/shard_map/all_to_all | solution.py:527
  43.2 0.8 pad_maximum_fusion.1
  44.1 0.1 fusion.1
  44.2 0.0 collective-permute-start.5
  44.2 1.7 %collective-permute-start.4 = (f32[8,4,4,1,128]{4,3,2,1,0:T(1,128)S(1)}, f32[8,4,4,1,128]{4,3,2,1,0:T(1,128)S(1)}, u32[]{:S(2)}, u32[]{:S(2)}) collective-permute-start(f32[8,4,4,1,128]{4,3,2,1,0:T(1,128)S(1)} %get-tuple-element.31), channel_id=1, source_target_pairs={{0,1},{1,2},{2,3},{3,4},{4,5},{5,6},{6,7},{7,0},{8,9},{9,10},{10,1... | collective-permute-start | bytes 196616 | tf_op jit(solution)/shard_map/ppermute | solution.py:523
  45.9 6.6 %collective-permute-done.5.refs_1_ = f32[8,4,4,1,128]{4,3,2,1,0:T(1,128)S(1)} collective-permute-done((f32[8,4,4,1,128]{4,3,2,1,0:T(1,128)S(1)}, f32[8,4,4,1,128]{4,3,2,1,0:T(1,128)S(1)}, u32[]{:S(2)}, u32[]{:S(2)}) %collective-permute-start.5) | collective-permute-done | bytes 65568 | tf_op jit(solution)/shard_map/ppermute | solution.py:523
  52.5 0.0 collective-permute-done.4.refs_0_
  52.5 0.4 all-to-all-done.1.got_ref
  52.9 0.3 copy-done.6
  53.1 0.0 copy-done.7
  53.1 3.0 %second.1 = (f32[8,64,128]{2,1,0:T(8,128)}, f32[128,512]{1,0:T(8,128)}, f32[128,512]{1,0:T(8,128)}, f32[8,128]{1,0:T(8,128)S(1)}) custom-call(f32[8,128,128]{2,1,0:T(8,128)} %all-to-all-done.1.got_ref, f32[1024,128]{1,0:T(8,128)} %bitcast.4.got_ref.gathered_ref, bf16[2,512,512]{2,1,0:T(8,128)(2,1)S(1)} %copy-done.1, f32[8,4,4,1,128]{4,3,2,1,0:T(1,128)} %copy-done.7, ...), custom_call_target="tpu_custom_call" | custom-call | tf_op jit(solution)/shard_map/second/pallas_call | solution.py:504
  56.1 5.5 %all-to-all-start.2 = ((f32[8,64,128]{2,1,0:T(8,128)}), f32[8,64,128]{2,1,0:T(8,128)}, u32[]{:S(2)}, u32[]{:S(2)}) async-start(f32[8,64,128]{2,1,0:T(8,128)} %get-tuple-element.17), calls=%async_computation.2 | async-start | bytes 524288 | tf_op jit(solution)/shard_map/all_to_all | solution.py:527
  62.3 1.1 pad_maximum_fusion
  63.5 8.9 %reach.1 = (f32[96,128,128]{2,1,0:T(8,128)}, f32[16,3,128,128]{3,2,1,0:T(8,128)}, f32[16,128,128]{2,1,0:T(8,128)}, f32[8,128]{1,0:T(8,128)S(1)}) custom-call(s32[2]{0:T(128)S(1)} %pad_add_fusion.ids_ref, s32[2,96]{1,0:T(2,128)S(1)} %bitcast.11, s32[1]{0:T(128)} %bitcast.7.count_ref, f32[8,64,128]{2,1,0:T(8,128)S(1)} %bitcast.9, ...), custom_call_target="tpu_custom_call" | custom-call | tf_op jit(solution)/shard_map/reach/pallas_call | solution.py:504
  72.4 0.0 all-to-all-done.2.got_ref
  72.4 2.9 %third.1 = (f32[8,64,128]{2,1,0:T(8,128)}, f32[64,1024]{1,0:T(8,128)}) custom-call(s32[2]{0:T(128)S(1)} %pad_add_fusion.ids_ref, f32[8,64,128]{2,1,0:T(8,128)} %all-to-all-done.2.got_ref, bf16[4,512,512]{2,1,0:T(8,128)(2,1)S(1)} %copy-done, f32[8,128]{1,0:T(8,128)S(1)} %get-tuple-element.19.token_ref), custom_call_target="tpu_custom_call" | custom-call | tf_op jit(solution)/shard_map/third/pallas_call | solution.py:504
  75.3 11.3 %all_to_all.30.got_ref = f32[8,64,128]{2,1,0:T(8,128)S(1)} all-to-all(f32[8,64,128]{2,1,0:T(8,128)} %get-tuple-element.20), channel_id=1, replica_groups=mesh['gx'=32,'gz'=8] {'gz'}, dimensions={0} | all-to-all | bytes 524288 | tf_op jit(solution)/shard_map/all_to_all | solution.py:527
  86.6 2.2 %fourth.1 = f32[8,64,128]{2,1,0:T(8,128)} custom-call(f32[8,64,128]{2,1,0:T(8,128)S(1)} %all_to_all.30.got_ref, f32[128,512]{1,0:T(8,128)} %get-tuple-element.21.eta_hbm, f32[128,512]{1,0:T(8,128)} %get-tuple-element.22.curve_hbm, bf16[2,512,512]{2,1,0:T(8,128)(2,1)S(1)} %copy-done.1), custom_call_target="tpu_custom_call" | custom-call | tf_op jit(solution)/shard_map/fourth/pallas_call | solution.py:504
  88.8 10.9 %all_to_all.31.got_ref = f32[8,64,128]{2,1,0:T(8,128)S(1)} all-to-all(f32[8,64,128]{2,1,0:T(8,128)} %fourth.1), channel_id=1, replica_groups=mesh['gx'=32,'gz'=8] {'gz'}, dimensions={0} | all-to-all | bytes 524288 | tf_op jit(solution)/shard_map/all_to_all | solution.py:527
  99.6 3.8 %fifth.1 = f32[8,72,320]{2,1,0:T(8,128)} custom-call(s32[2]{0:T(128)S(1)} %pad_add_fusion.ids_ref, f32[8,64,128]{2,1,0:T(8,128)S(1)} %all_to_all.31.got_ref, bf16[4,512,512]{2,1,0:T(8,128)(2,1)S(1)} %copy-done, bf16[1096,2048]{1,0:T(8,128)(2,1)} %constant.19.clone.own_hbm, f32[64,1024]{1,0:T(8,128)} %get-tuple-element.23.first_hbm, ...), custom_call_target="tpu_custom_call" | custom-call | tf_op jit(solution)/shard_map/fifth/pallas_call | solution.py:504
  103.5 18.0 %all_to_all.32.got_ref = f32[8,72,320]{2,1,0:T(8,128)S(1)} all-to-all(f32[8,72,320]{2,1,0:T(8,128)} %fifth.1), channel_id=1, replica_groups=mesh['gx'=32,'gz'=8] {'gz'}, dimensions={0} | all-to-all | bytes 1474560 | tf_op jit(solution)/shard_map/all_to_all | solution.py:527
  121.5 9.4 %last.1 = (f32[32,512]{1,0:T(8,128)}, f32[16,128]{1,0:T(8,128)}) custom-call(s32[2]{0:T(128)S(1)} %pad_add_fusion.ids_ref, s32[2,96]{1,0:T(2,128)S(1)} %bitcast.12, s32[1]{0:T(128)} %bitcast.8.count_ref, f32[8,72,320]{2,1,0:T(8,128)S(1)} %all_to_all.32.got_ref, f32[16,512]{1,0:T(8,128)} %copy-done.9, f32[32,512]{1,0:T(8,128)} %eta_hbm.3, ...), custom_call_target="tpu_custom_call" | custom-call | tf_op jit(solution)/shard_map/last/pallas_call | solution.py:504
  (11 shorter events, 0.0 us)
Async XLA Ops:
  0.6 52.5 %copy-start.1 = (bf16[2,512,512]{2,1,0:T(8,128)(2,1)S(1)}, bf16[2,512,512]{2,1,0:T(8,128)(2,1)}, u32[]{:S(2)}) copy-start(bf16[2,512,512]{2,1,0:T(8,128)(2,1)} %constant.17.clone.y_hbm.y_ref) | copy-start | bytes 3145732
  0.6 32.9 %copy-start = (bf16[4,512,512]{2,1,0:T(8,128)(2,1)S(1)}, bf16[4,512,512]{2,1,0:T(8,128)(2,1)}, u32[]{:S(2)}) copy-start(bf16[4,512,512]{2,1,0:T(8,128)(2,1)} %constant.18.clone.x_ref) | copy-start | bytes 6291460
  3.6 59.8 %copy-start.3 = (s32[1,1,2,96]{3,2,1,0:T(2,128)S(1)}, s32[1,1,2,96]{3,2,1,0:T(2,128)}, u32[]{:S(2)}) copy-start(s32[1,1,2,96]{3,2,1,0:T(2,128)} %param.13) | copy-start | bytes 2308
  3.7 29.3 %all-to-all-start = ((f32[32,32,128]{2,1,0:T(8,128)}), f32[32,32,128]{2,1,0:T(8,128)}, u32[]{:S(2)}, u32[]{:S(2)}) async-start(f32[32,32,128]{2,1,0:T(8,128)} %start.1), calls=%async_computation | async-start | bytes 1048576 | tf_op jit(solution)/shard_map/all_to_all | solution.py:527
  16.4 13.7 %collective-permute-start.2 = (f32[16,512]{1,0:T(8,128)S(1)}, f32[16,512]{1,0:T(8,128)S(1)}, u32[]{:S(2)}, u32[]{:S(2)}) collective-permute-start(f32[16,512]{1,0:T(8,128)S(1)} %slice.28), channel_id=1, source_target_pairs={{0,8},{8,16},{16,24},{24,32},{32,40},{40,48},{48,56},{56,64},{64,7... | collective-permute-start | bytes 98312 | tf_op jit(solution)/shard_map/ppermute | solution.py:523
  18.4 14.6 %collective-permute-start.3 = (f32[24,512]{1,0:T(8,128)S(1)}, f32[24,512]{1,0:T(8,128)S(1)}, u32[]{:S(2)}, u32[]{:S(2)}) collective-permute-start(f32[24,512]{1,0:T(8,128)S(1)} %slice.29), channel_id=1, source_target_pairs={{0,248},{8,0},{16,8},{24,16},{32,24},{40,32},{48,40},{56,48},{64,5... | collective-permute-start | bytes 147464 | tf_op jit(solution)/shard_map/ppermute | solution.py:523
  24.4 5.8 %collective-permute-start.1 = (f32[8,1,4,2,128]{4,3,2,1,0:T(2,128)S(1)}, f32[8,1,4,2,128]{4,3,2,1,0:T(2,128)S(1)}, u32[]{:S(2)}, u32[]{:S(2)}) collective-permute-start(f32[8,1,4,2,128]{4,3,2,1,0:T(2,128)S(1)} %get-tuple-element.32), channel_id=1, source_target_pairs={{0,248},{8,0},{16,8},{24,16},{32,24},{40,32},{48,40},{56,48},{64,5... | collective-permute-start | bytes 98312 | tf_op jit(solution)/shard_map/ppermute | solution.py:523
  25.8 7.2 %collective-permute-start = (f32[8,1,4,2,128]{4,3,2,1,0:T(2,128)S(1)}, f32[8,1,4,2,128]{4,3,2,1,0:T(2,128)S(1)}, u32[]{:S(2)}, u32[]{:S(2)}) collective-permute-start(f32[8,1,4,2,128]{4,3,2,1,0:T(2,128)S(1)} %get-tuple-element.33), channel_id=1, source_target_pairs={{0,8},{8,16},{16,24},{24,32},{32,40},{40,48},{48,56},{56,64},{64,7... | collective-permute-start | bytes 98312 | tf_op jit(solution)/shard_map/ppermute | solution.py:523
  30.2 2.8 %copy-start.9 = (f32[16,512]{1,0:T(8,128)}, f32[16,512]{1,0:T(8,128)S(1)}, u32[]{:S(2)}) copy-start(f32[16,512]{1,0:T(8,128)S(1)} %collective-permute-done.2.refs_2_.before_hbm) | copy-start | bytes 98308
  30.2 2.8 %copy-start.4 = (f32[8,1,4,2,128]{4,3,2,1,0:T(2,128)}, f32[8,1,4,2,128]{4,3,2,1,0:T(2,128)S(1)}, u32[]{:S(2)}) copy-start(f32[8,1,4,2,128]{4,3,2,1,0:T(2,128)S(1)} %collective-permute-done.1.refs_1_) | copy-start | bytes 98308
  33.0 0.6 copy-start.5
  33.0 0.6 copy-start.8
  36.6 16.2 %all-to-all-start.1 = ((f32[8,128,128]{2,1,0:T(8,128)}), f32[8,128,128]{2,1,0:T(8,128)}, u32[]{:S(2)}, u32[]{:S(2)}) async-start(f32[8,128,128]{2,1,0:T(8,128)} %get-tuple-element.16), calls=%async_computation.1 | async-start | bytes 1048576 | tf_op jit(solution)/shard_map/all_to_all | solution.py:527
  44.2 8.3 %collective-permute-start.5 = (f32[8,4,4,1,128]{4,3,2,1,0:T(1,128)S(1)}, f32[8,4,4,1,128]{4,3,2,1,0:T(1,128)S(1)}, u32[]{:S(2)}, u32[]{:S(2)}) collective-permute-start(f32[8,4,4,1,128]{4,3,2,1,0:T(1,128)S(1)} %get-tuple-element.30), channel_id=1, source_target_pairs={{0,7},{1,0},{2,1},{3,2},{4,3},{5,4},{6,5},{7,6},{8,15},{9,8},{10,9... | collective-permute-start | bytes 196616 | tf_op jit(solution)/shard_map/ppermute | solution.py:523
  44.2 8.3 %collective-permute-start.4 = (f32[8,4,4,1,128]{4,3,2,1,0:T(1,128)S(1)}, f32[8,4,4,1,128]{4,3,2,1,0:T(1,128)S(1)}, u32[]{:S(2)}, u32[]{:S(2)}) collective-permute-start(f32[8,4,4,1,128]{4,3,2,1,0:T(1,128)S(1)} %get-tuple-element.31), channel_id=1, source_target_pairs={{0,1},{1,2},{2,3},{3,4},{4,5},{5,6},{6,7},{7,0},{8,9},{9,10},{10,1... | collective-permute-start | bytes 196616 | tf_op jit(solution)/shard_map/ppermute | solution.py:523
  52.5 0.6 copy-start.6
  52.5 0.6 copy-start.7
  56.1 16.2 %all-to-all-start.2 = ((f32[8,64,128]{2,1,0:T(8,128)}), f32[8,64,128]{2,1,0:T(8,128)}, u32[]{:S(2)}, u32[]{:S(2)}) async-start(f32[8,64,128]{2,1,0:T(8,128)} %get-tuple-element.17), calls=%async_computation.2 | async-start | bytes 524288 | tf_op jit(solution)/shard_map/all_to_all | solution.py:527
  63.4 40.0 %copy-start.2 = (f32[8,4,4,4,128]{4,3,2,1,0:T(4,128)}, f32[8,4,4,4,128]{4,3,2,1,0:T(4,128)S(1)}, u32[]{:S(2)}) copy-start(f32[8,4,4,4,128]{4,3,2,1,0:T(4,128)S(1)} %pad_maximum_fusion) | copy-start | bytes 786436

commit v3 on v2

--- a/solution.py
+++ b/solution.py
@@ -23,6 +23,7 @@
 SM = pl.BlockSpec(memory_space=pltpu.SMEM)
 HB = pl.BlockSpec(memory_space=pltpu.HBM)
 GROUP = 8
+PART = 48
 
 
 def parts_of(table):
@@ -170,8 +171,9 @@
     send_block(block_ref, out_ref, out_sems)
 
 
-def first_kernel(ids_ref, got_ref, x_ref, *refs):
-    out_hbm, waves_hbm, out_ref, waves_ref, sems = refs[4:]
+def first_kernel(
+    ids_ref, got_ref, x_ref, wide_hbm, out_hbm, waves_hbm, out_ref, waves_ref, sems
+):
     kx, ky, squares = wave_squares(ids_ref)
     size = jnp.sqrt(squares)
     got = [
@@ -194,8 +196,10 @@
     wait_all(copies)
 
 
-def second_kernel(got_ref, gathered_ref, y_ref, *refs):
-    out_hbm, eta_hbm, curve_hbm, token_ref, out_ref, eta_ref, curve_ref, sems = refs[2:]
+def second_kernel(
+    got_ref, gathered_ref, y_ref, below_hbm, above_hbm, out_hbm, eta_hbm, curve_hbm, token_ref,
+    out_ref, eta_ref, curve_ref, sems,
+):
     pairs = [by_share(got_ref[2 * j], got_ref[2 * j + 1]) for j in range(4)]
     first = jnp.concatenate([p[0] for p in pairs], 1)
     second = jnp.concatenate([p[1] for p in pairs], 1)
@@ -220,7 +224,10 @@
     wait_all(copies)
 
 
-def third_kernel(ids_ref, got_ref, x_ref, token_ref, out_hbm, waves_hbm, out_ref, waves_ref, sems):
+def third_kernel(
+    ids_ref, got_ref, x_ref, token_ref, out_hbm, waves_hbm, next_ref, out_ref, waves_ref, sems
+):
+    next_ref[...] = token_ref[...]
     kx, ky, squares = wave_squares(ids_ref)
     size = jnp.sqrt(squares)
     waves = folded_waves(got_ref, x_ref)
@@ -235,7 +242,7 @@
 
 
 def fourth_kernel(
-    got_ref, eta_hbm, curve_hbm, y_ref, out_hbm, out_ref, eta_ref, curve_ref, sems
+    got_ref, eta_hbm, curve_hbm, y_ref, token_ref, out_hbm, out_ref, eta_ref, curve_ref, sems
 ):
     copies = [fetch(eta_hbm, eta_ref, sems, 8), fetch(curve_hbm, curve_ref, sems, 9)]
     pairs = [by_share(got_ref[2 * j], got_ref[2 * j + 1]) for j in range(4)]
@@ -254,7 +261,7 @@
 
 def fifth_kernel(
     ids_ref, got_ref, x_ref, own_hbm, first_hbm, second_hbm, out_hbm,
-    own_ref, out_ref, first_ref, second_ref, sems, out_sems,
+    own_ref, out_ref, first_ref, second_ref, sems,
 ):
     start = pl.multiple_of(32 * ids_ref[0], 32)
     copies = [
@@ -283,7 +290,7 @@
     oh, ol = own_ref[:, :NX], own_ref[:, NX:]
     rows = dot(oh, fh, NT) + dot(oh, fl, NT) + dot(ol, fh, NT)
     out_ref[...] = rows[:ROWS]
-    send_block(out_ref, out_hbm, out_sems)
+    fetch(out_ref, out_hbm, sems, 3).wait()
 
 
 def own_rows(values):
@@ -295,12 +302,69 @@
     return jnp.concatenate(pieces, 0)
 
 
-def live_mass(ids_ref, parts_ref):
+def live_mass(ids_ref, mass):
     cell = lax.broadcasted_iota(jnp.int32, (64, 128), 0)
     at_x = 2 * ids_ref[0] - 1 + cell // 16
     at_z = 2 * ids_ref[1] - 1 + cell % 4
     inside = (at_x >= 0) & (at_x < 64) & (at_z >= 0) & (at_z < 16)
-    return jnp.where(inside, parts_ref[7], 0.0)
+    return jnp.where(inside, mass, 0.0)
+
+
+def pack_kernel(
+    count_ref, parts_hbm, eta_hbm, own_hbm, up_hbm, down_hbm,
+    parts_ref, eta_ref, own_ref, up_ref, down_ref, sems,
+):
+    wait_all([fetch(parts_hbm, parts_ref, sems, 3), fetch(eta_hbm, eta_ref, sems, 4)])
+    lane = lax.broadcasted_iota(jnp.int32, (2, 128), 1)
+    row = lax.broadcasted_iota(jnp.int32, (2, 128), 0)
+    for i in range(8):
+        for cx in range(2):
+            for cy in range(4):
+                value = parts_ref[i, cx, cy]
+                if i == 7:
+                    live = jnp.where(row == 0, count_ref[cx, cy, 0], count_ref[cx, cy, 1])
+                    value = jnp.where(lane < live, value, 0.0)
+                at = 16 * i + 8 * cx + 2 * cy
+                own_ref[at : at + 2] = value
+                at = 8 * i + 2 * cy
+                side_ref = up_ref if cx == 1 else down_ref
+                side_ref[at : at + 2] = value
+    for j in range(4):
+        up_ref[64 + 16 * j : 80 + 16 * j] = eta_ref[16:, 128 * j : 128 * j + 128]
+        down_ref[64 + 24 * j : 88 + 24 * j] = eta_ref[:24, 128 * j : 128 * j + 128]
+    wait_all([
+        fetch(up_ref, up_hbm, sems, 0),
+        fetch(down_ref, down_hbm, sems, 1),
+        fetch(own_ref, own_hbm, sems, 2),
+    ])
+
+
+def extend_kernel(
+    before_hbm, own_hbm, after_hbm, eta_hbm, wide_hbm, low_hbm, high_hbm, rows_hbm,
+    before_ref, own_ref, after_ref, wide_ref, low_ref, high_ref, rows_ref, sems,
+):
+    wait_all([
+        fetch(before_hbm, before_ref, sems, 4),
+        fetch(own_hbm, own_ref, sems, 5),
+        fetch(after_hbm, after_ref, sems, 6),
+        fetch(eta_hbm, rows_ref.at[16:48], sems, 7),
+    ])
+    for i in range(8):
+        wide_ref[32 * i : 32 * i + 8] = before_ref[8 * i : 8 * i + 8]
+        wide_ref[32 * i + 8 : 32 * i + 24] = own_ref[16 * i : 16 * i + 16]
+        wide_ref[32 * i + 24 : 32 * i + 32] = after_ref[8 * i : 8 * i + 8]
+    for i in range(8):
+        low_ref[16 * i : 16 * i + 16] = wide_ref[pl.ds(32 * i, 16, stride=2), :]
+        high_ref[16 * i : 16 * i + 16] = wide_ref[pl.ds(32 * i + 1, 16, stride=2), :]
+    for j in range(4):
+        rows_ref[:16, 128 * j : 128 * j + 128] = before_ref[64 + 16 * j : 80 + 16 * j]
+        rows_ref[48:, 128 * j : 128 * j + 128] = after_ref[64 + 24 * j : 88 + 24 * j]
+    wait_all([
+        fetch(low_ref, low_hbm, sems, 0),
+        fetch(high_ref, high_hbm, sems, 1),
+        fetch(wide_ref, wide_hbm, sems, 2),
+        fetch(rows_ref, rows_hbm, sems, 3),
+    ])
 
 
 def spread_own(values, out_ref):
@@ -315,108 +379,186 @@
             out_ref[o, i] = jnp.broadcast_to(columns[:, k : k + 1], (128, 128))
 
 
-def reach_groups(count_ref):
-    return (count_ref[0] + GROUP - 1) // GROUP
+def reach_groups(count_ref, part):
+    used = jnp.clip(count_ref[0] - part * PART, 0, PART)
+    return (used + GROUP - 1) // GROUP
 
 
 def reach_copy(source, target, sems, group):
-    span = pl.ds(pl.multiple_of(group * GROUP, GROUP), GROUP)
-    return pltpu.make_async_copy(source.at[span], target.at[span], sems.at[group])
-
-
-def reach_kernel(
-    ids_ref, pairs_ref, count_ref, parts_ref, token_ref,
-    reach_hbm, place_hbm, sum_hbm, done_ref,
-    reach_ref, place_ref, density_ref, sum_ref, chan_ref, sems, reach_sems,
-):
-    mass = live_mass(ids_ref, parts_ref)
-    chan_ref[0] = parts_ref[6]
-    chan_ref[1] = KERNEL_COEF * mass
-    chan_ref[2] = (-2.0 * KERNEL_COEF) * (mass / parts_ref[6])
-    spread_own([parts_ref[i] for i in range(3)], place_ref)
-    copies = [fetch(place_ref, place_hbm, sems, 0)]
-    spread_own([parts_ref[6]], density_ref)
-    sum_ref[...] = jnp.zeros_like(sum_ref)
-    done_ref[...] = token_ref[...]
+    return pltpu.make_async_copy(source, target, sems.at[group])
+
+
+def span_of(ref, group):
+    return ref.at[pl.ds(pl.multiple_of(group * GROUP, GROUP), GROUP)]
+
+
+def reach_channels(ids_ref, cells_ref, chan_ref):
+    parts = [cells_ref[64 * i : 64 * i + 64] for i in (0, 1, 2, 6, 7)]
+    mass = live_mass(ids_ref, parts[4])
+    for i in range(3):
+        chan_ref[i] = 0.5 * parts[i]
+    chan_ref[3] = parts[3]
+    chan_ref[4] = (2.0 * KERNEL_COEF) * mass
+    chan_ref[5] = (-2.0 * KERNEL_COEF) * (mass / parts[3])
+
+
+def reach_pairs(
+    part, pairs_ref, count_ref, chan_ref, place_ref, density_ref,
+    reach_ref, reach_hbm, sum_ref, reach_sems,
+):
     def add_pair(t, carry):
         o = pairs_ref[0, t]
         cell = pairs_ref[1, t]
-        place = [parts_ref[i, pl.ds(cell, 1), :] for i in range(3)]
-        density, weight, volume = [chan_ref[i, pl.ds(cell, 1), :] for i in range(3)]
+        place = [chan_ref[i, pl.ds(cell, 1), :] for i in range(3)]
+        density, weight, volume = [chan_ref[i, pl.ds(cell, 1), :] for i in range(3, 6)]
         for piece in range(4):
             span = pl.ds(32 * piece, 32)
             gap_x = place_ref[o, 0, span, :] - place[0]
             gap_y = place_ref[o, 1, span, :] - place[1]
             gap_z = place_ref[o, 2, span, :] - place[2]
-            radius = jnp.sqrt(gap_x * gap_x + gap_y * gap_y + gap_z * gap_z)
-            reach = jnp.maximum(1.0 - 0.5 * radius, 0.0)
+            square = gap_x * gap_x + gap_y * gap_y + gap_z * gap_z
+            reach = jnp.maximum(1.0 - square * lax.rsqrt(jnp.maximum(square, 1e-30)), 0.0)
             reach = reach * reach * reach
-            reach_ref[t, span, :] = reach * weight
+            reach_ref[t - part * PART, span, :] = reach * weight
             sum_ref[o, span, :] += reach * ((density - density_ref[o, 0, span, :]) * volume)
         return carry
 
     def add_group(g, carry):
-        last = jnp.minimum(GROUP * g + GROUP, count_ref[0])
-        lax.fori_loop(GROUP * g, last, add_pair, 0)
-        reach_copy(reach_ref, reach_hbm, reach_sems, g).start()
+        start = part * PART + GROUP * g
+        stop = jnp.minimum(start + GROUP, count_ref[0])
+        lax.fori_loop(start, stop, add_pair, 0)
+        reach_copy(span_of(reach_ref, g), span_of(reach_hbm, g), reach_sems, g).start()
         return carry
 
+    lax.fori_loop(0, reach_groups(count_ref, part), add_group, 0)
+
+
+def reach_end(part, count_ref, reach_ref, reach_hbm, reach_sems):
     def wait_group(g, carry):
-        reach_copy(reach_ref, reach_hbm, reach_sems, g).wait()
+        reach_copy(span_of(reach_ref, g), span_of(reach_hbm, g), reach_sems, g).wait()
         return carry
 
-    groups = reach_groups(count_ref)
-    lax.fori_loop(0, groups, add_group, 0)
+    lax.fori_loop(0, reach_groups(count_ref, part), wait_group, 0)
+
+
+def reach_kernel(
+    ids_ref, pairs_ref, count_ref, wide_hbm, below_hbm, above_hbm, token_ref,
+    reach_hbm, place_hbm, density_hbm, sum_hbm, cells_hbm, done_ref,
+    wide_ref, below_ref, above_ref, reach_ref, place_ref, density_ref, sum_ref, cells_ref,
+    chan_ref, sems, reach_sems,
+):
+    copies = [
+        fetch(wide_hbm, wide_ref, sems, 3),
+        fetch(below_hbm, below_ref, sems, 4),
+        fetch(above_hbm, above_ref, sems, 5),
+    ]
+    sum_ref[...] = jnp.zeros_like(sum_ref)
+    done_ref[...] = token_ref[...]
+    wait_all(copies)
+    for i in range(8):
+        low = wide_ref[pl.ds(32 * i, 16, stride=2), :]
+        high = wide_ref[pl.ds(32 * i + 1, 16, stride=2), :]
+        cells_ref[pl.ds(64 * i, 16, stride=4), :] = below_ref[16 * i : 16 * i + 16]
+        cells_ref[pl.ds(64 * i + 1, 16, stride=4), :] = low
+        cells_ref[pl.ds(64 * i + 2, 16, stride=4), :] = high
+        cells_ref[pl.ds(64 * i + 3, 16, stride=4), :] = above_ref[16 * i : 16 * i + 16]
+    copies = [fetch(cells_ref, cells_hbm, sems, 2)]
+    reach_channels(ids_ref, cells_ref, chan_ref)
+    spread_own([chan_ref[i] for i in range(3)], place_ref)
+    copies.append(fetch(place_ref, place_hbm, sems, 0))
+    spread_own([chan_ref[3]], density_ref)
+    copies.append(fetch(density_ref, density_hbm, sems, 6))
+    reach_pairs(
+        0, pairs_ref, count_ref, chan_ref, place_ref, density_ref,
+        reach_ref, reach_hbm, sum_ref, reach_sems,
+    )
     copies.append(fetch(sum_ref, sum_hbm, sems, 1))
-    lax.fori_loop(0, groups, wait_group, 0)
+    reach_end(0, count_ref, reach_ref, reach_hbm, reach_sems)
     wait_all(copies)
 
 
-def last_kernel(
-    ids_ref, pairs_ref, count_ref, got_ref, before_hbm, eta_hbm, after_hbm, parts_hbm, y_ref,
-    reach_hbm, place_hbm, sum_hbm, surface_ref, rate_ref,
-    eta_ref, parts_ref, reach_ref, place_ref, sum_ref,
-    field_ref, target_ref, speed_ref, own_ref, sems, reach_sems,
+def reach_rest_kernel(
+    ids_ref, pairs_ref, count_ref, place_hbm, density_hbm, before_hbm, cells_hbm, token_ref,
+    reach_hbm, sum_hbm, done_ref,
+    reach_ref, place_ref, density_ref, sum_ref, cells_ref, chan_ref, sems, reach_sems,
 ):
     copies = [
-        fetch(before_hbm, eta_ref.at[:16], sems, 0),
-        fetch(eta_hbm, eta_ref.at[16:48], sems, 1),
-        fetch(after_hbm, eta_ref.at[48:], sems, 2),
-        fetch(parts_hbm, parts_ref, sems, 3),
-        fetch(place_hbm, place_ref, sems, 4),
-        fetch(sum_hbm, sum_ref, sems, 5),
+        fetch(cells_hbm, cells_ref, sems, 0),
+        fetch(place_hbm, place_ref, sems, 1),
+        fetch(density_hbm, density_ref, sems, 2),
+        fetch(before_hbm, sum_ref, sems, 3),
     ]
+    done_ref[...] = token_ref[...]
+    wait_all(copies[:1])
+    reach_channels(ids_ref, cells_ref, chan_ref)
+    wait_all(copies[1:])
+    reach_pairs(
+        1, pairs_ref, count_ref, chan_ref, place_ref, density_ref,
+        reach_ref, reach_hbm, sum_ref, reach_sems,
+    )
+    last_copy = fetch(sum_ref, sum_hbm, sems, 4)
+    reach_end(1, count_ref, reach_ref, reach_hbm, reach_sems)
+    last_copy.wait()
+
+
+def last_kernel(ids_ref, pairs_ref, count_ref, *refs):
+    blocks_hbm, refs = refs[:8], refs[8:]
+    (
+        eta_hbm, cells_hbm, y_ref, reach_hbm, rest_hbm, place_hbm, sum_hbm, surface_ref, rate_ref,
+        blocks, eta_ref, cells_ref, reach_ref, place_ref, sum_ref,
+        coef_ref, field_ref, target_ref, speed_ref, half_ref, own_ref, sems, reach_sems,
+    ) = refs
+    block_copies = [fetch(blocks_hbm[i], blocks.at[i], sems, 4 + i) for i in range(8)]
+    copies = [
+        fetch(eta_hbm, eta_ref, sems, 0),
+        fetch(cells_hbm, cells_ref, sems, 1),
+        fetch(place_hbm, place_ref, sems, 2),
+        fetch(sum_hbm, sum_ref, sems, 3),
+    ]
 
     def start_group(g, carry):
-        reach_copy(reach_hbm, reach_ref, reach_sems, g).start()
+        reach_copy(span_of(reach_hbm, g), span_of(reach_ref, g), reach_sems, g).start()
         return carry
 
+    def start_rest(g, carry):
+        at = g + PART // GROUP
+        reach_copy(span_of(rest_hbm, g), span_of(reach_ref, at), reach_sems, at).start()
+        return carry
+
     def wait_group(g, carry):
-        reach_copy(reach_hbm, reach_ref, reach_sems, g).wait()
+        reach_copy(span_of(reach_hbm, g), span_of(reach_ref, g), reach_sems, g).wait()
         return carry
 
-    groups = reach_groups(count_ref)
+    def wait_rest(g, carry):
+        at = g + PART // GROUP
+        reach_copy(span_of(rest_hbm, g), span_of(reach_ref, at), reach_sems, at).wait()
+        return carry
+
+    groups, rest_groups = reach_groups(count_ref, 0), reach_groups(count_ref, 1)
     lax.fori_loop(0, groups, start_group, 0)
+    lax.fori_loop(0, rest_groups, start_rest, 0)
     slab = ids_ref[0]
-    mask = low_lanes((ROWS, 128))
-    fields = []
-    for f in range(5):
-        pieces = []
-        lane = 128 * (f // 2)
-        for j in range(4):
-            first = got_ref[2 * j, :, lane : lane + 128] if f < 4 else got_ref[2 * j, :, 256:320]
-            second = got_ref[2 * j + 1, :, lane : lane + 128] if f < 4 else got_ref[2 * j + 1, :, 256:320]
-            if f == 4:
-                pieces.append(jnp.concatenate([first, second], 1))
-            elif f % 2 == 0:
-                pieces.append(jnp.where(mask, first, pltpu.roll(second, 64, 1)))
-            else:
-                pieces.append(jnp.where(mask, pltpu.roll(first, 64, 1), second))
-        fields.append(jnp.concatenate(pieces, 1))
-    fields = data_by_table(
-        jnp.concatenate(fields, 0), y_ref[0], y_ref[1], NN
-    )
-    wait_all(copies[:4])
+    layer = ids_ref[1]
+    wait_all(block_copies)
+    for step in range(4):
+        share = (layer // 2 + 4 - step) % 4
+        lanes = pl.ds(pl.multiple_of(128 * share, 128), 128)
+        mine, theirs = blocks[step], blocks[4 + step]
+        for f in range(0, 4, 2):
+            here = mine[:, 64 * f : 64 * f + 128]
+            there = theirs[:, 64 * f : 64 * f + 128]
+            first = jnp.where(layer % 2 == 0, here, there)
+            second = jnp.where(layer % 2 == 0, there, here)
+            first, second = by_share(first, second)
+            coef_ref[ROWS * f : ROWS * f + ROWS, lanes] = first
+            coef_ref[ROWS * f + ROWS : ROWS * f + 2 * ROWS, lanes] = second
+        here, there = mine[:, 256:320], theirs[:, 256:320]
+        first = jnp.where(layer % 2 == 0, here, there)
+        second = jnp.where(layer % 2 == 0, there, here)
+        coef_ref[4 * ROWS :, lanes] = jnp.concatenate([first, second], 1)
+    fields = data_by_table(coef_ref[...], y_ref[0], y_ref[1], NN)
+    wait_all(copies[:2])
+    parts = [cells_ref[64 * i : 64 * i + 64] for i in range(8)]
     eta = eta_ref[...]
     vertical = (
         fields[:ROWS]
@@ -434,8 +576,8 @@
         first_row = pl.multiple_of(16 * cx, 16)
         origin = (32 * slab - 16 + 16 * cx).astype(F32)
         found = [[], [], []]
-        place_x = parts_ref[0, pl.ds(first_row, 16), :] * 8.0 - origin
-        place_y = parts_ref[1, pl.ds(first_row, 16), :] * 64.0
+        place_x = cells_ref[pl.ds(first_row, 16), :] * 8.0 - origin
+        place_y = cells_ref[pl.ds(pl.multiple_of(first_row + 64, 16), 16), :] * 64.0
         for cy in range(4):
             for cz in range(4):
                 cell = 4 * cy + cz
@@ -458,20 +600,22 @@
         return carry
 
     lax.fori_loop(0, 4, sample, 0)
-    depth = jnp.exp((parts_ref[2] - 32.0) * (1.0 / 32.0))
-    close = jnp.clip(1.0 - parts_ref[0] * (1.0 / 256.0), 0.0, 1.0)
+    depth = jnp.exp((parts[2] - 32.0) * (1.0 / 32.0))
+    close = jnp.clip(1.0 - parts[0] * (1.0 / 256.0), 0.0, 1.0)
     close = close * close
     for i in range(3):
-        speed = parts_ref[3 + i]
+        half_ref[i] = 0.5 * parts[i]
+        speed = parts[3 + i]
         speed_ref[i] = speed + close * (target_ref[i] * depth - speed)
     spread_own([speed_ref[i] for i in range(3)], own_ref)
-    wait_all(copies[4:])
+    wait_all(copies[2:])
     lax.fori_loop(0, groups, wait_group, 0)
+    lax.fori_loop(0, rest_groups, wait_rest, 0)
 
     def add_pair(t, carry):
         o = pairs_ref[0, t]
         cell = pairs_ref[1, t]
-        place = [parts_ref[i, pl.ds(cell, 1), :] for i in range(3)]
+        place = [half_ref[i, pl.ds(cell, 1), :] for i in range(3)]
         speed = [speed_ref[i, pl.ds(cell, 1), :] for i in range(3)]
         for piece in range(4):
             span = pl.ds(32 * piece, 32)
@@ -491,7 +635,7 @@
         high, rest = split(total)
         middle, last = split(total - high.astype(F32))
         rates.append(dot(ones, jnp.concatenate([high, middle, last], 1), NT)[:1])
-    mass = own_rows(parts_ref[7])
+    mass = own_rows(parts[7])
     rate_ref[...] = jnp.where(mass > 0.0, jnp.concatenate(rates, 0), 0.0)
 
 
@@ -536,18 +680,31 @@
     x = jnp.asarray(table["x"])
     own = jnp.asarray(table["own"])
 
-    live = jnp.arange(128, dtype=jnp.int32) < cell_count[..., None]
-    mass = jnp.where(live, particles[7], 0.0)
-    cells = jnp.concatenate([particles[:7], mass[None]], 0)
-    eta_before = passed(eta[16:], "gx", 1)
-    eta_after = passed(eta[:24], "gx", -1)
-    cells_before = passed(cells[:, 1:], "gx", 1)
-    cells_after = passed(cells[:, :1], "gx", -1)
-    cells = jnp.concatenate([cells_before, cells, cells_after], 1)
-    below = passed(cells[:, :, :, 1:], "gz", 1)
-    above = passed(cells[:, :, :, :1], "gz", -1)
-    cells = jnp.concatenate([below, cells, above], 3)
-    cells = cells.reshape(8, 64, 128)
+    half_layers = lax.axis_size("gz") // 2
+
+    own_cells, up, down = call(
+        pack_kernel, (cell_count, particles, eta), "SHH",
+        [((128, 128), "H"), ((128, 128), "H"), ((160, 128), "H")], "pack", 4,
+        [(8, 2, 4, 2, 128), (32, NY), (128, 128), (128, 128), (160, 128), dma_sems(5)],
+    )
+    cells_before = passed(up, "gx", 1)
+    cells_after = passed(down, "gx", -1)
+    wide, low, high, eta_rows = call(
+        extend_kernel, (cells_before, own_cells, cells_after, eta), "HHHH",
+        [((256, 128), "H"), ((128, 128), "H"), ((128, 128), "H"), ((ROWS, NY), "H")], "extend", 4,
+        [
+            (128, 128),
+            (128, 128),
+            (160, 128),
+            (256, 128),
+            (128, 128),
+            (128, 128),
+            (ROWS, NY),
+            dma_sems(8),
+        ],
+    )
+    below = passed(high, "gz", 1)
+    above = passed(low, "gz", -1)
     pairs = pair_cells.reshape(2, 96)
     count = pair_count.reshape(1)
 
@@ -565,8 +722,8 @@
     gathered = swap(block, "gx").reshape(1024, 128)
     block, first = call(
         first_kernel,
-        (ids, gathered, x, cells_before, cells_after, eta_before, eta_after),
-        "SVVHHHH",
+        (ids, gathered, x, wide),
+        "SVVH",
         [((8, 128, 128), "H"), ((64, NX), "H")],
         "first",
         8,
@@ -583,42 +740,66 @@
         [(8, 64, 128), (128, NY), (128, NY), dma_sems(10)],
     )
     got = swap(block, "gz")
-    reach, place, before, token = call(
+    reach, place, density, before, cells, token = call(
         reach_kernel,
-        (ids, pairs, count, cells, token),
-        "SSSVV",
+        (ids, pairs, count, wide, below, above, token),
+        "SSSHHHV",
         [
-            ((96, 128, 128), "H"),
+            ((PART, 128, 128), "H"),
             ((16, 3, 128, 128), "H"),
+            ((16, 1, 128, 128), "H"),
             ((16, 128, 128), "H"),
+            ((512, 128), "H"),
             ((8, 128), "V"),
         ],
         "reach",
         16,
         [
-            (96, 128, 128),
+            (256, 128),
+            (128, 128),
+            (128, 128),
+            (PART, 128, 128),
             (16, 3, 128, 128),
             (16, 1, 128, 128),
             (16, 128, 128),
-            (3, 64, 128),
-            dma_sems(2),
-            dma_sems(96 // GROUP),
+            (512, 128),
+            (6, 64, 128),
+            dma_sems(7),
+            dma_sems(PART // GROUP),
         ],
     )
-    block, second = call(
+    block, second, token = call(
         third_kernel,
         (ids, got, x, token),
         "SVVV",
-        [((8, 64, 128), "H"), ((64, NX), "H")],
+        [((8, 64, 128), "H"), ((64, NX), "H"), ((8, 128), "V")],
         "third",
         8,
         [(8, 64, 128), (64, NX), dma_sems(9)],
     )
     got = swap(block, "gz")
+    rest, before, token = call(
+        reach_rest_kernel,
+        (ids, pairs, count, place, density, before, cells, token),
+        "SSSHHHHV",
+        [((PART, 128, 128), "H"), ((16, 128, 128), "H"), ((8, 128), "V")],
+        "rest",
+        16,
+        [
+            (PART, 128, 128),
+            (16, 3, 128, 128),
+            (16, 1, 128, 128),
+            (16, 128, 128),
+            (512, 128),
+            (6, 64, 128),
+            dma_sems(5),
+            dma_sems(PART // GROUP),
+        ],
+    )
     (block,) = call(
         fourth_kernel,
-        (got, eta_part, curve, y),
-        "VHHV",
+        (got, eta_part, curve, y, token),
+        "VHHVV",
         [((8, 64, 128), "H")],
         "fourth",
         8,
@@ -629,7 +810,7 @@
         fifth_kernel,
         (ids, got, x, own, first, second),
         "SVVHHH",
-        [((8, ROWS, 320), "H")],
+        [((ROWS, 320), "H")],
         "fifth",
         8,
         [
@@ -637,31 +818,45 @@
             (ROWS, 320),
             (64, NX),
             (64, NX),
-            dma_sems(3),
-            dma_sems(8),
+            dma_sems(4),
         ],
     )
-    got = swap(block, "gz")
+    along = [block] + [
+        lax.ppermute(
+            block,
+            "gz",
+            [
+                (2 * i + core, 2 * ((i + step) % half_layers) + core)
+                for i in range(half_layers)
+                for core in range(2)
+            ],
+        )
+        for step in range(1, half_layers)
+    ]
+    across = [
+        lax.ppermute(b, "gz", [(i, i ^ 1) for i in range(2 * half_layers)]) for b in along
+    ]
     surface, rate = call(
         last_kernel,
-        (
-            ids, pairs, count, got, eta_before, eta, eta_after, cells, y, reach, place, before
-        ),
-        "SSSVHHHHVHHH",
+        (ids, pairs, count, *along, *across, eta_rows, cells, y, reach, rest, place, before),
+        "SSS" + "H" * 10 + "VHHHH",
         [((32, NY), "V"), ((16, 128), "V")],
         "last",
         24,
         [
+            (8, ROWS, 320),
             (ROWS, NY),
-            (8, 64, 128),
+            (512, 128),
             (96, 128, 128),
             (16, 3, 128, 128),
             (16, 128, 128),
+            (5 * ROWS, NY),
             (6, ROWS, NY),
             (3, 64, 128),
             (3, 64, 128),
+            (3, 64, 128),
             (16, 3, 128, 128),
-            dma_sems(6),
+            dma_sems(12),
             dma_sems(96 // GROUP),
         ],
     )

time: 132 us -> 124 us (0.939)
  blocking collectives: 40.1 us -> 10.7 us
  starting transfers between devices: 32.2 us -> 44.2 us
  Pallas kernels: 36.1 us -> 46.2 us
  waiting for transfers between devices: 13.9 us -> 18.3 us
  other arithmetic: 2.81 us -> 0.08 us
  local copies, waits for them, and re-layouts: 4.18 us -> 2.33 us
    all_to_all x3 -> x1, blocking collectives: 40.1 us -> 10.7 us  [swap(): return lax.all_to_all(block, axis, split_axis=0, concat_axis=0, tiled=True)]
    ppermute x0 -> x7, starting transfers between devices: none -> 10.4 us  [the longest x4 8.23 us: per_device(): lax.ppermute(b, 'gz', [(i, i ^ 1) for i in range(2 * half_layers)])]
    pallas_call x8 -> x11, Pallas kernels: 36.1 us -> 46.2 us  [call(): pl.pallas_call(kernel, out_shape=[pltpu.HBM(s, F32) if k == 'H' else jax....]
    all_to_all x3 -> x4, starting transfers between devices: 24.1 us -> 27.5 us  [swap(): return lax.all_to_all(block, axis, split_axis=0, concat_axis=0, tiled=True)]
    ppermute x6 -> x4, waiting for transfers between devices: 13.5 us -> 16.8 us  [passed(): lax.ppermute(values, axis, [(i, (i + by) % size) for i in range(size)])]
    slice x4 -> x0, local copies, waits for them, and re-layouts: 2.49 us -> none  [the longest x1 0.82 us: per_device(): cells = jnp.concatenate([particles[:7], mass[None]], 0)]
    concatenate x3 -> x0, other arithmetic: 1.97 us -> none  [the longest x1 1.1 us: per_device(): cells = jnp.concatenate([below, cells, above], 3)]
    ppermute x6 -> x4, starting transfers between devices: 8.08 us -> 6.28 us  [passed(): lax.ppermute(values, axis, [(i, (i + by) % size) for i in range(size)])]
  transfers between devices with their start and end apart: 9 -> 15, of which waited for: 4 -> 6; matrix products, arithmetic and copies ran while one was open for 5% -> 1% of each run, Pallas kernels for 7% -> 15%
where the time goes in v3:
time: 124 us; the launch traced here: 123 us
  Pallas kernels  46.2 us (37%)
  starting transfers between devices  44.2 us (36%)
  waiting for transfers between devices  18.3 us (15%)
  blocking collectives  10.7 us (9%)
  local copies, waits for them, and re-layouts  2.33 us (2%)
  between operations  1.68 us (1%)
    pallas_call x11, Pallas kernels, call(): pl.pallas_call(kernel, out_shape=[pltpu.HBM(s, F32) if k == 'H' else jax....  46.2 us
    all_to_all x4, starting transfers between devices, swap(): return lax.all_to_all(block, axis, split_axis=0, concat_axis=0, tiled=True)  27.5 us
    ppermute x4, waiting for transfers between devices, passed(): lax.ppermute(values, axis, [(i, (i + by) % size) for i in range(size)])  16.8 us
    all_to_all x1, blocking collectives, swap(): return lax.all_to_all(block, axis, split_axis=0, concat_axis=0, tiled=True)  10.7 us
    ppermute x4, starting transfers between devices, per_device(): lax.ppermute(b, 'gz', [(i, i ^ 1) for i in range(2 * half_layers)])  8.23 us
    ppermute x4, starting transfers between devices, passed(): lax.ppermute(values, axis, [(i, (i + by) % size) for i in range(size)])  6.28 us
  transfers between devices with their start and end apart: 15, of which 6 were waited for; matrix products, arithmetic and copies ran while one was open for 1% of the time, Pallas kernels for 15%

profile of v3, /device:TPU:1, one launch (start us, length us, event | category | flops | bytes accessed | tf_op | source)
XLA Modules:
  0.0 123.5 jit_solution(15367332621503464196)
XLA Ops:
  0.6 0.0 copy-start
  0.6 0.1 pad_add_fusion.ids_ref
  0.7 3.1 %start.1 = f32[32,32,128]{2,1,0:T(8,128)} custom-call(s32[2]{0:T(128)S(1)} %pad_add_fusion.ids_ref, f32[32,512]{1,0:T(8,128)} %phis_hbm.1, f32[32,512]{1,0:T(8,128)} %eta_hbm.5, bf16[2,512,512]{2,1,0:T(8,128)(2,1)} %constant.15.clone.y_hbm.y_ref.refs_10_), custom_call_target="tpu_custom_call" | custom-call | tf_op jit(solution)/shard_map/start/pallas_call | solution.py:648
  3.9 12.0 %all-to-all-start = ((f32[32,32,128]{2,1,0:T(8,128)}), f32[32,32,128]{2,1,0:T(8,128)}, u32[]{:S(2)}, u32[]{:S(2)}) async-start(f32[32,32,128]{2,1,0:T(8,128)} %start.1), calls=%async_computation | async-start | bytes 1048576 | tf_op jit(solution)/shard_map/all_to_all | solution.py:671
  15.9 0.8 copy.11.count_ref
  16.7 2.2 %pack.1 = (f32[128,128]{1,0:T(8,128)}, f32[128,128]{1,0:T(8,128)}, f32[160,128]{1,0:T(8,128)}) custom-call(s32[2,4,2]{2,1,0:T(4,128)S(1)} %copy.11.count_ref, f32[8,2,4,2,128]{4,3,2,1,0:T(2,128)} %parts_hbm.1, f32[32,512]{1,0:T(8,128)} %eta_hbm.5), custom_call_target="tpu_custom_call" | custom-call | tf_op jit(solution)/shard_map/pack/pallas_call | solution.py:648
  18.9 4.6 %collective-permute-start.1 = (f32[160,128]{1,0:T(8,128)}, f32[160,128]{1,0:T(8,128)S(1)}, u32[]{:S(2)}, u32[]{:S(2)}) collective-permute-start(f32[160,128]{1,0:T(8,128)} %get-tuple-element.31), channel_id=1, source_target_pairs={{0,248},{8,0},{16,8},{24,16},{32,24},{40,32},{48,40},{56,48},{64,5... | collective-permute-start | bytes 245768 | tf_op jit(solution)/shard_map/ppermute | solution.py:667
  23.5 0.0 collective-permute-start
  23.5 9.2 %collective-permute-done.before_hbm = f32[128,128]{1,0:T(8,128)S(1)} collective-permute-done((f32[128,128]{1,0:T(8,128)}, f32[128,128]{1,0:T(8,128)S(1)}, u32[]{:S(2)}, u32[]{:S(2)}) %collective-permute-start) | collective-permute-done | bytes 65568 | tf_op jit(solution)/shard_map/ppermute | solution.py:667
  32.8 0.0 collective-permute-done.1.after_hbm
  32.8 0.6 copy-done.13
  33.4 0.0 copy-done.12
  33.4 1.8 %extend.1 = (f32[256,128]{1,0:T(8,128)}, f32[128,128]{1,0:T(8,128)}, f32[128,128]{1,0:T(8,128)}, f32[72,512]{1,0:T(8,128)}) custom-call(f32[128,128]{1,0:T(8,128)} %copy-done.13, f32[128,128]{1,0:T(8,128)} %get-tuple-element.30.own_hbm, f32[160,128]{1,0:T(8,128)} %copy-done.12, f32[32,512]{1,0:T(8,128)} %eta_hbm.5), custom_call_target="tpu_custom_call" | custom-call | tf_op jit(solution)/shard_map/extend/pallas_call | solution.py:648
  35.3 0.0 all-to-all-done
  35.3 0.0 copy-start.2
  35.3 3.1 %first.1 = (f32[8,128,128]{2,1,0:T(8,128)}, f32[64,1024]{1,0:T(8,128)}) custom-call(s32[2]{0:T(128)S(1)} %pad_add_fusion.ids_ref, f32[1024,128]{1,0:T(8,128)} %bitcast.4.got_ref.gathered_ref, bf16[4,512,512]{2,1,0:T(8,128)(2,1)S(1)} %copy-done, f32[256,128]{1,0:T(8,128)} %get-tuple-element.32.wide_hbm), custom_call_target="tpu_custom_call" | custom-call | tf_op jit(solution)/shard_map/first/pallas_call | solution.py:648
  38.4 6.0 %all-to-all-start.1 = ((f32[8,128,128]{2,1,0:T(8,128)}), f32[8,128,128]{2,1,0:T(8,128)}, u32[]{:S(2)}, u32[]{:S(2)}) async-start(f32[8,128,128]{2,1,0:T(8,128)} %get-tuple-element.33), calls=%async_computation.1 | async-start | bytes 1048576 | tf_op jit(solution)/shard_map/all_to_all | solution.py:671
  44.4 1.6 %collective-permute-start.2 = (f32[128,128]{1,0:T(8,128)S(1)}, f32[128,128]{1,0:T(8,128)S(1)}, u32[]{:S(2)}, u32[]{:S(2)}) collective-permute-start(f32[128,128]{1,0:T(8,128)S(1)} %copy-done.15), channel_id=1, source_target_pairs={{0,1},{1,2},{2,3},{3,4},{4,5},{5,6},{6,7},{7,0},{8,9},{9,10},{10,1... | collective-permute-start | bytes 196616 | tf_op jit(solution)/shard_map/ppermute | solution.py:667
  46.0 0.0 collective-permute-start.3
  46.0 5.4 %collective-permute-done.2.below_hbm = f32[128,128]{1,0:T(8,128)S(1)} collective-permute-done((f32[128,128]{1,0:T(8,128)S(1)}, f32[128,128]{1,0:T(8,128)S(1)}, u32[]{:S(2)}, u32[]{:S(2)}) %collective-permute-start.2) | collective-permute-done | bytes 65568 | tf_op jit(solution)/shard_map/ppermute | solution.py:667
  51.4 2.2 %collective-permute-done.3.above_hbm = f32[128,128]{1,0:T(8,128)S(1)} collective-permute-done((f32[128,128]{1,0:T(8,128)S(1)}, f32[128,128]{1,0:T(8,128)S(1)}, u32[]{:S(2)}, u32[]{:S(2)}) %collective-permute-start.3) | collective-permute-done | bytes 65568 | tf_op jit(solution)/shard_map/ppermute | solution.py:667
  53.6 0.4 all-to-all-done.1.got_ref
  54.0 0.3 copy-done.4
  54.3 3.0 %second.1 = (f32[8,64,128]{2,1,0:T(8,128)}, f32[128,512]{1,0:T(8,128)}, f32[128,512]{1,0:T(8,128)}, f32[8,128]{1,0:T(8,128)S(1)}) custom-call(f32[8,128,128]{2,1,0:T(8,128)} %all-to-all-done.1.got_ref, f32[1024,128]{1,0:T(8,128)} %bitcast.4.got_ref.gathered_ref, bf16[2,512,512]{2,1,0:T(8,128)(2,1)S(1)} %copy-done.1, f32[128,128]{1,0:T(8,128)} %copy-done.3, ...), custom_call_target="tpu_custom_call" | custom-call | tf_op jit(solution)/shard_map/second/pallas_call | solution.py:648
  57.2 4.7 %all-to-all-start.2 = ((f32[8,64,128]{2,1,0:T(8,128)}), f32[8,64,128]{2,1,0:T(8,128)S(1)}, u32[]{:S(2)}, u32[]{:S(2)}) async-start(f32[8,64,128]{2,1,0:T(8,128)} %get-tuple-element.36), calls=%async_computation.2 | async-start | bytes 524288 | tf_op jit(solution)/shard_map/all_to_all | solution.py:671
  62.7 6.9 %reach.1 = (f32[48,128,128]{2,1,0:T(8,128)}, f32[16,3,128,128]{3,2,1,0:T(8,128)}, f32[16,1,128,128]{3,2,1,0:T(8,128)}, f32[16,128,128]{2,1,0:T(8,128)}, f32[512,128]{1,0:T(8,128)}, /*index=5*/f32[8,128]{1,0:T(8,128)S(1)}) custom-call(s32[2]{0:T(128)S(1)} %pad_add_fusion.ids_ref, s32[2,96]{1,0:T(2,128)S(1)} %bitcast.9, s32[1]{0:T(128)} %bitcast.6.count_ref, ...), custom_call_target="tpu_custom_call" | custom-call | tf_op jit(solution)/shard_map/reach/pallas_call | solution.py:648
  69.6 0.0 all-to-all-done.2.got_ref
  69.6 2.5 %third.1 = (f32[8,64,128]{2,1,0:T(8,128)}, f32[64,1024]{1,0:T(8,128)}, f32[8,128]{1,0:T(8,128)S(1)}) custom-call(s32[2]{0:T(128)S(1)} %pad_add_fusion.ids_ref, f32[8,64,128]{2,1,0:T(8,128)S(1)} %all-to-all-done.2.got_ref, bf16[4,512,512]{2,1,0:T(8,128)(2,1)S(1)} %copy-done, f32[8,128]{1,0:T(8,128)S(1)} %get-tuple-element.38.token_ref), custom_call_target="tpu_custom_call" | custom-call | tf_op jit(solution)/shard_map/third/pallas_call | solution.py:648
  72.1 4.8 %all-to-all-start.3 = ((f32[8,64,128]{2,1,0:T(8,128)}), f32[8,64,128]{2,1,0:T(8,128)S(1)}, u32[]{:S(2)}, u32[]{:S(2)}) async-start(f32[8,64,128]{2,1,0:T(8,128)} %get-tuple-element.39), calls=%async_computation.3 | async-start | bytes 524288 | tf_op jit(solution)/shard_map/all_to_all | solution.py:671
  76.9 6.9 %rest.1 = (f32[48,128,128]{2,1,0:T(8,128)}, f32[16,128,128]{2,1,0:T(8,128)}, f32[8,128]{1,0:T(8,128)S(1)}) custom-call(s32[2]{0:T(128)S(1)} %pad_add_fusion.ids_ref, s32[2,96]{1,0:T(2,128)S(1)} %bitcast.10, s32[1]{0:T(128)} %bitcast.7.count_ref, f32[16,3,128,128]{3,2,1,0:T(8,128)} %get-tuple-element.42.place_hbm.refs_13_, ...), custom_call_target="tpu_custom_call" | custom-call | tf_op jit(solution)/shard_map/rest/pallas_call | solution.py:648
  83.9 0.0 all-to-all-done.3.got_ref
  83.9 2.2 %fourth.1 = f32[8,64,128]{2,1,0:T(8,128)} custom-call(f32[8,64,128]{2,1,0:T(8,128)S(1)} %all-to-all-done.3.got_ref, f32[128,512]{1,0:T(8,128)} %get-tuple-element.40.eta_hbm, f32[128,512]{1,0:T(8,128)} %get-tuple-element.41.curve_hbm, bf16[2,512,512]{2,1,0:T(8,128)(2,1)S(1)} %copy-done.1, f32[8,128]{1,0:T(8,128)S(1)} %get-tuple-element.47.token_ref), custom_call_target="tpu_custom_call" | custom-call | tf_op jit(solution)/shard_map/fourth/pallas_call | solution.py:648
  86.1 10.7 %all_to_all.25.got_ref = f32[8,64,128]{2,1,0:T(8,128)S(1)} all-to-all(f32[8,64,128]{2,1,0:T(8,128)} %fourth.1), channel_id=1, replica_groups=mesh['gx'=32,'gz'=8] {'gz'}, dimensions={0} | all-to-all | bytes 524288 | tf_op jit(solution)/shard_map/all_to_all | solution.py:671
  96.8 3.5 %fifth.1.refs_0_ = f32[72,320]{1,0:T(8,128)} custom-call(s32[2]{0:T(128)S(1)} %pad_add_fusion.ids_ref, f32[8,64,128]{2,1,0:T(8,128)S(1)} %all_to_all.25.got_ref, bf16[4,512,512]{2,1,0:T(8,128)(2,1)S(1)} %copy-done, bf16[1096,2048]{1,0:T(8,128)(2,1)} %constant.17.clone.own_hbm, f32[64,1024]{1,0:T(8,128)} %get-tuple-element.48.first_hbm, ...), custom_call_target="tpu_custom_call" | custom-call | tf_op jit(solution)/shard_map/fifth/pallas_call | solution.py:648
  100.2 1.0 collective-permute-start.6
  101.2 1.2 collective-permute-start.5
  102.4 0.0 collective-permute-start.4
  102.4 1.6 %collective-permute-start.7 = (f32[72,320]{1,0:T(8,128)}, f32[72,320]{1,0:T(8,128)S(1)}, u32[]{:S(2)}, u32[]{:S(2)}) collective-permute-start(f32[72,320]{1,0:T(8,128)} %fifth.1.refs_0_), channel_id=1, source_target_pairs={{0,1},{1,0},{2,3},{3,2},{4,5},{5,4},{6,7},{7,6},{8,9},{9,8},{10,11... | collective-permute-start | bytes 276488 | tf_op jit(solution)/shard_map/ppermute | solution.py:837
  104.0 0.1 collective-permute-done.6.refs_3_
  104.1 3.1 %collective-permute-start.10 = (f32[72,320]{1,0:T(8,128)S(1)}, f32[72,320]{1,0:T(8,128)S(1)}, u32[]{:S(2)}, u32[]{:S(2)}) collective-permute-start(f32[72,320]{1,0:T(8,128)S(1)} %collective-permute-done.6.refs_3_), channel_id=1, source_target_pairs={{0,1},{1,0},{2,3},{3,2},{4,5},{5,4},{6,7},{7,6},{8,9},{9,8},{10,11... | collective-permute-start | bytes 276488 | tf_op jit(solution)/shard_map/ppermute | solution.py:837
  107.2 0.0 collective-permute-done.5.refs_2_
  107.2 2.4 %collective-permute-start.9 = (f32[72,320]{1,0:T(8,128)S(1)}, f32[72,320]{1,0:T(8,128)S(1)}, u32[]{:S(2)}, u32[]{:S(2)}) collective-permute-start(f32[72,320]{1,0:T(8,128)S(1)} %collective-permute-done.5.refs_2_), channel_id=1, source_target_pairs={{0,1},{1,0},{2,3},{3,2},{4,5},{5,4},{6,7},{7,6},{8,9},{9,8},{10,11... | collective-permute-start | bytes 276488 | tf_op jit(solution)/shard_map/ppermute | solution.py:837
  109.6 1.1 collective-permute-start.8
  110.8 0.0 collective-permute-done.7.refs_4_
  110.8 0.0 collective-permute-done.10.refs_7_
  110.8 0.9 collective-permute-done.8.refs_5_
  111.8 0.6 copy-done.11
  112.4 10.9 %last.1 = (f32[32,512]{1,0:T(8,128)}, f32[16,128]{1,0:T(8,128)}) custom-call(s32[2]{0:T(128)S(1)} %pad_add_fusion.ids_ref, s32[2,96]{1,0:T(2,128)S(1)} %bitcast.11, s32[1]{0:T(128)} %bitcast.8.count_ref, f32[72,320]{1,0:T(8,128)} %fifth.1.refs_0_, f32[72,320]{1,0:T(8,128)} %copy-done.7, f32[72,320]{1,0:T(8,128)} %copy-done.6, f32[72,320]{1,0:T(8,128)} %copy-done.5, ...), custom_call_target="tpu_custom_call" | custom-call | tf_op jit(solution)/shard_map/last/pallas_call | solution.py:648
  (28 shorter events, 0.1 us)
Async XLA Ops:
  0.6 34.7 %copy-start = (bf16[4,512,512]{2,1,0:T(8,128)(2,1)S(1)}, bf16[4,512,512]{2,1,0:T(8,128)(2,1)}, u32[]{:S(2)}) copy-start(bf16[4,512,512]{2,1,0:T(8,128)(2,1)} %constant.16.clone.x_ref) | copy-start | bytes 6291460
  0.7 53.5 %copy-start.1 = (bf16[2,512,512]{2,1,0:T(8,128)(2,1)S(1)}, bf16[2,512,512]{2,1,0:T(8,128)(2,1)}, u32[]{:S(2)}) copy-start(bf16[2,512,512]{2,1,0:T(8,128)(2,1)} %constant.15.clone.y_hbm.y_ref.refs_10_) | copy-start | bytes 3145732
  3.9 31.4 %all-to-all-start = ((f32[32,32,128]{2,1,0:T(8,128)}), f32[32,32,128]{2,1,0:T(8,128)}, u32[]{:S(2)}, u32[]{:S(2)}) async-start(f32[32,32,128]{2,1,0:T(8,128)} %start.1), calls=%async_computation | async-start | bytes 1048576 | tf_op jit(solution)/shard_map/all_to_all | solution.py:671
  18.9 13.9 %collective-permute-start.1 = (f32[160,128]{1,0:T(8,128)}, f32[160,128]{1,0:T(8,128)S(1)}, u32[]{:S(2)}, u32[]{:S(2)}) collective-permute-start(f32[160,128]{1,0:T(8,128)} %get-tuple-element.31), channel_id=1, source_target_pairs={{0,248},{8,0},{16,8},{24,16},{32,24},{40,32},{48,40},{56,48},{64,5... | collective-permute-start | bytes 245768 | tf_op jit(solution)/shard_map/ppermute | solution.py:667
  23.5 9.2 %collective-permute-start = (f32[128,128]{1,0:T(8,128)}, f32[128,128]{1,0:T(8,128)S(1)}, u32[]{:S(2)}, u32[]{:S(2)}) collective-permute-start(f32[128,128]{1,0:T(8,128)} %get-tuple-element.29), channel_id=1, source_target_pairs={{0,8},{8,16},{16,24},{24,32},{32,40},{40,48},{48,56},{56,64},{64,7... | collective-permute-start | bytes 196616 | tf_op jit(solution)/shard_map/ppermute | solution.py:667
  32.8 0.6 copy-start.13
  32.8 0.6 copy-start.12
  35.3 9.1 %copy-start.15 = (f32[128,128]{1,0:T(8,128)S(1)}, f32[128,128]{1,0:T(8,128)}, u32[]{:S(2)}) copy-start(f32[128,128]{1,0:T(8,128)} %get-tuple-element.34) | copy-start | bytes 196612
  35.3 10.7 %copy-start.14 = (f32[128,128]{1,0:T(8,128)S(1)}, f32[128,128]{1,0:T(8,128)}, u32[]{:S(2)}) copy-start(f32[128,128]{1,0:T(8,128)} %get-tuple-element.35) | copy-start | bytes 196612
  35.3 27.3 %copy-start.2 = (s32[1,1,2,96]{3,2,1,0:T(2,128)S(1)}, s32[1,1,2,96]{3,2,1,0:T(2,128)}, u32[]{:S(2)}) copy-start(s32[1,1,2,96]{3,2,1,0:T(2,128)} %param.13) | copy-start | bytes 2308
  38.4 15.6 %all-to-all-start.1 = ((f32[8,128,128]{2,1,0:T(8,128)}), f32[8,128,128]{2,1,0:T(8,128)}, u32[]{:S(2)}, u32[]{:S(2)}) async-start(f32[8,128,128]{2,1,0:T(8,128)} %get-tuple-element.33), calls=%async_computation.1 | async-start | bytes 1048576 | tf_op jit(solution)/shard_map/all_to_all | solution.py:671
  44.4 7.1 %collective-permute-start.2 = (f32[128,128]{1,0:T(8,128)S(1)}, f32[128,128]{1,0:T(8,128)S(1)}, u32[]{:S(2)}, u32[]{:S(2)}) collective-permute-start(f32[128,128]{1,0:T(8,128)S(1)} %copy-done.15), channel_id=1, source_target_pairs={{0,1},{1,2},{2,3},{3,4},{4,5},{5,6},{6,7},{7,0},{8,9},{9,10},{10,1... | collective-permute-start | bytes 196616 | tf_op jit(solution)/shard_map/ppermute | solution.py:667
  46.0 7.6 %collective-permute-start.3 = (f32[128,128]{1,0:T(8,128)S(1)}, f32[128,128]{1,0:T(8,128)S(1)}, u32[]{:S(2)}, u32[]{:S(2)}) collective-permute-start(f32[128,128]{1,0:T(8,128)S(1)} %copy-done.14), channel_id=1, source_target_pairs={{0,7},{1,0},{2,1},{3,2},{4,3},{5,4},{6,5},{7,6},{8,15},{9,8},{10,9... | collective-permute-start | bytes 196616 | tf_op jit(solution)/shard_map/ppermute | solution.py:667
  51.4 2.6 %copy-start.3 = (f32[128,128]{1,0:T(8,128)}, f32[128,128]{1,0:T(8,128)S(1)}, u32[]{:S(2)}) copy-start(f32[128,128]{1,0:T(8,128)S(1)} %collective-permute-done.2.below_hbm) | copy-start | bytes 196612
  53.6 0.6 copy-start.4
  57.2 12.4 %all-to-all-start.2 = ((f32[8,64,128]{2,1,0:T(8,128)}), f32[8,64,128]{2,1,0:T(8,128)S(1)}, u32[]{:S(2)}, u32[]{:S(2)}) async-start(f32[8,64,128]{2,1,0:T(8,128)} %get-tuple-element.36), calls=%async_computation.2 | async-start | bytes 524288 | tf_op jit(solution)/shard_map/all_to_all | solution.py:671
  72.1 11.8 %all-to-all-start.3 = ((f32[8,64,128]{2,1,0:T(8,128)}), f32[8,64,128]{2,1,0:T(8,128)S(1)}, u32[]{:S(2)}, u32[]{:S(2)}) async-start(f32[8,64,128]{2,1,0:T(8,128)} %get-tuple-element.39), calls=%async_computation.3 | async-start | bytes 524288 | tf_op jit(solution)/shard_map/all_to_all | solution.py:671
  100.2 3.9 %collective-permute-start.6 = (f32[72,320]{1,0:T(8,128)}, f32[72,320]{1,0:T(8,128)S(1)}, u32[]{:S(2)}, u32[]{:S(2)}) collective-permute-start(f32[72,320]{1,0:T(8,128)} %fifth.1.refs_0_), channel_id=1, source_target_pairs={{0,6},{1,7},{2,0},{3,1},{4,2},{5,3},{6,4},{7,5},{8,14},{9,15},{10,... | collective-permute-start | bytes 276488 | tf_op jit(solution)/shard_map/ppermute | solution.py:825
  101.2 6.0 %collective-permute-start.5 = (f32[72,320]{1,0:T(8,128)}, f32[72,320]{1,0:T(8,128)S(1)}, u32[]{:S(2)}, u32[]{:S(2)}) collective-permute-start(f32[72,320]{1,0:T(8,128)} %fifth.1.refs_0_), channel_id=1, source_target_pairs={{0,4},{1,5},{2,6},{3,7},{4,0},{5,1},{6,2},{7,3},{8,12},{9,13},{10,... | collective-permute-start | bytes 276488 | tf_op jit(solution)/shard_map/ppermute | solution.py:825
  102.4 7.3 %collective-permute-start.4 = (f32[72,320]{1,0:T(8,128)}, f32[72,320]{1,0:T(8,128)S(1)}, u32[]{:S(2)}, u32[]{:S(2)}) collective-permute-start(f32[72,320]{1,0:T(8,128)} %fifth.1.refs_0_), channel_id=1, source_target_pairs={{0,2},{1,3},{2,4},{3,5},{4,6},{5,7},{6,0},{7,1},{8,10},{9,11},{10,... | collective-permute-start | bytes 276488 | tf_op jit(solution)/shard_map/ppermute | solution.py:825
  102.4 8.4 %collective-permute-start.7 = (f32[72,320]{1,0:T(8,128)}, f32[72,320]{1,0:T(8,128)S(1)}, u32[]{:S(2)}, u32[]{:S(2)}) collective-permute-start(f32[72,320]{1,0:T(8,128)} %fifth.1.refs_0_), channel_id=1, source_target_pairs={{0,1},{1,0},{2,3},{3,2},{4,5},{5,4},{6,7},{7,6},{8,9},{9,8},{10,11... | collective-permute-start | bytes 276488 | tf_op jit(solution)/shard_map/ppermute | solution.py:837
  104.1 7.6 %copy-start.5 = (f32[72,320]{1,0:T(8,128)}, f32[72,320]{1,0:T(8,128)S(1)}, u32[]{:S(2)}) copy-start(f32[72,320]{1,0:T(8,128)S(1)} %collective-permute-done.6.refs_3_) | copy-start | bytes 276484
  104.1 6.6 %collective-permute-start.10 = (f32[72,320]{1,0:T(8,128)S(1)}, f32[72,320]{1,0:T(8,128)S(1)}, u32[]{:S(2)}, u32[]{:S(2)}) collective-permute-start(f32[72,320]{1,0:T(8,128)S(1)} %collective-permute-done.6.refs_3_), channel_id=1, source_target_pairs={{0,1},{1,0},{2,3},{3,2},{4,5},{5,4},{6,7},{7,6},{8,9},{9,8},{10,11... | collective-permute-start | bytes 276488 | tf_op jit(solution)/shard_map/ppermute | solution.py:837
  107.2 4.5 %copy-start.6 = (f32[72,320]{1,0:T(8,128)}, f32[72,320]{1,0:T(8,128)S(1)}, u32[]{:S(2)}) copy-start(f32[72,320]{1,0:T(8,128)S(1)} %collective-permute-done.5.refs_2_) | copy-start | bytes 276484
  107.2 3.6 %collective-permute-start.9 = (f32[72,320]{1,0:T(8,128)S(1)}, f32[72,320]{1,0:T(8,128)S(1)}, u32[]{:S(2)}, u32[]{:S(2)}) collective-permute-start(f32[72,320]{1,0:T(8,128)S(1)} %collective-permute-done.5.refs_2_), channel_id=1, source_target_pairs={{0,1},{1,0},{2,3},{3,2},{4,5},{5,4},{6,7},{7,6},{8,9},{9,8},{10,11... | collective-permute-start | bytes 276488 | tf_op jit(solution)/shard_map/ppermute | solution.py:837
  109.6 2.1 %copy-start.7 = (f32[72,320]{1,0:T(8,128)}, f32[72,320]{1,0:T(8,128)S(1)}, u32[]{:S(2)}) copy-start(f32[72,320]{1,0:T(8,128)S(1)} %collective-permute-done.4.refs_1_) | copy-start | bytes 276484
  109.6 2.1 %collective-permute-start.8 = (f32[72,320]{1,0:T(8,128)S(1)}, f32[72,320]{1,0:T(8,128)S(1)}, u32[]{:S(2)}, u32[]{:S(2)}) collective-permute-start(f32[72,320]{1,0:T(8,128)S(1)} %collective-permute-done.4.refs_1_), channel_id=1, source_target_pairs={{0,1},{1,0},{2,3},{3,2},{4,5},{5,4},{6,7},{7,6},{8,9},{9,8},{10,11... | collective-permute-start | bytes 276488 | tf_op jit(solution)/shard_map/ppermute | solution.py:837
  110.8 1.0 copy-start.8
  110.8 1.0 copy-start.9
  110.8 1.0 copy-start.10
  111.7 0.6 copy-start.11

commit v4 on v3

--- a/solution.py
+++ b/solution.py
@@ -24,6 +24,8 @@
 HB = pl.BlockSpec(memory_space=pltpu.HBM)
 GROUP = 8
 PART = 48
+TALL = 80
+EARLY = 2 * ROWS
 
 
 def parts_of(table):
@@ -242,8 +244,9 @@
 
 
 def fourth_kernel(
-    got_ref, eta_hbm, curve_hbm, y_ref, token_ref, out_hbm, out_ref, eta_ref, curve_ref, sems
-):
+    got_ref, eta_hbm, curve_hbm, y_ref, token_ref, out_hbm, next_ref, out_ref, eta_ref, curve_ref, sems
+):
+    next_ref[...] = token_ref[...]
     copies = [fetch(eta_hbm, eta_ref, sems, 8), fetch(curve_hbm, curve_ref, sems, 9)]
     pairs = [by_share(got_ref[2 * j], got_ref[2 * j + 1]) for j in range(4)]
     coefs = jnp.concatenate(
@@ -259,19 +262,24 @@
     wait_all(copies)
 
 
-def fifth_kernel(
-    ids_ref, got_ref, x_ref, own_hbm, first_hbm, second_hbm, out_hbm,
-    own_ref, out_ref, first_ref, second_ref, sems,
+def own_fields(own_ref, fields):
+    fh, fl = split(fields)
+    oh, ol = own_ref[:, :NX], own_ref[:, NX:]
+    return dot(oh, fh, NT) + dot(oh, fl, NT) + dot(ol, fh, NT)
+
+
+def early_kernel(
+    ids_ref, own_hbm, first_hbm, second_hbm, token_ref, out_hbm,
+    own_ref, first_ref, second_ref, out_ref, sems,
 ):
     start = pl.multiple_of(32 * ids_ref[0], 32)
     copies = [
         fetch(first_hbm, first_ref, sems, 1),
         fetch(second_hbm, second_ref, sems, 2),
-        fetch(own_hbm.at[pl.ds(start, 80), :], own_ref, sems, 0),
+        fetch(own_hbm.at[pl.ds(start, TALL), :], own_ref, sems, 0),
     ]
     kx, ky, squares = wave_squares(ids_ref)
     size = jnp.sqrt(squares)
-    third = folded_waves(got_ref, x_ref)
     wait_all(copies)
     first = first_ref[...]
     both = first + second_ref[...]
@@ -283,13 +291,33 @@
     slope_x = jnp.concatenate(blocks, 1)
     speed = ky[:32]
     slope_y = jnp.concatenate([speed * first[32:], -speed * first[:32]], 0)
-    fields = jnp.concatenate(
-        [size * (both + third), squares * both, size * squares * first, slope_x, slope_y], 0
-    )
-    fh, fl = split(fields)
-    oh, ol = own_ref[:, :NX], own_ref[:, NX:]
-    rows = dot(oh, fh, NT) + dot(oh, fl, NT) + dot(ol, fh, NT)
-    out_ref[...] = rows[:ROWS]
+    rows = own_fields(
+        own_ref,
+        jnp.concatenate([squares * both, size * squares * first, slope_x, slope_y], 0),
+    )
+    out_ref[:ROWS] = rows[:ROWS, :128]
+    out_ref[ROWS:] = rows[:ROWS, 128:]
+    fetch(out_ref, out_hbm, sems, 3).wait()
+
+
+def fifth_kernel(
+    ids_ref, got_ref, x_ref, own_hbm, first_hbm, second_hbm, early_hbm, out_hbm,
+    own_ref, out_ref, first_ref, second_ref, sems,
+):
+    start = pl.multiple_of(32 * ids_ref[0], 32)
+    copies = [
+        fetch(first_hbm, first_ref, sems, 1),
+        fetch(second_hbm, second_ref, sems, 2),
+        fetch(own_hbm.at[pl.ds(start, TALL), :], own_ref, sems, 0),
+        fetch(early_hbm, out_ref.at[:EARLY], sems, 4),
+    ]
+    kx, ky, squares = wave_squares(ids_ref)
+    size = jnp.sqrt(squares)
+    third = folded_waves(got_ref, x_ref)
+    wait_all(copies[:3])
+    rows = own_fields(own_ref, size * (first_ref[...] + second_ref[...] + third))
+    out_ref[EARLY:] = jnp.concatenate([rows[: TALL // 2], rows[TALL // 2 :]], 1)
+    wait_all(copies[3:])
     fetch(out_ref, out_hbm, sems, 3).wait()
 
 
@@ -543,30 +571,26 @@
     for step in range(4):
         share = (layer // 2 + 4 - step) % 4
         lanes = pl.ds(pl.multiple_of(128 * share, 128), 128)
-        mine, theirs = blocks[step], blocks[4 + step]
-        for f in range(0, 4, 2):
-            here = mine[:, 64 * f : 64 * f + 128]
-            there = theirs[:, 64 * f : 64 * f + 128]
+        mine, theirs = blocks.at[step], blocks.at[4 + step]
+        for at, size in ((0, ROWS), (ROWS, ROWS), (EARLY, TALL // 2)):
+            here = mine[at : at + size, :]
+            there = theirs[at : at + size, :]
             first = jnp.where(layer % 2 == 0, here, there)
             second = jnp.where(layer % 2 == 0, there, here)
             first, second = by_share(first, second)
-            coef_ref[ROWS * f : ROWS * f + ROWS, lanes] = first
-            coef_ref[ROWS * f + ROWS : ROWS * f + 2 * ROWS, lanes] = second
-        here, there = mine[:, 256:320], theirs[:, 256:320]
-        first = jnp.where(layer % 2 == 0, here, there)
-        second = jnp.where(layer % 2 == 0, there, here)
-        coef_ref[4 * ROWS :, lanes] = jnp.concatenate([first, second], 1)
+            coef_ref[2 * at : 2 * at + size, lanes] = first
+            coef_ref[2 * at + size : 2 * at + 2 * size, lanes] = second
     fields = data_by_table(coef_ref[...], y_ref[0], y_ref[1], NN)
     wait_all(copies[:2])
     parts = [cells_ref[64 * i : 64 * i + 64] for i in range(8)]
     eta = eta_ref[...]
     vertical = (
-        fields[:ROWS]
-        + eta * fields[ROWS : 2 * ROWS]
-        + 0.5 * eta * eta * fields[2 * ROWS : 3 * ROWS]
+        fields[4 * ROWS : 5 * ROWS]
+        + eta * fields[:ROWS]
+        + 0.5 * eta * eta * fields[ROWS : 2 * ROWS]
     )
     surface_ref[...] = vertical[16:48]
-    sampled = (fields[3 * ROWS : 4 * ROWS], fields[4 * ROWS :], vertical)
+    sampled = (fields[2 * ROWS : 3 * ROWS], fields[3 * ROWS : 4 * ROWS], vertical)
     for f in range(3):
         field_ref[2 * f] = sampled[f]
         field_ref[2 * f + 1] = pltpu.roll(sampled[f], NY - 1, 1) - sampled[f]
@@ -609,8 +633,6 @@
         speed_ref[i] = speed + close * (target_ref[i] * depth - speed)
     spread_own([speed_ref[i] for i in range(3)], own_ref)
     wait_all(copies[2:])
-    lax.fori_loop(0, groups, wait_group, 0)
-    lax.fori_loop(0, rest_groups, wait_rest, 0)
 
     def add_pair(t, carry):
         o = pairs_ref[0, t]
@@ -627,7 +649,19 @@
             sum_ref[o, span, :] += reach_ref[t, span, :] * approach
         return carry
 
-    lax.fori_loop(0, count_ref[0], add_pair, 0)
+    def add_group(g, carry):
+        wait_group(g, 0)
+        stop = jnp.minimum(GROUP * g + GROUP, count_ref[0])
+        return lax.fori_loop(GROUP * g, stop, add_pair, carry)
+
+    def add_rest(g, carry):
+        wait_rest(g, 0)
+        start = PART + GROUP * g
+        stop = jnp.minimum(start + GROUP, count_ref[0])
+        return lax.fori_loop(start, stop, add_pair, carry)
+
+    lax.fori_loop(0, groups, add_group, 0)
+    lax.fori_loop(0, rest_groups, add_rest, 0)
     ones = jnp.ones((8, 384), BF16)
     rates = []
     for o in range(16):
@@ -796,29 +830,38 @@
             dma_sems(PART // GROUP),
         ],
     )
-    (block,) = call(
+    block, token = call(
         fourth_kernel,
         (got, eta_part, curve, y, token),
         "VHHVV",
-        [((8, 64, 128), "H")],
+        [((8, 64, 128), "H"), ((8, 128), "V")],
         "fourth",
         8,
         [(8, 64, 128), (128, NY), (128, NY), dma_sems(10)],
     )
     got = swap(block, "gz")
+    (early,) = call(
+        early_kernel,
+        (ids, own, first, second, token),
+        "SHHHV",
+        [((EARLY, 128), "H")],
+        "early",
+        8,
+        [pltpu.VMEM((TALL, 2 * NX), BF16), (64, NX), (64, NX), (EARLY, 128), dma_sems(4)],
+    )
     (block,) = call(
         fifth_kernel,
-        (ids, got, x, own, first, second),
-        "SVVHHH",
-        [((ROWS, 320), "H")],
+        (ids, got, x, own, first, second, early),
+        "SVVHHHH",
+        [((EARLY + TALL // 2, 128), "H")],
         "fifth",
         8,
         [
-            pltpu.VMEM((80, 2 * NX), BF16),
-            (ROWS, 320),
+            pltpu.VMEM((TALL, 2 * NX), BF16),
+            (EARLY + TALL // 2, 128),
             (64, NX),
             (64, NX),
-            dma_sems(4),
+            dma_sems(5),
         ],
     )
     along = [block] + [
@@ -844,13 +887,13 @@
         "last",
         24,
         [
-            (8, ROWS, 320),
+            (8, EARLY + TALL // 2, 128),
             (ROWS, NY),
             (512, 128),
             (96, 128, 128),
             (16, 3, 128, 128),
             (16, 128, 128),
-            (5 * ROWS, NY),
+            (2 * EARLY + TALL, NY),
             (6, ROWS, NY),
             (3, 64, 128),
             (3, 64, 128),

time: 124 us -> 123 us (level)
  blocking collectives: 10.7 us -> 0 us
  starting transfers between devices: 44.2 us -> 48.8 us
  waiting for transfers between devices: 18.3 us -> 21.7 us
  Pallas kernels: 46.2 us -> 48 us
    all_to_all x1 -> x0, blocking collectives: 10.7 us -> none  [swap(): return lax.all_to_all(block, axis, split_axis=0, concat_axis=0, tiled=True)]
    all_to_all x4 -> x5, starting transfers between devices: 27.5 us -> 32.5 us  [swap(): return lax.all_to_all(block, axis, split_axis=0, concat_axis=0, tiled=True)]
    all_to_all x4 -> x5, waiting for transfers between devices: 0.38 us -> 3.93 us  [swap(): return lax.all_to_all(block, axis, split_axis=0, concat_axis=0, tiled=True)]
    pallas_call x11 -> x12, Pallas kernels: 46.2 us -> 48 us  [call(): pl.pallas_call(kernel, out_shape=[pltpu.HBM(s, F32) if k == 'H' else jax....]
  transfers between devices with their start and end apart: 15 -> 16, of which waited for: 6 -> 6; matrix products, arithmetic and copies ran while one was open for 1% -> 1% of each run, Pallas kernels for 15% -> 17%
where the time goes in v4:
time: 123 us
  starting transfers between devices  48.8 us (40%)
  Pallas kernels  48 us (39%)
  waiting for transfers between devices  21.7 us (18%)
  local copies, waits for them, and re-layouts  2.31 us (2%)
  between operations  1.69 us (1%)
    pallas_call x12, Pallas kernels, call(): pl.pallas_call(kernel, out_shape=[pltpu.HBM(s, F32) if k == 'H' else jax....  48 us
    all_to_all x5, starting transfers between devices, swap(): return lax.all_to_all(block, axis, split_axis=0, concat_axis=0, tiled=True)  32.5 us
    ppermute x4, waiting for transfers between devices, passed(): lax.ppermute(values, axis, [(i, (i + by) % size) for i in range(size)])  16.8 us
    ppermute x4, starting transfers between devices, per_device(): lax.ppermute(b, 'gz', [(i, i ^ 1) for i in range(2 * half_layers)])  7.83 us
    ppermute x4, starting transfers between devices, passed(): lax.ppermute(values, axis, [(i, (i + by) % size) for i in range(size)])  6.28 us
    all_to_all x5, waiting for transfers between devices, swap(): return lax.all_to_all(block, axis, split_axis=0, concat_axis=0, tiled=True)  3.93 us
  transfers between devices with their start and end apart: 16, of which 6 were waited for; matrix products, arithmetic and copies ran while one was open for 1% of the time, Pallas kernels for 17%

profile of v4, /device:TPU:1, one launch (start us, length us, event | category | flops | bytes accessed | tf_op | source)
XLA Modules:
  0.0 122.6 jit_solution(3424936711695038014)
XLA Ops:
  0.6 0.0 copy-start
  0.6 0.1 pad_add_fusion.ids_ref
  0.7 3.1 %start.1 = f32[32,32,128]{2,1,0:T(8,128)} custom-call(s32[2]{0:T(128)S(1)} %pad_add_fusion.ids_ref, f32[32,512]{1,0:T(8,128)} %phis_hbm.1, f32[32,512]{1,0:T(8,128)} %eta_hbm.5, bf16[2,512,512]{2,1,0:T(8,128)(2,1)} %constant.15.clone.y_hbm.y_ref.refs_10_), custom_call_target="tpu_custom_call" | custom-call | tf_op jit(solution)/shard_map/start/pallas_call | solution.py:682
  3.9 12.0 %all-to-all-start = ((f32[32,32,128]{2,1,0:T(8,128)}), f32[32,32,128]{2,1,0:T(8,128)}, u32[]{:S(2)}, u32[]{:S(2)}) async-start(f32[32,32,128]{2,1,0:T(8,128)} %start.1), calls=%async_computation | async-start | bytes 1048576 | tf_op jit(solution)/shard_map/all_to_all | solution.py:705
  15.9 0.8 copy.11.count_ref
  16.7 2.2 %pack.1 = (f32[128,128]{1,0:T(8,128)}, f32[128,128]{1,0:T(8,128)}, f32[160,128]{1,0:T(8,128)}) custom-call(s32[2,4,2]{2,1,0:T(4,128)S(1)} %copy.11.count_ref, f32[8,2,4,2,128]{4,3,2,1,0:T(2,128)} %parts_hbm.1, f32[32,512]{1,0:T(8,128)} %eta_hbm.5), custom_call_target="tpu_custom_call" | custom-call | tf_op jit(solution)/shard_map/pack/pallas_call | solution.py:682
  18.9 4.6 %collective-permute-start.1 = (f32[160,128]{1,0:T(8,128)}, f32[160,128]{1,0:T(8,128)S(1)}, u32[]{:S(2)}, u32[]{:S(2)}) collective-permute-start(f32[160,128]{1,0:T(8,128)} %get-tuple-element.33), channel_id=1, source_target_pairs={{0,248},{8,0},{16,8},{24,16},{32,24},{40,32},{48,40},{56,48},{64,5... | collective-permute-start | bytes 245768 | tf_op jit(solution)/shard_map/ppermute | solution.py:701
  23.5 0.0 collective-permute-start
  23.5 9.2 %collective-permute-done.before_hbm = f32[128,128]{1,0:T(8,128)S(1)} collective-permute-done((f32[128,128]{1,0:T(8,128)}, f32[128,128]{1,0:T(8,128)S(1)}, u32[]{:S(2)}, u32[]{:S(2)}) %collective-permute-start) | collective-permute-done | bytes 65568 | tf_op jit(solution)/shard_map/ppermute | solution.py:701
  32.8 0.0 collective-permute-done.1.after_hbm
  32.8 0.6 copy-done.13
  33.4 0.0 copy-done.12
  33.4 1.8 %extend.1 = (f32[256,128]{1,0:T(8,128)}, f32[128,128]{1,0:T(8,128)}, f32[128,128]{1,0:T(8,128)}, f32[72,512]{1,0:T(8,128)}) custom-call(f32[128,128]{1,0:T(8,128)} %copy-done.13, f32[128,128]{1,0:T(8,128)} %get-tuple-element.32.own_hbm, f32[160,128]{1,0:T(8,128)} %copy-done.12, f32[32,512]{1,0:T(8,128)} %eta_hbm.5), custom_call_target="tpu_custom_call" | custom-call | tf_op jit(solution)/shard_map/extend/pallas_call | solution.py:682
  35.3 0.0 all-to-all-done
  35.3 0.0 copy-start.2
  35.3 3.1 %first.1 = (f32[8,128,128]{2,1,0:T(8,128)}, f32[64,1024]{1,0:T(8,128)}) custom-call(s32[2]{0:T(128)S(1)} %pad_add_fusion.ids_ref, f32[1024,128]{1,0:T(8,128)} %bitcast.4.got_ref.gathered_ref, bf16[4,512,512]{2,1,0:T(8,128)(2,1)S(1)} %copy-done, f32[256,128]{1,0:T(8,128)} %get-tuple-element.34.wide_hbm), custom_call_target="tpu_custom_call" | custom-call | tf_op jit(solution)/shard_map/first/pallas_call | solution.py:682
  38.4 6.0 %all-to-all-start.1 = ((f32[8,128,128]{2,1,0:T(8,128)}), f32[8,128,128]{2,1,0:T(8,128)}, u32[]{:S(2)}, u32[]{:S(2)}) async-start(f32[8,128,128]{2,1,0:T(8,128)} %get-tuple-element.35), calls=%async_computation.1 | async-start | bytes 1048576 | tf_op jit(solution)/shard_map/all_to_all | solution.py:705
  44.3 1.6 %collective-permute-start.2 = (f32[128,128]{1,0:T(8,128)S(1)}, f32[128,128]{1,0:T(8,128)S(1)}, u32[]{:S(2)}, u32[]{:S(2)}) collective-permute-start(f32[128,128]{1,0:T(8,128)S(1)} %copy-done.15), channel_id=1, source_target_pairs={{0,1},{1,2},{2,3},{3,4},{4,5},{5,6},{6,7},{7,0},{8,9},{9,10},{10,1... | collective-permute-start | bytes 196616 | tf_op jit(solution)/shard_map/ppermute | solution.py:701
  46.0 0.0 collective-permute-start.3
  46.0 5.4 %collective-permute-done.2.below_hbm = f32[128,128]{1,0:T(8,128)S(1)} collective-permute-done((f32[128,128]{1,0:T(8,128)S(1)}, f32[128,128]{1,0:T(8,128)S(1)}, u32[]{:S(2)}, u32[]{:S(2)}) %collective-permute-start.2) | collective-permute-done | bytes 65568 | tf_op jit(solution)/shard_map/ppermute | solution.py:701
  51.4 2.2 %collective-permute-done.3.above_hbm = f32[128,128]{1,0:T(8,128)S(1)} collective-permute-done((f32[128,128]{1,0:T(8,128)S(1)}, f32[128,128]{1,0:T(8,128)S(1)}, u32[]{:S(2)}, u32[]{:S(2)}) %collective-permute-start.3) | collective-permute-done | bytes 65568 | tf_op jit(solution)/shard_map/ppermute | solution.py:701
  53.6 0.4 all-to-all-done.1.got_ref
  54.0 0.2 copy-done.4
  54.2 3.0 %second.1 = (f32[8,64,128]{2,1,0:T(8,128)}, f32[128,512]{1,0:T(8,128)}, f32[128,512]{1,0:T(8,128)}, f32[8,128]{1,0:T(8,128)S(1)}) custom-call(f32[8,128,128]{2,1,0:T(8,128)} %all-to-all-done.1.got_ref, f32[1024,128]{1,0:T(8,128)} %bitcast.4.got_ref.gathered_ref, bf16[2,512,512]{2,1,0:T(8,128)(2,1)S(1)} %copy-done.1, f32[128,128]{1,0:T(8,128)} %copy-done.3, ...), custom_call_target="tpu_custom_call" | custom-call | tf_op jit(solution)/shard_map/second/pallas_call | solution.py:682
  57.2 4.7 %all-to-all-start.2 = ((f32[8,64,128]{2,1,0:T(8,128)}), f32[8,64,128]{2,1,0:T(8,128)S(1)}, u32[]{:S(2)}, u32[]{:S(2)}) async-start(f32[8,64,128]{2,1,0:T(8,128)} %get-tuple-element.38), calls=%async_computation.2 | async-start | bytes 524288 | tf_op jit(solution)/shard_map/all_to_all | solution.py:705
  62.6 6.9 %reach.1 = (f32[48,128,128]{2,1,0:T(8,128)}, f32[16,3,128,128]{3,2,1,0:T(8,128)}, f32[16,1,128,128]{3,2,1,0:T(8,128)}, f32[16,128,128]{2,1,0:T(8,128)}, f32[512,128]{1,0:T(8,128)}, /*index=5*/f32[8,128]{1,0:T(8,128)S(1)}) custom-call(s32[2]{0:T(128)S(1)} %pad_add_fusion.ids_ref, s32[2,96]{1,0:T(2,128)S(1)} %bitcast.9, s32[1]{0:T(128)} %bitcast.6.count_ref, ...), custom_call_target="tpu_custom_call" | custom-call | tf_op jit(solution)/shard_map/reach/pallas_call | solution.py:682
  69.6 2.5 %third.1 = (f32[8,64,128]{2,1,0:T(8,128)}, f32[64,1024]{1,0:T(8,128)}, f32[8,128]{1,0:T(8,128)S(1)}) custom-call(s32[2]{0:T(128)S(1)} %pad_add_fusion.ids_ref, f32[8,64,128]{2,1,0:T(8,128)S(1)} %all-to-all-done.2.got_ref, bf16[4,512,512]{2,1,0:T(8,128)(2,1)S(1)} %copy-done, f32[8,128]{1,0:T(8,128)S(1)} %get-tuple-element.40.token_ref), custom_call_target="tpu_custom_call" | custom-call | tf_op jit(solution)/shard_map/third/pallas_call | solution.py:682
  72.1 4.8 %all-to-all-start.3 = ((f32[8,64,128]{2,1,0:T(8,128)}), f32[8,64,128]{2,1,0:T(8,128)S(1)}, u32[]{:S(2)}, u32[]{:S(2)}) async-start(f32[8,64,128]{2,1,0:T(8,128)} %get-tuple-element.41), calls=%async_computation.3 | async-start | bytes 524288 | tf_op jit(solution)/shard_map/all_to_all | solution.py:705
  76.9 6.6 %rest.1 = (f32[48,128,128]{2,1,0:T(8,128)}, f32[16,128,128]{2,1,0:T(8,128)}, f32[8,128]{1,0:T(8,128)S(1)}) custom-call(s32[2]{0:T(128)S(1)} %pad_add_fusion.ids_ref, s32[2,96]{1,0:T(2,128)S(1)} %bitcast.10, s32[1]{0:T(128)} %bitcast.7.count_ref, f32[16,3,128,128]{3,2,1,0:T(8,128)} %get-tuple-element.44.place_hbm.refs_13_, ...), custom_call_target="tpu_custom_call" | custom-call | tf_op jit(solution)/shard_map/rest/pallas_call | solution.py:682
  83.5 2.2 %fourth.1 = (f32[8,64,128]{2,1,0:T(8,128)}, f32[8,128]{1,0:T(8,128)S(1)}) custom-call(f32[8,64,128]{2,1,0:T(8,128)S(1)} %all-to-all-done.3.got_ref, f32[128,512]{1,0:T(8,128)} %get-tuple-element.42.eta_hbm, f32[128,512]{1,0:T(8,128)} %get-tuple-element.43.curve_hbm, bf16[2,512,512]{2,1,0:T(8,128)(2,1)S(1)} %copy-done.1, f32[8,128]{1,0:T(8,128)S(1)} %get-tuple-element.49.token_ref), custom_call_target="tpu_custom_call" | custom-call | tf_op jit(solution)/shard_map/fourth/pallas_call | solution.py:682
  85.7 5.0 %all-to-all-start.4 = ((f32[8,64,128]{2,1,0:T(8,128)}), f32[8,64,128]{2,1,0:T(8,128)S(1)}, u32[]{:S(2)}, u32[]{:S(2)}) async-start(f32[8,64,128]{2,1,0:T(8,128)} %get-tuple-element.50), calls=%async_computation.4 | async-start | bytes 524288 | tf_op jit(solution)/shard_map/all_to_all | solution.py:705
  90.7 2.9 %early.1.early_hbm = f32[144,128]{1,0:T(8,128)} custom-call(s32[2]{0:T(128)S(1)} %pad_add_fusion.ids_ref, bf16[1096,2048]{1,0:T(8,128)(2,1)} %constant.17.clone.own_hbm, f32[64,1024]{1,0:T(8,128)} %get-tuple-element.51.first_hbm, f32[64,1024]{1,0:T(8,128)} %get-tuple-element.52.second_hbm, f32[8,128]{1,0:T(8,128)S(1)} %get-tuple-element.53.token_ref), custom_call_target="tpu_custom_call" | custom-call | tf_op jit(solution)/shard_map/early/pallas_call | solution.py:682
  93.7 3.6 %all-to-all-done.4.got_ref = f32[8,64,128]{2,1,0:T(8,128)S(1)} async-done(((f32[8,64,128]{2,1,0:T(8,128)}), f32[8,64,128]{2,1,0:T(8,128)S(1)}, u32[]{:S(2)}, u32[]{:S(2)}) %all-to-all-start.4) | async-done | bytes 262176 | tf_op jit(solution)/shard_map/all_to_all | solution.py:705
  97.2 2.8 %fifth.1.refs_0_ = f32[184,128]{1,0:T(8,128)} custom-call(s32[2]{0:T(128)S(1)} %pad_add_fusion.ids_ref, f32[8,64,128]{2,1,0:T(8,128)S(1)} %all-to-all-done.4.got_ref, bf16[4,512,512]{2,1,0:T(8,128)(2,1)S(1)} %copy-done, bf16[1096,2048]{1,0:T(8,128)(2,1)} %constant.17.clone.own_hbm, f32[64,1024]{1,0:T(8,128)} %get-tuple-element.51.first_hbm, ...), custom_call_target="tpu_custom_call" | custom-call | tf_op jit(solution)/shard_map/fifth/pallas_call | solution.py:682
  100.0 1.0 collective-permute-start.6
  101.0 1.2 collective-permute-start.5
  102.2 0.0 collective-permute-start.4
  102.2 1.6 %collective-permute-start.7 = (f32[184,128]{1,0:T(8,128)}, f32[184,128]{1,0:T(8,128)S(1)}, u32[]{:S(2)}, u32[]{:S(2)}) collective-permute-start(f32[184,128]{1,0:T(8,128)} %fifth.1.refs_0_), channel_id=1, source_target_pairs={{0,1},{1,0},{2,3},{3,2},{4,5},{5,4},{6,7},{7,6},{8,9},{9,8},{10,11... | collective-permute-start | bytes 282632 | tf_op jit(solution)/shard_map/ppermute | solution.py:880
  103.8 0.0 collective-permute-done.6.refs_3_
  103.8 2.7 %collective-permute-start.10 = (f32[184,128]{1,0:T(8,128)S(1)}, f32[184,128]{1,0:T(8,128)S(1)}, u32[]{:S(2)}, u32[]{:S(2)}) collective-permute-start(f32[184,128]{1,0:T(8,128)S(1)} %collective-permute-done.6.refs_3_), channel_id=1, source_target_pairs={{0,1},{1,0},{2,3},{3,2},{4,5},{5,4},{6,7},{7,6},{8,9},{9,8},{10,11... | collective-permute-start | bytes 282632 | tf_op jit(solution)/shard_map/ppermute | solution.py:880
  106.4 0.0 collective-permute-done.5.refs_2_
  106.4 2.6 %collective-permute-start.9 = (f32[184,128]{1,0:T(8,128)S(1)}, f32[184,128]{1,0:T(8,128)S(1)}, u32[]{:S(2)}, u32[]{:S(2)}) collective-permute-start(f32[184,128]{1,0:T(8,128)S(1)} %collective-permute-done.5.refs_2_), channel_id=1, source_target_pairs={{0,1},{1,0},{2,3},{3,2},{4,5},{5,4},{6,7},{7,6},{8,9},{9,8},{10,11... | collective-permute-start | bytes 282632 | tf_op jit(solution)/shard_map/ppermute | solution.py:880
  109.0 1.0 collective-permute-start.8
  110.0 0.0 collective-permute-done.7.refs_4_
  110.0 0.0 collective-permute-done.10.refs_7_
  110.0 0.9 collective-permute-done.8.refs_5_
  111.0 0.6 copy-done.11
  111.6 10.8 %last.1 = (f32[32,512]{1,0:T(8,128)}, f32[16,128]{1,0:T(8,128)}) custom-call(s32[2]{0:T(128)S(1)} %pad_add_fusion.ids_ref, s32[2,96]{1,0:T(2,128)S(1)} %bitcast.11, s32[1]{0:T(128)} %bitcast.8.count_ref, f32[184,128]{1,0:T(8,128)} %fifth.1.refs_0_, f32[184,128]{1,0:T(8,128)} %copy-done.7, f32[184,128]{1,0:T(8,128)} %copy-done.6, f32[184,128]{1,0:T(8,128)} %copy-done.5, ...), custom_call_target="tpu_custom_call" | custom-call | tf_op jit(solution)/shard_map/last/pallas_call | solution.py:682
  (30 shorter events, 0.1 us)
Async XLA Ops:
  0.6 34.6 %copy-start = (bf16[4,512,512]{2,1,0:T(8,128)(2,1)S(1)}, bf16[4,512,512]{2,1,0:T(8,128)(2,1)}, u32[]{:S(2)}) copy-start(bf16[4,512,512]{2,1,0:T(8,128)(2,1)} %constant.16.clone.x_ref) | copy-start | bytes 6291460
  0.7 53.5 %copy-start.1 = (bf16[2,512,512]{2,1,0:T(8,128)(2,1)S(1)}, bf16[2,512,512]{2,1,0:T(8,128)(2,1)}, u32[]{:S(2)}) copy-start(bf16[2,512,512]{2,1,0:T(8,128)(2,1)} %constant.15.clone.y_hbm.y_ref.refs_10_) | copy-start | bytes 3145732
  3.9 31.4 %all-to-all-start = ((f32[32,32,128]{2,1,0:T(8,128)}), f32[32,32,128]{2,1,0:T(8,128)}, u32[]{:S(2)}, u32[]{:S(2)}) async-start(f32[32,32,128]{2,1,0:T(8,128)} %start.1), calls=%async_computation | async-start | bytes 1048576 | tf_op jit(solution)/shard_map/all_to_all | solution.py:705
  18.9 13.9 %collective-permute-start.1 = (f32[160,128]{1,0:T(8,128)}, f32[160,128]{1,0:T(8,128)S(1)}, u32[]{:S(2)}, u32[]{:S(2)}) collective-permute-start(f32[160,128]{1,0:T(8,128)} %get-tuple-element.33), channel_id=1, source_target_pairs={{0,248},{8,0},{16,8},{24,16},{32,24},{40,32},{48,40},{56,48},{64,5... | collective-permute-start | bytes 245768 | tf_op jit(solution)/shard_map/ppermute | solution.py:701
  23.5 9.2 %collective-permute-start = (f32[128,128]{1,0:T(8,128)}, f32[128,128]{1,0:T(8,128)S(1)}, u32[]{:S(2)}, u32[]{:S(2)}) collective-permute-start(f32[128,128]{1,0:T(8,128)} %get-tuple-element.31), channel_id=1, source_target_pairs={{0,8},{8,16},{16,24},{24,32},{32,40},{40,48},{48,56},{56,64},{64,7... | collective-permute-start | bytes 196616 | tf_op jit(solution)/shard_map/ppermute | solution.py:701
  32.8 0.6 copy-start.13
  32.8 0.7 copy-start.12
  35.2 9.1 %copy-start.15 = (f32[128,128]{1,0:T(8,128)S(1)}, f32[128,128]{1,0:T(8,128)}, u32[]{:S(2)}) copy-start(f32[128,128]{1,0:T(8,128)} %get-tuple-element.36) | copy-start | bytes 196612
  35.3 10.7 %copy-start.14 = (f32[128,128]{1,0:T(8,128)S(1)}, f32[128,128]{1,0:T(8,128)}, u32[]{:S(2)}) copy-start(f32[128,128]{1,0:T(8,128)} %get-tuple-element.37) | copy-start | bytes 196612
  35.3 27.3 %copy-start.2 = (s32[1,1,2,96]{3,2,1,0:T(2,128)S(1)}, s32[1,1,2,96]{3,2,1,0:T(2,128)}, u32[]{:S(2)}) copy-start(s32[1,1,2,96]{3,2,1,0:T(2,128)} %param.13) | copy-start | bytes 2308
  38.4 15.6 %all-to-all-start.1 = ((f32[8,128,128]{2,1,0:T(8,128)}), f32[8,128,128]{2,1,0:T(8,128)}, u32[]{:S(2)}, u32[]{:S(2)}) async-start(f32[8,128,128]{2,1,0:T(8,128)} %get-tuple-element.35), calls=%async_computation.1 | async-start | bytes 1048576 | tf_op jit(solution)/shard_map/all_to_all | solution.py:705
  44.3 7.1 %collective-permute-start.2 = (f32[128,128]{1,0:T(8,128)S(1)}, f32[128,128]{1,0:T(8,128)S(1)}, u32[]{:S(2)}, u32[]{:S(2)}) collective-permute-start(f32[128,128]{1,0:T(8,128)S(1)} %copy-done.15), channel_id=1, source_target_pairs={{0,1},{1,2},{2,3},{3,4},{4,5},{5,6},{6,7},{7,0},{8,9},{9,10},{10,1... | collective-permute-start | bytes 196616 | tf_op jit(solution)/shard_map/ppermute | solution.py:701
  46.0 7.6 %collective-permute-start.3 = (f32[128,128]{1,0:T(8,128)S(1)}, f32[128,128]{1,0:T(8,128)S(1)}, u32[]{:S(2)}, u32[]{:S(2)}) collective-permute-start(f32[128,128]{1,0:T(8,128)S(1)} %copy-done.14), channel_id=1, source_target_pairs={{0,7},{1,0},{2,1},{3,2},{4,3},{5,4},{6,5},{7,6},{8,15},{9,8},{10,9... | collective-permute-start | bytes 196616 | tf_op jit(solution)/shard_map/ppermute | solution.py:701
  51.4 2.6 %copy-start.3 = (f32[128,128]{1,0:T(8,128)}, f32[128,128]{1,0:T(8,128)S(1)}, u32[]{:S(2)}) copy-start(f32[128,128]{1,0:T(8,128)S(1)} %collective-permute-done.2.below_hbm) | copy-start | bytes 196612
  53.6 0.6 copy-start.4
  57.2 12.4 %all-to-all-start.2 = ((f32[8,64,128]{2,1,0:T(8,128)}), f32[8,64,128]{2,1,0:T(8,128)S(1)}, u32[]{:S(2)}, u32[]{:S(2)}) async-start(f32[8,64,128]{2,1,0:T(8,128)} %get-tuple-element.38), calls=%async_computation.2 | async-start | bytes 524288 | tf_op jit(solution)/shard_map/all_to_all | solution.py:705
  72.1 11.4 %all-to-all-start.3 = ((f32[8,64,128]{2,1,0:T(8,128)}), f32[8,64,128]{2,1,0:T(8,128)S(1)}, u32[]{:S(2)}, u32[]{:S(2)}) async-start(f32[8,64,128]{2,1,0:T(8,128)} %get-tuple-element.41), calls=%async_computation.3 | async-start | bytes 524288 | tf_op jit(solution)/shard_map/all_to_all | solution.py:705
  85.7 11.5 %all-to-all-start.4 = ((f32[8,64,128]{2,1,0:T(8,128)}), f32[8,64,128]{2,1,0:T(8,128)S(1)}, u32[]{:S(2)}, u32[]{:S(2)}) async-start(f32[8,64,128]{2,1,0:T(8,128)} %get-tuple-element.50), calls=%async_computation.4 | async-start | bytes 524288 | tf_op jit(solution)/shard_map/all_to_all | solution.py:705
  100.0 3.8 %collective-permute-start.6 = (f32[184,128]{1,0:T(8,128)}, f32[184,128]{1,0:T(8,128)S(1)}, u32[]{:S(2)}, u32[]{:S(2)}) collective-permute-start(f32[184,128]{1,0:T(8,128)} %fifth.1.refs_0_), channel_id=1, source_target_pairs={{0,6},{1,7},{2,0},{3,1},{4,2},{5,3},{6,4},{7,5},{8,14},{9,15},{10,... | collective-permute-start | bytes 282632 | tf_op jit(solution)/shard_map/ppermute | solution.py:868
  101.0 5.5 %collective-permute-start.5 = (f32[184,128]{1,0:T(8,128)}, f32[184,128]{1,0:T(8,128)S(1)}, u32[]{:S(2)}, u32[]{:S(2)}) collective-permute-start(f32[184,128]{1,0:T(8,128)} %fifth.1.refs_0_), channel_id=1, source_target_pairs={{0,4},{1,5},{2,6},{3,7},{4,0},{5,1},{6,2},{7,3},{8,12},{9,13},{10,... | collective-permute-start | bytes 282632 | tf_op jit(solution)/shard_map/ppermute | solution.py:868
  102.2 6.9 %collective-permute-start.4 = (f32[184,128]{1,0:T(8,128)}, f32[184,128]{1,0:T(8,128)S(1)}, u32[]{:S(2)}, u32[]{:S(2)}) collective-permute-start(f32[184,128]{1,0:T(8,128)} %fifth.1.refs_0_), channel_id=1, source_target_pairs={{0,2},{1,3},{2,4},{3,5},{4,6},{5,7},{6,0},{7,1},{8,10},{9,11},{10,... | collective-permute-start | bytes 282632 | tf_op jit(solution)/shard_map/ppermute | solution.py:868
  102.2 7.8 %collective-permute-start.7 = (f32[184,128]{1,0:T(8,128)}, f32[184,128]{1,0:T(8,128)S(1)}, u32[]{:S(2)}, u32[]{:S(2)}) collective-permute-start(f32[184,128]{1,0:T(8,128)} %fifth.1.refs_0_), channel_id=1, source_target_pairs={{0,1},{1,0},{2,3},{3,2},{4,5},{5,4},{6,7},{7,6},{8,9},{9,8},{10,11... | collective-permute-start | bytes 282632 | tf_op jit(solution)/shard_map/ppermute | solution.py:880
  103.8 7.2 %copy-start.5 = (f32[184,128]{1,0:T(8,128)}, f32[184,128]{1,0:T(8,128)S(1)}, u32[]{:S(2)}) copy-start(f32[184,128]{1,0:T(8,128)S(1)} %collective-permute-done.6.refs_3_) | copy-start | bytes 282628
  103.8 6.2 %collective-permute-start.10 = (f32[184,128]{1,0:T(8,128)S(1)}, f32[184,128]{1,0:T(8,128)S(1)}, u32[]{:S(2)}, u32[]{:S(2)}) collective-permute-start(f32[184,128]{1,0:T(8,128)S(1)} %collective-permute-done.6.refs_3_), channel_id=1, source_target_pairs={{0,1},{1,0},{2,3},{3,2},{4,5},{5,4},{6,7},{7,6},{8,9},{9,8},{10,11... | collective-permute-start | bytes 282632 | tf_op jit(solution)/shard_map/ppermute | solution.py:880
  106.4 4.5 %copy-start.6 = (f32[184,128]{1,0:T(8,128)}, f32[184,128]{1,0:T(8,128)S(1)}, u32[]{:S(2)}) copy-start(f32[184,128]{1,0:T(8,128)S(1)} %collective-permute-done.5.refs_2_) | copy-start | bytes 282628
  106.4 3.6 %collective-permute-start.9 = (f32[184,128]{1,0:T(8,128)S(1)}, f32[184,128]{1,0:T(8,128)S(1)}, u32[]{:S(2)}, u32[]{:S(2)}) collective-permute-start(f32[184,128]{1,0:T(8,128)S(1)} %collective-permute-done.5.refs_2_), channel_id=1, source_target_pairs={{0,1},{1,0},{2,3},{3,2},{4,5},{5,4},{6,7},{7,6},{8,9},{9,8},{10,11... | collective-permute-start | bytes 282632 | tf_op jit(solution)/shard_map/ppermute | solution.py:880
  109.0 1.9 %copy-start.7 = (f32[184,128]{1,0:T(8,128)}, f32[184,128]{1,0:T(8,128)S(1)}, u32[]{:S(2)}) copy-start(f32[184,128]{1,0:T(8,128)S(1)} %collective-permute-done.4.refs_1_) | copy-start | bytes 282628
  109.0 1.9 %collective-permute-start.8 = (f32[184,128]{1,0:T(8,128)S(1)}, f32[184,128]{1,0:T(8,128)S(1)}, u32[]{:S(2)}, u32[]{:S(2)}) collective-permute-start(f32[184,128]{1,0:T(8,128)S(1)} %collective-permute-done.4.refs_1_), channel_id=1, source_target_pairs={{0,1},{1,0},{2,3},{3,2},{4,5},{5,4},{6,7},{7,6},{8,9},{9,8},{10,11... | collective-permute-start | bytes 282632 | tf_op jit(solution)/shard_map/ppermute | solution.py:880
  110.0 1.0 copy-start.8
  110.0 1.0 copy-start.9
  110.0 0.9 copy-start.10
  110.9 0.6 copy-start.11

commit v5 on v4

--- a/solution.py
+++ b/solution.py
@@ -339,10 +339,9 @@
 
 
 def pack_kernel(
-    count_ref, parts_hbm, eta_hbm, own_hbm, up_hbm, down_hbm,
-    parts_ref, eta_ref, own_ref, up_ref, down_ref, sems,
-):
-    wait_all([fetch(parts_hbm, parts_ref, sems, 3), fetch(eta_hbm, eta_ref, sems, 4)])
+    count_ref, parts_hbm, own_hbm, low_hbm, high_hbm, parts_ref, own_ref, low_ref, high_ref, sems
+):
+    fetch(parts_hbm, parts_ref, sems, 3).wait()
     lane = lax.broadcasted_iota(jnp.int32, (2, 128), 1)
     row = lax.broadcasted_iota(jnp.int32, (2, 128), 0)
     for i in range(8):
@@ -352,46 +351,42 @@
                 if i == 7:
                     live = jnp.where(row == 0, count_ref[cx, cy, 0], count_ref[cx, cy, 1])
                     value = jnp.where(lane < live, value, 0.0)
-                at = 16 * i + 8 * cx + 2 * cy
-                own_ref[at : at + 2] = value
-                at = 8 * i + 2 * cy
-                side_ref = up_ref if cx == 1 else down_ref
-                side_ref[at : at + 2] = value
+                at = 8 * i + 4 * cx + cy
+                own_ref[2 * at : 2 * at + 2] = value
+                low_ref[at : at + 1] = value[:1]
+                high_ref[at : at + 1] = value[1:]
+    wait_all([
+        fetch(low_ref, low_hbm, sems, 0),
+        fetch(high_ref, high_hbm, sems, 1),
+        fetch(own_ref, own_hbm, sems, 2),
+    ])
+
+
+def extend_kernel(
+    below_hbm, own_hbm, above_hbm, eta_hbm, wide_hbm, up_hbm, down_hbm,
+    below_ref, own_ref, above_ref, eta_ref, wide_ref, up_ref, down_ref, sems,
+):
+    wait_all([
+        fetch(below_hbm, below_ref, sems, 3),
+        fetch(own_hbm, own_ref, sems, 4),
+        fetch(above_hbm, above_ref, sems, 5),
+        fetch(eta_hbm, eta_ref, sems, 6),
+    ])
+    for i in range(8):
+        wide_ref[pl.ds(32 * i, 8, stride=4), :] = below_ref[8 * i : 8 * i + 8]
+        wide_ref[pl.ds(32 * i + 1, 8, stride=4), :] = own_ref[pl.ds(16 * i, 8, stride=2), :]
+        wide_ref[pl.ds(32 * i + 2, 8, stride=4), :] = own_ref[pl.ds(16 * i + 1, 8, stride=2), :]
+        wide_ref[pl.ds(32 * i + 3, 8, stride=4), :] = above_ref[8 * i : 8 * i + 8]
+    for i in range(8):
+        down_ref[16 * i : 16 * i + 16] = wide_ref[32 * i : 32 * i + 16]
+        up_ref[16 * i : 16 * i + 16] = wide_ref[32 * i + 16 : 32 * i + 32]
     for j in range(4):
-        up_ref[64 + 16 * j : 80 + 16 * j] = eta_ref[16:, 128 * j : 128 * j + 128]
-        down_ref[64 + 24 * j : 88 + 24 * j] = eta_ref[:24, 128 * j : 128 * j + 128]
+        up_ref[128 + 16 * j : 144 + 16 * j] = eta_ref[16:, 128 * j : 128 * j + 128]
+        down_ref[128 + 24 * j : 152 + 24 * j] = eta_ref[:24, 128 * j : 128 * j + 128]
     wait_all([
         fetch(up_ref, up_hbm, sems, 0),
         fetch(down_ref, down_hbm, sems, 1),
-        fetch(own_ref, own_hbm, sems, 2),
-    ])
-
-
-def extend_kernel(
-    before_hbm, own_hbm, after_hbm, eta_hbm, wide_hbm, low_hbm, high_hbm, rows_hbm,
-    before_ref, own_ref, after_ref, wide_ref, low_ref, high_ref, rows_ref, sems,
-):
-    wait_all([
-        fetch(before_hbm, before_ref, sems, 4),
-        fetch(own_hbm, own_ref, sems, 5),
-        fetch(after_hbm, after_ref, sems, 6),
-        fetch(eta_hbm, rows_ref.at[16:48], sems, 7),
-    ])
-    for i in range(8):
-        wide_ref[32 * i : 32 * i + 8] = before_ref[8 * i : 8 * i + 8]
-        wide_ref[32 * i + 8 : 32 * i + 24] = own_ref[16 * i : 16 * i + 16]
-        wide_ref[32 * i + 24 : 32 * i + 32] = after_ref[8 * i : 8 * i + 8]
-    for i in range(8):
-        low_ref[16 * i : 16 * i + 16] = wide_ref[pl.ds(32 * i, 16, stride=2), :]
-        high_ref[16 * i : 16 * i + 16] = wide_ref[pl.ds(32 * i + 1, 16, stride=2), :]
-    for j in range(4):
-        rows_ref[:16, 128 * j : 128 * j + 128] = before_ref[64 + 16 * j : 80 + 16 * j]
-        rows_ref[48:, 128 * j : 128 * j + 128] = after_ref[64 + 24 * j : 88 + 24 * j]
-    wait_all([
-        fetch(low_ref, low_hbm, sems, 0),
-        fetch(high_ref, high_hbm, sems, 1),
         fetch(wide_ref, wide_hbm, sems, 2),
-        fetch(rows_ref, rows_hbm, sems, 3),
     ])
 
 
@@ -470,26 +465,23 @@
 
 
 def reach_kernel(
-    ids_ref, pairs_ref, count_ref, wide_hbm, below_hbm, above_hbm, token_ref,
+    ids_ref, pairs_ref, count_ref, wide_hbm, before_hbm, after_hbm, token_ref,
     reach_hbm, place_hbm, density_hbm, sum_hbm, cells_hbm, done_ref,
-    wide_ref, below_ref, above_ref, reach_ref, place_ref, density_ref, sum_ref, cells_ref,
+    wide_ref, before_ref, after_ref, reach_ref, place_ref, density_ref, sum_ref, cells_ref,
     chan_ref, sems, reach_sems,
 ):
     copies = [
         fetch(wide_hbm, wide_ref, sems, 3),
-        fetch(below_hbm, below_ref, sems, 4),
-        fetch(above_hbm, above_ref, sems, 5),
+        fetch(before_hbm.at[pl.ds(0, 128), :], before_ref, sems, 4),
+        fetch(after_hbm.at[pl.ds(0, 128), :], after_ref, sems, 5),
     ]
     sum_ref[...] = jnp.zeros_like(sum_ref)
     done_ref[...] = token_ref[...]
     wait_all(copies)
     for i in range(8):
-        low = wide_ref[pl.ds(32 * i, 16, stride=2), :]
-        high = wide_ref[pl.ds(32 * i + 1, 16, stride=2), :]
-        cells_ref[pl.ds(64 * i, 16, stride=4), :] = below_ref[16 * i : 16 * i + 16]
-        cells_ref[pl.ds(64 * i + 1, 16, stride=4), :] = low
-        cells_ref[pl.ds(64 * i + 2, 16, stride=4), :] = high
-        cells_ref[pl.ds(64 * i + 3, 16, stride=4), :] = above_ref[16 * i : 16 * i + 16]
+        cells_ref[64 * i : 64 * i + 16] = before_ref[16 * i : 16 * i + 16]
+        cells_ref[64 * i + 16 : 64 * i + 48] = wide_ref[32 * i : 32 * i + 32]
+        cells_ref[64 * i + 48 : 64 * i + 64] = after_ref[16 * i : 16 * i + 16]
     copies = [fetch(cells_ref, cells_hbm, sems, 2)]
     reach_channels(ids_ref, cells_ref, chan_ref)
     spread_own([chan_ref[i] for i in range(3)], place_ref)
@@ -532,17 +524,24 @@
 def last_kernel(ids_ref, pairs_ref, count_ref, *refs):
     blocks_hbm, refs = refs[:8], refs[8:]
     (
-        eta_hbm, cells_hbm, y_ref, reach_hbm, rest_hbm, place_hbm, sum_hbm, surface_ref, rate_ref,
+        before_hbm, eta_hbm, after_hbm, cells_hbm, y_ref, reach_hbm, rest_hbm, place_hbm, sum_hbm, surface_ref, rate_ref,
         blocks, eta_ref, cells_ref, reach_ref, place_ref, sum_ref,
         coef_ref, field_ref, target_ref, speed_ref, half_ref, own_ref, sems, reach_sems,
     ) = refs
     block_copies = [fetch(blocks_hbm[i], blocks.at[i], sems, 4 + i) for i in range(8)]
     copies = [
-        fetch(eta_hbm, eta_ref, sems, 0),
+        fetch(eta_hbm, eta_ref.at[pl.ds(16, 32), :], sems, 0),
         fetch(cells_hbm, cells_ref, sems, 1),
         fetch(place_hbm, place_ref, sems, 2),
         fetch(sum_hbm, sum_ref, sems, 3),
     ]
+
+    for j in range(4):
+        lanes = pl.ds(128 * j, 128)
+        from_before = before_hbm.at[pl.ds(128 + 16 * j, 16), :]
+        from_after = after_hbm.at[pl.ds(128 + 24 * j, 24), :]
+        block_copies.append(fetch(from_before, eta_ref.at[pl.ds(0, 16), lanes], sems, 12 + j))
+        block_copies.append(fetch(from_after, eta_ref.at[pl.ds(48, 24), lanes], sems, 16 + j))
 
     def start_group(g, carry):
         reach_copy(span_of(reach_hbm, g), span_of(reach_ref, g), reach_sems, g).start()
@@ -716,29 +715,29 @@
 
     half_layers = lax.axis_size("gz") // 2
 
-    own_cells, up, down = call(
-        pack_kernel, (cell_count, particles, eta), "SHH",
-        [((128, 128), "H"), ((128, 128), "H"), ((160, 128), "H")], "pack", 4,
-        [(8, 2, 4, 2, 128), (32, NY), (128, 128), (128, 128), (160, 128), dma_sems(5)],
+    own_cells, low, high = call(
+        pack_kernel, (cell_count, particles), "SH",
+        [((128, 128), "H"), ((64, 128), "H"), ((64, 128), "H")], "pack", 4,
+        [(8, 2, 4, 2, 128), (128, 128), (64, 128), (64, 128), dma_sems(4)],
+    )
+    below = passed(high, "gz", 1)
+    above = passed(low, "gz", -1)
+    wide, up, down = call(
+        extend_kernel, (below, own_cells, above, eta), "HHHH",
+        [((256, 128), "H"), ((192, 128), "H"), ((224, 128), "H")], "extend", 4,
+        [
+            (64, 128),
+            (128, 128),
+            (64, 128),
+            (32, NY),
+            (256, 128),
+            (192, 128),
+            (224, 128),
+            dma_sems(7),
+        ],
     )
     cells_before = passed(up, "gx", 1)
     cells_after = passed(down, "gx", -1)
-    wide, low, high, eta_rows = call(
-        extend_kernel, (cells_before, own_cells, cells_after, eta), "HHHH",
-        [((256, 128), "H"), ((128, 128), "H"), ((128, 128), "H"), ((ROWS, NY), "H")], "extend", 4,
-        [
-            (128, 128),
-            (128, 128),
-            (160, 128),
-            (256, 128),
-            (128, 128),
-            (128, 128),
-            (ROWS, NY),
-            dma_sems(8),
-        ],
-    )
-    below = passed(high, "gz", 1)
-    above = passed(low, "gz", -1)
     pairs = pair_cells.reshape(2, 96)
     count = pair_count.reshape(1)
 
@@ -766,7 +765,7 @@
     got = swap(block, "gz")
     block, eta_part, curve, token = call(
         second_kernel,
-        (got, gathered, y, below, above),
+        (got, gathered, y, cells_before, cells_after),
         "VVVHH",
         [((8, 64, 128), "H"), ((128, NY), "H"), ((128, NY), "H"), ((8, 128), "V")],
         "second",
@@ -776,7 +775,7 @@
     got = swap(block, "gz")
     reach, place, density, before, cells, token = call(
         reach_kernel,
-        (ids, pairs, count, wide, below, above, token),
+        (ids, pairs, count, wide, cells_before, cells_after, token),
         "SSSHHHV",
         [
             ((PART, 128, 128), "H"),
@@ -881,8 +880,8 @@
     ]
     surface, rate = call(
         last_kernel,
-        (ids, pairs, count, *along, *across, eta_rows, cells, y, reach, rest, place, before),
-        "SSS" + "H" * 10 + "VHHHH",
+        (ids, pairs, count, *along, *across, cells_before, eta, cells_after, cells, y, reach, rest, place, before),
+        "SSS" + "H" * 12 + "VHHHH",
         [((32, NY), "V"), ((16, 128), "V")],
         "last",
         24,
@@ -899,7 +898,7 @@
             (3, 64, 128),
             (3, 64, 128),
             (16, 3, 128, 128),
-            dma_sems(12),
+            dma_sems(20),
             dma_sems(96 // GROUP),
         ],
     )

time: 123 us -> 121 us (0.984)
  starting transfers between devices: 48.8 us -> 46.7 us
    all_to_all x5, waiting for transfers between devices: 3.93 us -> 10.7 us  [swap(): return lax.all_to_all(block, axis, split_axis=0, concat_axis=0, tiled=True)]
    ppermute x4, waiting for transfers between devices: 16.8 us -> 10.7 us  [passed(): lax.ppermute(values, axis, [(i, (i + by) % size) for i in range(size)])]
    ppermute x4, starting transfers between devices: 6.28 us -> 3.63 us  [passed(): lax.ppermute(values, axis, [(i, (i + by) % size) for i in range(size)])]
  transfers between devices with their start and end apart: 16 -> 16, of which waited for: 6 -> 8; matrix products, arithmetic and copies ran while one was open for 1% -> 1% of each run, Pallas kernels for 17% -> 16%
where the time goes in v5:
time: 121 us; the launch traced here: 120 us
  Pallas kernels  47.3 us (39%)
  starting transfers between devices  46.7 us (39%)
  waiting for transfers between devices  22.3 us (18%)
  local copies, waits for them, and re-layouts  2.03 us (2%)
  between operations  1.66 us (1%)
    pallas_call x12, Pallas kernels, call(): pl.pallas_call(kernel, out_shape=[pltpu.HBM(s, F32) if k == 'H' else jax....  47.3 us
    all_to_all x5, starting transfers between devices, swap(): return lax.all_to_all(block, axis, split_axis=0, concat_axis=0, tiled=True)  33.1 us
    ppermute x4, waiting for transfers between devices, passed(): lax.ppermute(values, axis, [(i, (i + by) % size) for i in range(size)])  10.7 us
    all_to_all x5, waiting for transfers between devices, swap(): return lax.all_to_all(block, axis, split_axis=0, concat_axis=0, tiled=True)  10.7 us
    ppermute x4, starting transfers between devices, per_device(): lax.ppermute(b, 'gz', [(i, i ^ 1) for i in range(2 * half_layers)])  7.82 us
    ppermute x4, starting transfers between devices, passed(): lax.ppermute(values, axis, [(i, (i + by) % size) for i in range(size)])  3.63 us
  transfers between devices with their start and end apart: 16, of which 8 were waited for; matrix products, arithmetic and copies ran while one was open for 1% of the time, Pallas kernels for 16%

profile of v5, /device:TPU:1, one launch (start us, length us, event | category | flops | bytes accessed | tf_op | source)
XLA Modules:
  0.0 120.1 jit_solution(6719760938837170290)
XLA Ops:
  0.6 0.0 copy-start
  0.6 0.1 pad_add_fusion.ids_ref
  0.7 3.1 %start.1 = f32[32,32,128]{2,1,0:T(8,128)} custom-call(s32[2]{0:T(128)S(1)} %pad_add_fusion.ids_ref, f32[32,512]{1,0:T(8,128)} %phis_hbm.1, f32[32,512]{1,0:T(8,128)} %refs_9_.1, bf16[2,512,512]{2,1,0:T(8,128)(2,1)} %constant.15.clone.y_hbm.y_ref.refs_12_), custom_call_target="tpu_custom_call" | custom-call | tf_op jit(solution)/shard_map/start/pallas_call | solution.py:681
  3.9 12.0 %all-to-all-start = ((f32[32,32,128]{2,1,0:T(8,128)}), f32[32,32,128]{2,1,0:T(8,128)}, u32[]{:S(2)}, u32[]{:S(2)}) async-start(f32[32,32,128]{2,1,0:T(8,128)} %start.1), calls=%async_computation | async-start | bytes 1048576 | tf_op jit(solution)/shard_map/all_to_all | solution.py:704
  15.9 0.8 copy.11.count_ref
  16.6 2.2 %pack.1 = (f32[128,128]{1,0:T(8,128)}, f32[64,128]{1,0:T(8,128)}, f32[64,128]{1,0:T(8,128)}) custom-call(s32[2,4,2]{2,1,0:T(4,128)S(1)} %copy.11.count_ref, f32[8,2,4,2,128]{4,3,2,1,0:T(2,128)} %parts_hbm.1), custom_call_target="tpu_custom_call" | custom-call | tf_op jit(solution)/shard_map/pack/pallas_call | solution.py:681
  18.8 2.1 %collective-permute-start = (f32[64,128]{1,0:T(8,128)}, f32[64,128]{1,0:T(8,128)S(1)}, u32[]{:S(2)}, u32[]{:S(2)}) collective-permute-start(f32[64,128]{1,0:T(8,128)} %get-tuple-element.30), channel_id=1, source_target_pairs={{0,1},{1,2},{2,3},{3,4},{4,5},{5,6},{6,7},{7,0},{8,9},{9,10},{10,1... | collective-permute-start | bytes 98312 | tf_op jit(solution)/shard_map/ppermute | solution.py:700
  21.0 0.0 collective-permute-start.1
  21.0 1.3 %collective-permute-done.below_hbm = f32[64,128]{1,0:T(8,128)S(1)} collective-permute-done((f32[64,128]{1,0:T(8,128)}, f32[64,128]{1,0:T(8,128)S(1)}, u32[]{:S(2)}, u32[]{:S(2)}) %collective-permute-start) | collective-permute-done | bytes 32800 | tf_op jit(solution)/shard_map/ppermute | solution.py:700
  22.3 2.6 %collective-permute-done.1.above_hbm = f32[64,128]{1,0:T(8,128)S(1)} collective-permute-done((f32[64,128]{1,0:T(8,128)}, f32[64,128]{1,0:T(8,128)S(1)}, u32[]{:S(2)}, u32[]{:S(2)}) %collective-permute-start.1) | collective-permute-done | bytes 32800 | tf_op jit(solution)/shard_map/ppermute | solution.py:700
  24.9 0.6 copy-done.13
  25.5 1.7 %extend.1 = (f32[256,128]{1,0:T(8,128)}, f32[192,128]{1,0:T(8,128)}, f32[224,128]{1,0:T(8,128)}) custom-call(f32[64,128]{1,0:T(8,128)} %copy-done.12, f32[128,128]{1,0:T(8,128)} %get-tuple-element.31.own_hbm, f32[64,128]{1,0:T(8,128)} %copy-done.13, f32[32,512]{1,0:T(8,128)} %refs_9_.1), custom_call_target="tpu_custom_call" | custom-call | tf_op jit(solution)/shard_map/extend/pallas_call | solution.py:681
  27.3 4.8 %all-to-all-done = f32[32,32,128]{2,1,0:T(8,128)} async-done(((f32[32,32,128]{2,1,0:T(8,128)}), f32[32,32,128]{2,1,0:T(8,128)}, u32[]{:S(2)}, u32[]{:S(2)}) %all-to-all-start) | async-done | bytes 524320 | tf_op jit(solution)/shard_map/all_to_all | solution.py:704
  32.1 3.1 %first.1 = (f32[8,128,128]{2,1,0:T(8,128)}, f32[64,1024]{1,0:T(8,128)}) custom-call(s32[2]{0:T(128)S(1)} %pad_add_fusion.ids_ref, f32[1024,128]{1,0:T(8,128)} %bitcast.4.got_ref.gathered_ref, bf16[4,512,512]{2,1,0:T(8,128)(2,1)S(1)} %copy-done, f32[256,128]{1,0:T(8,128)} %get-tuple-element.33.wide_hbm), custom_call_target="tpu_custom_call" | custom-call | tf_op jit(solution)/shard_map/first/pallas_call | solution.py:681
  35.2 6.9 %all-to-all-start.1 = ((f32[8,128,128]{2,1,0:T(8,128)}), f32[8,128,128]{2,1,0:T(8,128)}, u32[]{:S(2)}, u32[]{:S(2)}) async-start(f32[8,128,128]{2,1,0:T(8,128)} %get-tuple-element.34), calls=%async_computation.1 | async-start | bytes 1048576 | tf_op jit(solution)/shard_map/all_to_all | solution.py:704
  42.1 0.7 collective-permute-start.3
  42.8 0.8 collective-permute-start.2
  43.6 6.8 %collective-permute-done.2.below_hbm.before_hbm.refs_8_ = f32[192,128]{1,0:T(8,128)S(1)} collective-permute-done((f32[192,128]{1,0:T(8,128)}, f32[192,128]{1,0:T(8,128)S(1)}, u32[]{:S(2)}, u32[]{:S(2)}) %collective-permute-start.2) | collective-permute-done | bytes 98336 | tf_op jit(solution)/shard_map/ppermute | solution.py:700
  50.4 0.0 collective-permute-done.3.above_hbm.after_hbm.refs_10_
  50.4 1.3 %all-to-all-done.1.got_ref = f32[8,128,128]{2,1,0:T(8,128)} async-done(((f32[8,128,128]{2,1,0:T(8,128)}), f32[8,128,128]{2,1,0:T(8,128)}, u32[]{:S(2)}, u32[]{:S(2)}) %all-to-all-start.1) | async-done | bytes 524320 | tf_op jit(solution)/shard_map/all_to_all | solution.py:704
  51.7 3.0 %second.1 = (f32[8,64,128]{2,1,0:T(8,128)}, f32[128,512]{1,0:T(8,128)}, f32[128,512]{1,0:T(8,128)}, f32[8,128]{1,0:T(8,128)S(1)}) custom-call(f32[8,128,128]{2,1,0:T(8,128)} %all-to-all-done.1.got_ref, f32[1024,128]{1,0:T(8,128)} %bitcast.4.got_ref.gathered_ref, bf16[2,512,512]{2,1,0:T(8,128)(2,1)S(1)} %copy-done.1, f32[192,128]{1,0:T(8,128)} %copy-done.4, ...), custom_call_target="tpu_custom_call" | custom-call | tf_op jit(solution)/shard_map/second/pallas_call | solution.py:681
  54.7 5.0 %all-to-all-start.2 = ((f32[8,64,128]{2,1,0:T(8,128)}), f32[8,64,128]{2,1,0:T(8,128)S(1)}, u32[]{:S(2)}, u32[]{:S(2)}) async-start(f32[8,64,128]{2,1,0:T(8,128)} %get-tuple-element.37), calls=%async_computation.2 | async-start | bytes 524288 | tf_op jit(solution)/shard_map/all_to_all | solution.py:704
  60.4 6.9 %reach.1 = (f32[48,128,128]{2,1,0:T(8,128)}, f32[16,3,128,128]{3,2,1,0:T(8,128)}, f32[16,1,128,128]{3,2,1,0:T(8,128)}, f32[16,128,128]{2,1,0:T(8,128)}, f32[512,128]{1,0:T(8,128)}, /*index=5*/f32[8,128]{1,0:T(8,128)S(1)}) custom-call(s32[2]{0:T(128)S(1)} %pad_add_fusion.ids_ref, s32[2,96]{1,0:T(2,128)S(1)} %bitcast.9, s32[1]{0:T(128)} %bitcast.6.count_ref, ...), custom_call_target="tpu_custom_call" | custom-call | tf_op jit(solution)/shard_map/reach/pallas_call | solution.py:681
  67.3 0.0 all-to-all-done.2.got_ref
  67.3 2.5 %third.1 = (f32[8,64,128]{2,1,0:T(8,128)}, f32[64,1024]{1,0:T(8,128)}, f32[8,128]{1,0:T(8,128)S(1)}) custom-call(s32[2]{0:T(128)S(1)} %pad_add_fusion.ids_ref, f32[8,64,128]{2,1,0:T(8,128)S(1)} %all-to-all-done.2.got_ref, bf16[4,512,512]{2,1,0:T(8,128)(2,1)S(1)} %copy-done, f32[8,128]{1,0:T(8,128)S(1)} %get-tuple-element.39.token_ref), custom_call_target="tpu_custom_call" | custom-call | tf_op jit(solution)/shard_map/third/pallas_call | solution.py:681
  69.8 4.8 %all-to-all-start.3 = ((f32[8,64,128]{2,1,0:T(8,128)}), f32[8,64,128]{2,1,0:T(8,128)S(1)}, u32[]{:S(2)}, u32[]{:S(2)}) async-start(f32[8,64,128]{2,1,0:T(8,128)} %get-tuple-element.40), calls=%async_computation.3 | async-start | bytes 524288 | tf_op jit(solution)/shard_map/all_to_all | solution.py:704
  74.6 5.5 %rest.1 = (f32[48,128,128]{2,1,0:T(8,128)}, f32[16,128,128]{2,1,0:T(8,128)}, f32[8,128]{1,0:T(8,128)S(1)}) custom-call(s32[2]{0:T(128)S(1)} %pad_add_fusion.ids_ref, s32[2,96]{1,0:T(2,128)S(1)} %bitcast.10, s32[1]{0:T(128)} %bitcast.7.count_ref, f32[16,3,128,128]{3,2,1,0:T(8,128)} %get-tuple-element.43.place_hbm.refs_15_, ...), custom_call_target="tpu_custom_call" | custom-call | tf_op jit(solution)/shard_map/rest/pallas_call | solution.py:681
  80.2 1.0 all-to-all-done.3.got_ref
  81.2 2.2 %fourth.1 = (f32[8,64,128]{2,1,0:T(8,128)}, f32[8,128]{1,0:T(8,128)S(1)}) custom-call(f32[8,64,128]{2,1,0:T(8,128)S(1)} %all-to-all-done.3.got_ref, f32[128,512]{1,0:T(8,128)} %get-tuple-element.41.eta_hbm, f32[128,512]{1,0:T(8,128)} %get-tuple-element.42.curve_hbm, bf16[2,512,512]{2,1,0:T(8,128)(2,1)S(1)} %copy-done.1, f32[8,128]{1,0:T(8,128)S(1)} %get-tuple-element.48.token_ref), custom_call_target="tpu_custom_call" | custom-call | tf_op jit(solution)/shard_map/fourth/pallas_call | solution.py:681
  83.4 4.4 %all-to-all-start.4 = ((f32[8,64,128]{2,1,0:T(8,128)}), f32[8,64,128]{2,1,0:T(8,128)S(1)}, u32[]{:S(2)}, u32[]{:S(2)}) async-start(f32[8,64,128]{2,1,0:T(8,128)} %get-tuple-element.49), calls=%async_computation.4 | async-start | bytes 524288 | tf_op jit(solution)/shard_map/all_to_all | solution.py:704
  87.7 2.9 %early.1.early_hbm = f32[144,128]{1,0:T(8,128)} custom-call(s32[2]{0:T(128)S(1)} %pad_add_fusion.ids_ref, bf16[1096,2048]{1,0:T(8,128)(2,1)} %constant.17.clone.own_hbm, f32[64,1024]{1,0:T(8,128)} %get-tuple-element.50.first_hbm, f32[64,1024]{1,0:T(8,128)} %get-tuple-element.51.second_hbm, f32[8,128]{1,0:T(8,128)S(1)} %get-tuple-element.52.token_ref), custom_call_target="tpu_custom_call" | custom-call | tf_op jit(solution)/shard_map/early/pallas_call | solution.py:681
  90.7 3.6 %all-to-all-done.4.got_ref = f32[8,64,128]{2,1,0:T(8,128)S(1)} async-done(((f32[8,64,128]{2,1,0:T(8,128)}), f32[8,64,128]{2,1,0:T(8,128)S(1)}, u32[]{:S(2)}, u32[]{:S(2)}) %all-to-all-start.4) | async-done | bytes 262176 | tf_op jit(solution)/shard_map/all_to_all | solution.py:704
  94.3 2.8 %fifth.1.refs_0_ = f32[184,128]{1,0:T(8,128)} custom-call(s32[2]{0:T(128)S(1)} %pad_add_fusion.ids_ref, f32[8,64,128]{2,1,0:T(8,128)S(1)} %all-to-all-done.4.got_ref, bf16[4,512,512]{2,1,0:T(8,128)(2,1)S(1)} %copy-done, bf16[1096,2048]{1,0:T(8,128)(2,1)} %constant.17.clone.own_hbm, f32[64,1024]{1,0:T(8,128)} %get-tuple-element.50.first_hbm, ...), custom_call_target="tpu_custom_call" | custom-call | tf_op jit(solution)/shard_map/fifth/pallas_call | solution.py:681
  97.1 1.0 collective-permute-start.6
  98.0 1.2 %collective-permute-start.5 = (f32[184,128]{1,0:T(8,128)}, f32[184,128]{1,0:T(8,128)S(1)}, u32[]{:S(2)}, u32[]{:S(2)}) collective-permute-start(f32[184,128]{1,0:T(8,128)} %fifth.1.refs_0_), channel_id=1, source_target_pairs={{0,4},{1,5},{2,6},{3,7},{4,0},{5,1},{6,2},{7,3},{8,12},{9,13},{10,... | collective-permute-start | bytes 282632 | tf_op jit(solution)/shard_map/ppermute | solution.py:867
  99.2 0.0 collective-permute-start.4
  99.2 1.6 %collective-permute-start.7 = (f32[184,128]{1,0:T(8,128)}, f32[184,128]{1,0:T(8,128)S(1)}, u32[]{:S(2)}, u32[]{:S(2)}) collective-permute-start(f32[184,128]{1,0:T(8,128)} %fifth.1.refs_0_), channel_id=1, source_target_pairs={{0,1},{1,0},{2,3},{3,2},{4,5},{5,4},{6,7},{7,6},{8,9},{9,8},{10,11... | collective-permute-start | bytes 282632 | tf_op jit(solution)/shard_map/ppermute | solution.py:879
  100.8 0.0 collective-permute-done.6.refs_3_
  100.8 2.6 %collective-permute-start.10 = (f32[184,128]{1,0:T(8,128)S(1)}, f32[184,128]{1,0:T(8,128)S(1)}, u32[]{:S(2)}, u32[]{:S(2)}) collective-permute-start(f32[184,128]{1,0:T(8,128)S(1)} %collective-permute-done.6.refs_3_), channel_id=1, source_target_pairs={{0,1},{1,0},{2,3},{3,2},{4,5},{5,4},{6,7},{7,6},{8,9},{9,8},{10,11... | collective-permute-start | bytes 282632 | tf_op jit(solution)/shard_map/ppermute | solution.py:879
  103.5 0.0 collective-permute-done.5.refs_2_
  103.5 2.6 %collective-permute-start.9 = (f32[184,128]{1,0:T(8,128)S(1)}, f32[184,128]{1,0:T(8,128)S(1)}, u32[]{:S(2)}, u32[]{:S(2)}) collective-permute-start(f32[184,128]{1,0:T(8,128)S(1)} %collective-permute-done.5.refs_2_), channel_id=1, source_target_pairs={{0,1},{1,0},{2,3},{3,2},{4,5},{5,4},{6,7},{7,6},{8,9},{9,8},{10,11... | collective-permute-start | bytes 282632 | tf_op jit(solution)/shard_map/ppermute | solution.py:879
  106.1 0.0 collective-permute-done.4.refs_1_
  106.1 1.0 collective-permute-start.8
  107.1 0.0 collective-permute-done.7.refs_4_
  107.1 0.0 collective-permute-done.10.refs_7_
  107.1 0.9 collective-permute-done.8.refs_5_
  108.0 0.6 copy-done.11
  108.6 11.3 %last.1 = (f32[32,512]{1,0:T(8,128)}, f32[16,128]{1,0:T(8,128)}) custom-call(s32[2]{0:T(128)S(1)} %pad_add_fusion.ids_ref, s32[2,96]{1,0:T(2,128)S(1)} %bitcast.11, s32[1]{0:T(128)} %bitcast.8.count_ref, f32[184,128]{1,0:T(8,128)} %fifth.1.refs_0_, f32[184,128]{1,0:T(8,128)} %copy-done.7, f32[184,128]{1,0:T(8,128)} %copy-done.6, f32[184,128]{1,0:T(8,128)} %copy-done.5, ...), custom_call_target="tpu_custom_call" | custom-call | tf_op jit(solution)/shard_map/last/pallas_call | solution.py:681
  (28 shorter events, 0.1 us)
Async XLA Ops:
  0.6 31.5 %copy-start = (bf16[4,512,512]{2,1,0:T(8,128)(2,1)S(1)}, bf16[4,512,512]{2,1,0:T(8,128)(2,1)}, u32[]{:S(2)}) copy-start(bf16[4,512,512]{2,1,0:T(8,128)(2,1)} %constant.16.clone.x_ref) | copy-start | bytes 6291460
  0.7 50.9 %copy-start.1 = (bf16[2,512,512]{2,1,0:T(8,128)(2,1)S(1)}, bf16[2,512,512]{2,1,0:T(8,128)(2,1)}, u32[]{:S(2)}) copy-start(bf16[2,512,512]{2,1,0:T(8,128)(2,1)} %constant.15.clone.y_hbm.y_ref.refs_12_) | copy-start | bytes 3145732
  3.9 28.3 %all-to-all-start = ((f32[32,32,128]{2,1,0:T(8,128)}), f32[32,32,128]{2,1,0:T(8,128)}, u32[]{:S(2)}, u32[]{:S(2)}) async-start(f32[32,32,128]{2,1,0:T(8,128)} %start.1), calls=%async_computation | async-start | bytes 1048576 | tf_op jit(solution)/shard_map/all_to_all | solution.py:704
  18.8 3.5 %collective-permute-start = (f32[64,128]{1,0:T(8,128)}, f32[64,128]{1,0:T(8,128)S(1)}, u32[]{:S(2)}, u32[]{:S(2)}) collective-permute-start(f32[64,128]{1,0:T(8,128)} %get-tuple-element.30), channel_id=1, source_target_pairs={{0,1},{1,2},{2,3},{3,4},{4,5},{5,6},{6,7},{7,0},{8,9},{9,10},{10,1... | collective-permute-start | bytes 98312 | tf_op jit(solution)/shard_map/ppermute | solution.py:700
  21.0 4.0 %collective-permute-start.1 = (f32[64,128]{1,0:T(8,128)}, f32[64,128]{1,0:T(8,128)S(1)}, u32[]{:S(2)}, u32[]{:S(2)}) collective-permute-start(f32[64,128]{1,0:T(8,128)} %get-tuple-element.32), channel_id=1, source_target_pairs={{0,7},{1,0},{2,1},{3,2},{4,3},{5,4},{6,5},{7,6},{8,15},{9,8},{10,9... | collective-permute-start | bytes 98312 | tf_op jit(solution)/shard_map/ppermute | solution.py:700
  22.3 2.6 %copy-start.12 = (f32[64,128]{1,0:T(8,128)}, f32[64,128]{1,0:T(8,128)S(1)}, u32[]{:S(2)}) copy-start(f32[64,128]{1,0:T(8,128)S(1)} %collective-permute-done.below_hbm) | copy-start | bytes 98308
  24.9 0.6 copy-start.13
  27.3 14.8 %copy-start.14 = (f32[224,128]{1,0:T(8,128)S(1)}, f32[224,128]{1,0:T(8,128)}, u32[]{:S(2)}) copy-start(f32[224,128]{1,0:T(8,128)} %get-tuple-element.36) | copy-start | bytes 344068
  32.1 28.3 %copy-start.2 = (s32[1,1,2,96]{3,2,1,0:T(2,128)S(1)}, s32[1,1,2,96]{3,2,1,0:T(2,128)}, u32[]{:S(2)}) copy-start(s32[1,1,2,96]{3,2,1,0:T(2,128)} %param.13) | copy-start | bytes 2308
  35.2 16.5 %all-to-all-start.1 = ((f32[8,128,128]{2,1,0:T(8,128)}), f32[8,128,128]{2,1,0:T(8,128)}, u32[]{:S(2)}, u32[]{:S(2)}) async-start(f32[8,128,128]{2,1,0:T(8,128)} %get-tuple-element.34), calls=%async_computation.1 | async-start | bytes 1048576 | tf_op jit(solution)/shard_map/all_to_all | solution.py:704
  42.1 8.3 %collective-permute-start.3 = (f32[224,128]{1,0:T(8,128)S(1)}, f32[224,128]{1,0:T(8,128)S(1)}, u32[]{:S(2)}, u32[]{:S(2)}) collective-permute-start(f32[224,128]{1,0:T(8,128)S(1)} %copy-done.14), channel_id=1, source_target_pairs={{0,248},{8,0},{16,8},{24,16},{32,24},{40,32},{48,40},{56,48},{64,5... | collective-permute-start | bytes 344072 | tf_op jit(solution)/shard_map/ppermute | solution.py:700
  42.8 7.6 %collective-permute-start.2 = (f32[192,128]{1,0:T(8,128)}, f32[192,128]{1,0:T(8,128)S(1)}, u32[]{:S(2)}, u32[]{:S(2)}) collective-permute-start(f32[192,128]{1,0:T(8,128)} %get-tuple-element.35), channel_id=1, source_target_pairs={{0,8},{8,16},{16,24},{24,32},{32,40},{40,48},{48,56},{56,64},{64,7... | collective-permute-start | bytes 294920 | tf_op jit(solution)/shard_map/ppermute | solution.py:700
  50.4 1.3 %copy-start.4 = (f32[192,128]{1,0:T(8,128)}, f32[192,128]{1,0:T(8,128)S(1)}, u32[]{:S(2)}) copy-start(f32[192,128]{1,0:T(8,128)S(1)} %collective-permute-done.2.below_hbm.before_hbm.refs_8_) | copy-start | bytes 294916
  50.4 1.3 %copy-start.3 = (f32[224,128]{1,0:T(8,128)}, f32[224,128]{1,0:T(8,128)S(1)}, u32[]{:S(2)}) copy-start(f32[224,128]{1,0:T(8,128)S(1)} %collective-permute-done.3.above_hbm.after_hbm.refs_10_) | copy-start | bytes 344068
  54.7 12.7 %all-to-all-start.2 = ((f32[8,64,128]{2,1,0:T(8,128)}), f32[8,64,128]{2,1,0:T(8,128)S(1)}, u32[]{:S(2)}, u32[]{:S(2)}) async-start(f32[8,64,128]{2,1,0:T(8,128)} %get-tuple-element.37), calls=%async_computation.2 | async-start | bytes 524288 | tf_op jit(solution)/shard_map/all_to_all | solution.py:704
  69.8 11.3 %all-to-all-start.3 = ((f32[8,64,128]{2,1,0:T(8,128)}), f32[8,64,128]{2,1,0:T(8,128)S(1)}, u32[]{:S(2)}, u32[]{:S(2)}) async-start(f32[8,64,128]{2,1,0:T(8,128)} %get-tuple-element.40), calls=%async_computation.3 | async-start | bytes 524288 | tf_op jit(solution)/shard_map/all_to_all | solution.py:704
  83.4 10.9 %all-to-all-start.4 = ((f32[8,64,128]{2,1,0:T(8,128)}), f32[8,64,128]{2,1,0:T(8,128)S(1)}, u32[]{:S(2)}, u32[]{:S(2)}) async-start(f32[8,64,128]{2,1,0:T(8,128)} %get-tuple-element.49), calls=%async_computation.4 | async-start | bytes 524288 | tf_op jit(solution)/shard_map/all_to_all | solution.py:704
  97.1 3.8 %collective-permute-start.6 = (f32[184,128]{1,0:T(8,128)}, f32[184,128]{1,0:T(8,128)S(1)}, u32[]{:S(2)}, u32[]{:S(2)}) collective-permute-start(f32[184,128]{1,0:T(8,128)} %fifth.1.refs_0_), channel_id=1, source_target_pairs={{0,6},{1,7},{2,0},{3,1},{4,2},{5,3},{6,4},{7,5},{8,14},{9,15},{10,... | collective-permute-start | bytes 282632 | tf_op jit(solution)/shard_map/ppermute | solution.py:867
  98.0 5.5 %collective-permute-start.5 = (f32[184,128]{1,0:T(8,128)}, f32[184,128]{1,0:T(8,128)S(1)}, u32[]{:S(2)}, u32[]{:S(2)}) collective-permute-start(f32[184,128]{1,0:T(8,128)} %fifth.1.refs_0_), channel_id=1, source_target_pairs={{0,4},{1,5},{2,6},{3,7},{4,0},{5,1},{6,2},{7,3},{8,12},{9,13},{10,... | collective-permute-start | bytes 282632 | tf_op jit(solution)/shard_map/ppermute | solution.py:867
  99.2 6.9 %collective-permute-start.4 = (f32[184,128]{1,0:T(8,128)}, f32[184,128]{1,0:T(8,128)S(1)}, u32[]{:S(2)}, u32[]{:S(2)}) collective-permute-start(f32[184,128]{1,0:T(8,128)} %fifth.1.refs_0_), channel_id=1, source_target_pairs={{0,2},{1,3},{2,4},{3,5},{4,6},{5,7},{6,0},{7,1},{8,10},{9,11},{10,... | collective-permute-start | bytes 282632 | tf_op jit(solution)/shard_map/ppermute | solution.py:867
  99.2 7.8 %collective-permute-start.7 = (f32[184,128]{1,0:T(8,128)}, f32[184,128]{1,0:T(8,128)S(1)}, u32[]{:S(2)}, u32[]{:S(2)}) collective-permute-start(f32[184,128]{1,0:T(8,128)} %fifth.1.refs_0_), channel_id=1, source_target_pairs={{0,1},{1,0},{2,3},{3,2},{4,5},{5,4},{6,7},{7,6},{8,9},{9,8},{10,11... | collective-permute-start | bytes 282632 | tf_op jit(solution)/shard_map/ppermute | solution.py:879
  100.8 7.2 %copy-start.5 = (f32[184,128]{1,0:T(8,128)}, f32[184,128]{1,0:T(8,128)S(1)}, u32[]{:S(2)}) copy-start(f32[184,128]{1,0:T(8,128)S(1)} %collective-permute-done.6.refs_3_) | copy-start | bytes 282628
  100.8 6.2 %collective-permute-start.10 = (f32[184,128]{1,0:T(8,128)S(1)}, f32[184,128]{1,0:T(8,128)S(1)}, u32[]{:S(2)}, u32[]{:S(2)}) collective-permute-start(f32[184,128]{1,0:T(8,128)S(1)} %collective-permute-done.6.refs_3_), channel_id=1, source_target_pairs={{0,1},{1,0},{2,3},{3,2},{4,5},{5,4},{6,7},{7,6},{8,9},{9,8},{10,11... | collective-permute-start | bytes 282632 | tf_op jit(solution)/shard_map/ppermute | solution.py:879
  103.5 4.5 %copy-start.6 = (f32[184,128]{1,0:T(8,128)}, f32[184,128]{1,0:T(8,128)S(1)}, u32[]{:S(2)}) copy-start(f32[184,128]{1,0:T(8,128)S(1)} %collective-permute-done.5.refs_2_) | copy-start | bytes 282628
  103.5 3.6 %collective-permute-start.9 = (f32[184,128]{1,0:T(8,128)S(1)}, f32[184,128]{1,0:T(8,128)S(1)}, u32[]{:S(2)}, u32[]{:S(2)}) collective-permute-start(f32[184,128]{1,0:T(8,128)S(1)} %collective-permute-done.5.refs_2_), channel_id=1, source_target_pairs={{0,1},{1,0},{2,3},{3,2},{4,5},{5,4},{6,7},{7,6},{8,9},{9,8},{10,11... | collective-permute-start | bytes 282632 | tf_op jit(solution)/shard_map/ppermute | solution.py:879
  106.1 1.9 %copy-start.7 = (f32[184,128]{1,0:T(8,128)}, f32[184,128]{1,0:T(8,128)S(1)}, u32[]{:S(2)}) copy-start(f32[184,128]{1,0:T(8,128)S(1)} %collective-permute-done.4.refs_1_) | copy-start | bytes 282628
  106.1 1.9 %collective-permute-start.8 = (f32[184,128]{1,0:T(8,128)S(1)}, f32[184,128]{1,0:T(8,128)S(1)}, u32[]{:S(2)}, u32[]{:S(2)}) collective-permute-start(f32[184,128]{1,0:T(8,128)S(1)} %collective-permute-done.4.refs_1_), channel_id=1, source_target_pairs={{0,1},{1,0},{2,3},{3,2},{4,5},{5,4},{6,7},{7,6},{8,9},{9,8},{10,11... | collective-permute-start | bytes 282632 | tf_op jit(solution)/shard_map/ppermute | solution.py:879
  107.1 1.0 copy-start.8
  107.1 1.0 copy-start.9
  107.1 0.9 copy-start.10
  108.0 0.6 copy-start.11

commit v6 on v5

--- a/solution.py
+++ b/solution.py
@@ -23,7 +23,9 @@
 SM = pl.BlockSpec(memory_space=pltpu.SMEM)
 HB = pl.BlockSpec(memory_space=pltpu.HBM)
 GROUP = 8
-PART = 48
+PAIRS = 96
+PART = 32
+REST = PAIRS - PART
 TALL = 80
 EARLY = 2 * ROWS
 
@@ -149,12 +151,9 @@
         copy.wait()
 
 
-def send_block(block_ref, out_ref, sems):
-    wait_all([fetch(block_ref, out_ref.at[s], sems, s) for s in range(out_ref.shape[0])])
-
-
 def start_kernel(
-    ids_ref, phis_hbm, eta_hbm, y_hbm, out_ref, phis_ref, eta_ref, table_ref, block_ref, sems, out_sems
+    ids_ref, phis_hbm, eta_hbm, y_hbm, out_ref, phis_ref, eta_ref, table_ref, block_ref, all_ref,
+    sems, out_sems,
 ):
     first = pl.multiple_of(64 * ids_ref[1], 64)
     rows = pl.multiple_of(8 * (ids_ref[1] // 2), 8)
@@ -170,7 +169,11 @@
     block_ref[:16] = jnp.concatenate([coefs[:16], coefs[16:]], 1)
     for j in range(4):
         block_ref[16 + 4 * j : 20 + 4 * j] = eta[:, 128 * j : 128 * j + 128]
-    send_block(block_ref, out_ref, out_sems)
+    all_ref[...] = jnp.broadcast_to(block_ref[...][None], all_ref.shape)
+    wait_all([
+        fetch(all_ref.at[pl.ds(8 * k, 8)], out_ref.at[pl.ds(8 * k, 8)], out_sems, k)
+        for k in range(4)
+    ])
 
 
 def first_kernel(
@@ -403,7 +406,7 @@
 
 
 def reach_groups(count_ref, part):
-    used = jnp.clip(count_ref[0] - part * PART, 0, PART)
+    used = jnp.clip(count_ref[0] - part * PART, 0, REST if part else PART)
     return (used + GROUP - 1) // GROUP
 
 
@@ -532,8 +535,6 @@
     copies = [
         fetch(eta_hbm, eta_ref.at[pl.ds(16, 32), :], sems, 0),
         fetch(cells_hbm, cells_ref, sems, 1),
-        fetch(place_hbm, place_ref, sems, 2),
-        fetch(sum_hbm, sum_ref, sems, 3),
     ]
 
     for j in range(4):
@@ -562,11 +563,12 @@
         return carry
 
     groups, rest_groups = reach_groups(count_ref, 0), reach_groups(count_ref, 1)
-    lax.fori_loop(0, groups, start_group, 0)
-    lax.fori_loop(0, rest_groups, start_rest, 0)
     slab = ids_ref[0]
     layer = ids_ref[1]
     wait_all(block_copies)
+    copies += [fetch(place_hbm, place_ref, sems, 2), fetch(sum_hbm, sum_ref, sems, 3)]
+    lax.fori_loop(0, groups, start_group, 0)
+    lax.fori_loop(0, rest_groups, start_rest, 0)
     for step in range(4):
         share = (layer // 2 + 4 - step) % 4
         lanes = pl.ds(pl.multiple_of(128 * share, 128), 128)
@@ -748,8 +750,9 @@
             (8, NY),
             pltpu.VMEM((2, 64, NY), BF16),
             (32, 128),
+            (32, 32, 128),
             dma_sems(3),
-            dma_sems(32),
+            dma_sems(4),
         ],
     )
     gathered = swap(block, "gx").reshape(1024, 128)
@@ -815,18 +818,18 @@
         reach_rest_kernel,
         (ids, pairs, count, place, density, before, cells, token),
         "SSSHHHHV",
-        [((PART, 128, 128), "H"), ((16, 128, 128), "H"), ((8, 128), "V")],
+        [((REST, 128, 128), "H"), ((16, 128, 128), "H"), ((8, 128), "V")],
         "rest",
         16,
         [
-            (PART, 128, 128),
+            (REST, 128, 128),
             (16, 3, 128, 128),
             (16, 1, 128, 128),
             (16, 128, 128),
             (512, 128),
             (6, 64, 128),
             dma_sems(5),
-            dma_sems(PART // GROUP),
+            dma_sems(REST // GROUP),
         ],
     )
     block, token = call(

time: 121 us -> 119 us (0.983); the launches traced: 120 us -> 117 us
  Pallas kernels: 47.3 us -> 42.1 us
  waiting for transfers between devices: 22.3 us -> 23.6 us
    pallas_call x12, Pallas kernels: 47.3 us -> 42.1 us  [call(): pl.pallas_call(kernel, out_shape=[pltpu.HBM(s, F32) if k == 'H' else jax....]
    all_to_all x5, waiting for transfers between devices: 10.7 us -> 11.9 us  [swap(): return lax.all_to_all(block, axis, split_axis=0, concat_axis=0, tiled=True)]
  transfers between devices with their start and end apart: 16 -> 16, of which waited for: 8 -> 8; matrix products, arithmetic and copies ran while one was open for 1% -> 1% of each run, Pallas kernels for 16% -> 15%
where the time goes in v6:
time: 119 us; the launch traced here: 117 us
  starting transfers between devices  47.4 us (40%)
  Pallas kernels  42.1 us (35%)
  waiting for transfers between devices  23.6 us (20%)
  local copies, waits for them, and re-layouts  2.03 us (2%)
  between operations  1.66 us (1%)
    pallas_call x12, Pallas kernels, call(): pl.pallas_call(kernel, out_shape=[pltpu.HBM(s, F32) if k == 'H' else jax....  42.1 us
    all_to_all x5, starting transfers between devices, swap(): return lax.all_to_all(block, axis, split_axis=0, concat_axis=0, tiled=True)  33.8 us
    all_to_all x5, waiting for transfers between devices, swap(): return lax.all_to_all(block, axis, split_axis=0, concat_axis=0, tiled=True)  11.9 us
    ppermute x4, waiting for transfers between devices, passed(): lax.ppermute(values, axis, [(i, (i + by) % size) for i in range(size)])  10.7 us
    ppermute x4, starting transfers between devices, per_device(): lax.ppermute(b, 'gz', [(i, i ^ 1) for i in range(2 * half_layers)])  7.81 us
    ppermute x4, starting transfers between devices, passed(): lax.ppermute(values, axis, [(i, (i + by) % size) for i in range(size)])  3.63 us
  transfers between devices with their start and end apart: 16, of which 8 were waited for; matrix products, arithmetic and copies ran while one was open for 1% of the time, Pallas kernels for 15%

profile of v6, /device:TPU:1, one launch (start us, length us, event | category | flops | bytes accessed | tf_op | source)
XLA Modules:
  0.0 116.9 jit_solution(3957317504962740683)
XLA Ops:
  0.6 0.0 copy-start
  0.6 0.1 pad_add_fusion.ids_ref
  0.7 2.9 %start.1 = f32[32,32,128]{2,1,0:T(8,128)} custom-call(s32[2]{0:T(128)S(1)} %pad_add_fusion.ids_ref, f32[32,512]{1,0:T(8,128)} %phis_hbm.1, f32[32,512]{1,0:T(8,128)} %refs_9_.1, bf16[2,512,512]{2,1,0:T(8,128)(2,1)} %constant.15.clone.y_hbm.y_ref.refs_12_), custom_call_target="tpu_custom_call" | custom-call | tf_op jit(solution)/shard_map/start/pallas_call | solution.py:683
  3.6 12.0 %all-to-all-start = ((f32[32,32,128]{2,1,0:T(8,128)}), f32[32,32,128]{2,1,0:T(8,128)}, u32[]{:S(2)}, u32[]{:S(2)}) async-start(f32[32,32,128]{2,1,0:T(8,128)} %start.1), calls=%async_computation | async-start | bytes 1048576 | tf_op jit(solution)/shard_map/all_to_all | solution.py:706
  15.6 0.8 copy.11.count_ref
  16.4 2.2 %pack.1 = (f32[128,128]{1,0:T(8,128)}, f32[64,128]{1,0:T(8,128)}, f32[64,128]{1,0:T(8,128)}) custom-call(s32[2,4,2]{2,1,0:T(4,128)S(1)} %copy.11.count_ref, f32[8,2,4,2,128]{4,3,2,1,0:T(2,128)} %parts_hbm.1), custom_call_target="tpu_custom_call" | custom-call | tf_op jit(solution)/shard_map/pack/pallas_call | solution.py:683
  18.6 2.1 %collective-permute-start = (f32[64,128]{1,0:T(8,128)}, f32[64,128]{1,0:T(8,128)S(1)}, u32[]{:S(2)}, u32[]{:S(2)}) collective-permute-start(f32[64,128]{1,0:T(8,128)} %get-tuple-element.30), channel_id=1, source_target_pairs={{0,1},{1,2},{2,3},{3,4},{4,5},{5,6},{6,7},{7,0},{8,9},{9,10},{10,1... | collective-permute-start | bytes 98312 | tf_op jit(solution)/shard_map/ppermute | solution.py:702
  20.8 0.0 collective-permute-start.1
  20.8 1.3 %collective-permute-done.below_hbm = f32[64,128]{1,0:T(8,128)S(1)} collective-permute-done((f32[64,128]{1,0:T(8,128)}, f32[64,128]{1,0:T(8,128)S(1)}, u32[]{:S(2)}, u32[]{:S(2)}) %collective-permute-start) | collective-permute-done | bytes 32800 | tf_op jit(solution)/shard_map/ppermute | solution.py:702
  22.1 2.6 %collective-permute-done.1.above_hbm = f32[64,128]{1,0:T(8,128)S(1)} collective-permute-done((f32[64,128]{1,0:T(8,128)}, f32[64,128]{1,0:T(8,128)S(1)}, u32[]{:S(2)}, u32[]{:S(2)}) %collective-permute-start.1) | collective-permute-done | bytes 32800 | tf_op jit(solution)/shard_map/ppermute | solution.py:702
  24.7 0.6 copy-done.13
  25.3 1.8 %extend.1 = (f32[256,128]{1,0:T(8,128)}, f32[192,128]{1,0:T(8,128)}, f32[224,128]{1,0:T(8,128)}) custom-call(f32[64,128]{1,0:T(8,128)} %copy-done.12, f32[128,128]{1,0:T(8,128)} %get-tuple-element.31.own_hbm, f32[64,128]{1,0:T(8,128)} %copy-done.13, f32[32,512]{1,0:T(8,128)} %refs_9_.1), custom_call_target="tpu_custom_call" | custom-call | tf_op jit(solution)/shard_map/extend/pallas_call | solution.py:683
  27.1 4.8 %all-to-all-done = f32[32,32,128]{2,1,0:T(8,128)} async-done(((f32[32,32,128]{2,1,0:T(8,128)}), f32[32,32,128]{2,1,0:T(8,128)}, u32[]{:S(2)}, u32[]{:S(2)}) %all-to-all-start) | async-done | bytes 524320 | tf_op jit(solution)/shard_map/all_to_all | solution.py:706
  31.9 3.1 %first.1 = (f32[8,128,128]{2,1,0:T(8,128)}, f32[64,1024]{1,0:T(8,128)}) custom-call(s32[2]{0:T(128)S(1)} %pad_add_fusion.ids_ref, f32[1024,128]{1,0:T(8,128)} %bitcast.4.got_ref.gathered_ref, bf16[4,512,512]{2,1,0:T(8,128)(2,1)S(1)} %copy-done, f32[256,128]{1,0:T(8,128)} %get-tuple-element.33.wide_hbm), custom_call_target="tpu_custom_call" | custom-call | tf_op jit(solution)/shard_map/first/pallas_call | solution.py:683
  35.0 6.9 %all-to-all-start.1 = ((f32[8,128,128]{2,1,0:T(8,128)}), f32[8,128,128]{2,1,0:T(8,128)}, u32[]{:S(2)}, u32[]{:S(2)}) async-start(f32[8,128,128]{2,1,0:T(8,128)} %get-tuple-element.34), calls=%async_computation.1 | async-start | bytes 1048576 | tf_op jit(solution)/shard_map/all_to_all | solution.py:706
  41.8 0.7 collective-permute-start.3
  42.6 0.8 collective-permute-start.2
  43.3 6.8 %collective-permute-done.2.below_hbm.before_hbm.refs_8_ = f32[192,128]{1,0:T(8,128)S(1)} collective-permute-done((f32[192,128]{1,0:T(8,128)}, f32[192,128]{1,0:T(8,128)S(1)}, u32[]{:S(2)}, u32[]{:S(2)}) %collective-permute-start.2) | collective-permute-done | bytes 98336 | tf_op jit(solution)/shard_map/ppermute | solution.py:702
  50.1 0.0 collective-permute-done.3.above_hbm.after_hbm.refs_10_
  50.1 1.3 %all-to-all-done.1.got_ref = f32[8,128,128]{2,1,0:T(8,128)} async-done(((f32[8,128,128]{2,1,0:T(8,128)}), f32[8,128,128]{2,1,0:T(8,128)}, u32[]{:S(2)}, u32[]{:S(2)}) %all-to-all-start.1) | async-done | bytes 524320 | tf_op jit(solution)/shard_map/all_to_all | solution.py:706
  51.4 3.0 %second.1 = (f32[8,64,128]{2,1,0:T(8,128)}, f32[128,512]{1,0:T(8,128)}, f32[128,512]{1,0:T(8,128)}, f32[8,128]{1,0:T(8,128)S(1)}) custom-call(f32[8,128,128]{2,1,0:T(8,128)} %all-to-all-done.1.got_ref, f32[1024,128]{1,0:T(8,128)} %bitcast.4.got_ref.gathered_ref, bf16[2,512,512]{2,1,0:T(8,128)(2,1)S(1)} %copy-done.1, f32[192,128]{1,0:T(8,128)} %copy-done.4, ...), custom_call_target="tpu_custom_call" | custom-call | tf_op jit(solution)/shard_map/second/pallas_call | solution.py:683
  54.4 5.0 %all-to-all-start.2 = ((f32[8,64,128]{2,1,0:T(8,128)}), f32[8,64,128]{2,1,0:T(8,128)S(1)}, u32[]{:S(2)}, u32[]{:S(2)}) async-start(f32[8,64,128]{2,1,0:T(8,128)} %get-tuple-element.37), calls=%async_computation.2 | async-start | bytes 524288 | tf_op jit(solution)/shard_map/all_to_all | solution.py:706
  60.1 5.9 %reach.1 = (f32[32,128,128]{2,1,0:T(8,128)}, f32[16,3,128,128]{3,2,1,0:T(8,128)}, f32[16,1,128,128]{3,2,1,0:T(8,128)}, f32[16,128,128]{2,1,0:T(8,128)}, f32[512,128]{1,0:T(8,128)}, /*index=5*/f32[8,128]{1,0:T(8,128)S(1)}) custom-call(s32[2]{0:T(128)S(1)} %pad_add_fusion.ids_ref, s32[2,96]{1,0:T(2,128)S(1)} %bitcast.9, s32[1]{0:T(128)} %bitcast.6.count_ref, ...), custom_call_target="tpu_custom_call" | custom-call | tf_op jit(solution)/shard_map/reach/pallas_call | solution.py:683
  66.1 0.0 all-to-all-done.2.got_ref
  66.1 2.5 %third.1 = (f32[8,64,128]{2,1,0:T(8,128)}, f32[64,1024]{1,0:T(8,128)}, f32[8,128]{1,0:T(8,128)S(1)}) custom-call(s32[2]{0:T(128)S(1)} %pad_add_fusion.ids_ref, f32[8,64,128]{2,1,0:T(8,128)S(1)} %all-to-all-done.2.got_ref, bf16[4,512,512]{2,1,0:T(8,128)(2,1)S(1)} %copy-done, f32[8,128]{1,0:T(8,128)S(1)} %get-tuple-element.39.token_ref), custom_call_target="tpu_custom_call" | custom-call | tf_op jit(solution)/shard_map/third/pallas_call | solution.py:683
  68.6 4.9 %all-to-all-start.3 = ((f32[8,64,128]{2,1,0:T(8,128)}), f32[8,64,128]{2,1,0:T(8,128)S(1)}, u32[]{:S(2)}, u32[]{:S(2)}) async-start(f32[8,64,128]{2,1,0:T(8,128)} %get-tuple-element.40), calls=%async_computation.3 | async-start | bytes 524288 | tf_op jit(solution)/shard_map/all_to_all | solution.py:706
  73.4 4.2 %rest.1 = (f32[64,128,128]{2,1,0:T(8,128)}, f32[16,128,128]{2,1,0:T(8,128)}, f32[8,128]{1,0:T(8,128)S(1)}) custom-call(s32[2]{0:T(128)S(1)} %pad_add_fusion.ids_ref, s32[2,96]{1,0:T(2,128)S(1)} %bitcast.10, s32[1]{0:T(128)} %bitcast.7.count_ref, f32[16,3,128,128]{3,2,1,0:T(8,128)} %get-tuple-element.43.place_hbm.refs_15_, ...), custom_call_target="tpu_custom_call" | custom-call | tf_op jit(solution)/shard_map/rest/pallas_call | solution.py:683
  77.7 2.3 %all-to-all-done.3.got_ref = f32[8,64,128]{2,1,0:T(8,128)S(1)} async-done(((f32[8,64,128]{2,1,0:T(8,128)}), f32[8,64,128]{2,1,0:T(8,128)S(1)}, u32[]{:S(2)}, u32[]{:S(2)}) %all-to-all-start.3) | async-done | bytes 262176 | tf_op jit(solution)/shard_map/all_to_all | solution.py:706
  80.0 2.2 %fourth.1 = (f32[8,64,128]{2,1,0:T(8,128)}, f32[8,128]{1,0:T(8,128)S(1)}) custom-call(f32[8,64,128]{2,1,0:T(8,128)S(1)} %all-to-all-done.3.got_ref, f32[128,512]{1,0:T(8,128)} %get-tuple-element.41.eta_hbm, f32[128,512]{1,0:T(8,128)} %get-tuple-element.42.curve_hbm, bf16[2,512,512]{2,1,0:T(8,128)(2,1)S(1)} %copy-done.1, f32[8,128]{1,0:T(8,128)S(1)} %get-tuple-element.48.token_ref), custom_call_target="tpu_custom_call" | custom-call | tf_op jit(solution)/shard_map/fourth/pallas_call | solution.py:683
  82.2 5.0 %all-to-all-start.4 = ((f32[8,64,128]{2,1,0:T(8,128)}), f32[8,64,128]{2,1,0:T(8,128)S(1)}, u32[]{:S(2)}, u32[]{:S(2)}) async-start(f32[8,64,128]{2,1,0:T(8,128)} %get-tuple-element.49), calls=%async_computation.4 | async-start | bytes 524288 | tf_op jit(solution)/shard_map/all_to_all | solution.py:706
  87.2 2.9 %early.1.early_hbm = f32[144,128]{1,0:T(8,128)} custom-call(s32[2]{0:T(128)S(1)} %pad_add_fusion.ids_ref, bf16[1096,2048]{1,0:T(8,128)(2,1)} %constant.17.clone.own_hbm, f32[64,1024]{1,0:T(8,128)} %get-tuple-element.50.first_hbm, f32[64,1024]{1,0:T(8,128)} %get-tuple-element.51.second_hbm, f32[8,128]{1,0:T(8,128)S(1)} %get-tuple-element.52.token_ref), custom_call_target="tpu_custom_call" | custom-call | tf_op jit(solution)/shard_map/early/pallas_call | solution.py:683
  90.1 3.6 %all-to-all-done.4.got_ref = f32[8,64,128]{2,1,0:T(8,128)S(1)} async-done(((f32[8,64,128]{2,1,0:T(8,128)}), f32[8,64,128]{2,1,0:T(8,128)S(1)}, u32[]{:S(2)}, u32[]{:S(2)}) %all-to-all-start.4) | async-done | bytes 262176 | tf_op jit(solution)/shard_map/all_to_all | solution.py:706
  93.7 2.8 %fifth.1.refs_0_ = f32[184,128]{1,0:T(8,128)} custom-call(s32[2]{0:T(128)S(1)} %pad_add_fusion.ids_ref, f32[8,64,128]{2,1,0:T(8,128)S(1)} %all-to-all-done.4.got_ref, bf16[4,512,512]{2,1,0:T(8,128)(2,1)S(1)} %copy-done, bf16[1096,2048]{1,0:T(8,128)(2,1)} %constant.17.clone.own_hbm, f32[64,1024]{1,0:T(8,128)} %get-tuple-element.50.first_hbm, ...), custom_call_target="tpu_custom_call" | custom-call | tf_op jit(solution)/shard_map/fifth/pallas_call | solution.py:683
  96.5 1.0 collective-permute-start.6
  97.4 1.2 %collective-permute-start.5 = (f32[184,128]{1,0:T(8,128)}, f32[184,128]{1,0:T(8,128)S(1)}, u32[]{:S(2)}, u32[]{:S(2)}) collective-permute-start(f32[184,128]{1,0:T(8,128)} %fifth.1.refs_0_), channel_id=1, source_target_pairs={{0,4},{1,5},{2,6},{3,7},{4,0},{5,1},{6,2},{7,3},{8,12},{9,13},{10,... | collective-permute-start | bytes 282632 | tf_op jit(solution)/shard_map/ppermute | solution.py:870
  98.7 0.0 collective-permute-start.4
  98.7 1.6 %collective-permute-start.7 = (f32[184,128]{1,0:T(8,128)}, f32[184,128]{1,0:T(8,128)S(1)}, u32[]{:S(2)}, u32[]{:S(2)}) collective-permute-start(f32[184,128]{1,0:T(8,128)} %fifth.1.refs_0_), channel_id=1, source_target_pairs={{0,1},{1,0},{2,3},{3,2},{4,5},{5,4},{6,7},{7,6},{8,9},{9,8},{10,11... | collective-permute-start | bytes 282632 | tf_op jit(solution)/shard_map/ppermute | solution.py:882
  100.3 0.0 collective-permute-done.6.refs_3_
  100.3 2.6 %collective-permute-start.10 = (f32[184,128]{1,0:T(8,128)S(1)}, f32[184,128]{1,0:T(8,128)S(1)}, u32[]{:S(2)}, u32[]{:S(2)}) collective-permute-start(f32[184,128]{1,0:T(8,128)S(1)} %collective-permute-done.6.refs_3_), channel_id=1, source_target_pairs={{0,1},{1,0},{2,3},{3,2},{4,5},{5,4},{6,7},{7,6},{8,9},{9,8},{10,11... | collective-permute-start | bytes 282632 | tf_op jit(solution)/shard_map/ppermute | solution.py:882
  102.9 0.0 collective-permute-done.5.refs_2_
  102.9 2.6 %collective-permute-start.9 = (f32[184,128]{1,0:T(8,128)S(1)}, f32[184,128]{1,0:T(8,128)S(1)}, u32[]{:S(2)}, u32[]{:S(2)}) collective-permute-start(f32[184,128]{1,0:T(8,128)S(1)} %collective-permute-done.5.refs_2_), channel_id=1, source_target_pairs={{0,1},{1,0},{2,3},{3,2},{4,5},{5,4},{6,7},{7,6},{8,9},{9,8},{10,11... | collective-permute-start | bytes 282632 | tf_op jit(solution)/shard_map/ppermute | solution.py:882
  105.5 0.0 collective-permute-done.4.refs_1_
  105.5 1.0 collective-permute-start.8
  106.5 0.0 collective-permute-done.7.refs_4_
  106.5 0.0 collective-permute-done.9.refs_6_
  106.5 0.9 collective-permute-done.8.refs_5_
  107.5 0.6 copy-done.11
  108.1 8.7 %last.1 = (f32[32,512]{1,0:T(8,128)}, f32[16,128]{1,0:T(8,128)}) custom-call(s32[2]{0:T(128)S(1)} %pad_add_fusion.ids_ref, s32[2,96]{1,0:T(2,128)S(1)} %bitcast.11, s32[1]{0:T(128)} %bitcast.8.count_ref, f32[184,128]{1,0:T(8,128)} %fifth.1.refs_0_, f32[184,128]{1,0:T(8,128)} %copy-done.7, f32[184,128]{1,0:T(8,128)} %copy-done.6, f32[184,128]{1,0:T(8,128)} %copy-done.5, ...), custom_call_target="tpu_custom_call" | custom-call | tf_op jit(solution)/shard_map/last/pallas_call | solution.py:683
  (28 shorter events, 0.1 us)
Async XLA Ops:
  0.6 31.2 %copy-start = (bf16[4,512,512]{2,1,0:T(8,128)(2,1)S(1)}, bf16[4,512,512]{2,1,0:T(8,128)(2,1)}, u32[]{:S(2)}) copy-start(bf16[4,512,512]{2,1,0:T(8,128)(2,1)} %constant.16.clone.x_ref) | copy-start | bytes 6291460
  0.7 50.7 %copy-start.1 = (bf16[2,512,512]{2,1,0:T(8,128)(2,1)S(1)}, bf16[2,512,512]{2,1,0:T(8,128)(2,1)}, u32[]{:S(2)}) copy-start(bf16[2,512,512]{2,1,0:T(8,128)(2,1)} %constant.15.clone.y_hbm.y_ref.refs_12_) | copy-start | bytes 3145732
  3.6 28.2 %all-to-all-start = ((f32[32,32,128]{2,1,0:T(8,128)}), f32[32,32,128]{2,1,0:T(8,128)}, u32[]{:S(2)}, u32[]{:S(2)}) async-start(f32[32,32,128]{2,1,0:T(8,128)} %start.1), calls=%async_computation | async-start | bytes 1048576 | tf_op jit(solution)/shard_map/all_to_all | solution.py:706
  18.6 3.5 %collective-permute-start = (f32[64,128]{1,0:T(8,128)}, f32[64,128]{1,0:T(8,128)S(1)}, u32[]{:S(2)}, u32[]{:S(2)}) collective-permute-start(f32[64,128]{1,0:T(8,128)} %get-tuple-element.30), channel_id=1, source_target_pairs={{0,1},{1,2},{2,3},{3,4},{4,5},{5,6},{6,7},{7,0},{8,9},{9,10},{10,1... | collective-permute-start | bytes 98312 | tf_op jit(solution)/shard_map/ppermute | solution.py:702
  20.8 4.0 %collective-permute-start.1 = (f32[64,128]{1,0:T(8,128)}, f32[64,128]{1,0:T(8,128)S(1)}, u32[]{:S(2)}, u32[]{:S(2)}) collective-permute-start(f32[64,128]{1,0:T(8,128)} %get-tuple-element.32), channel_id=1, source_target_pairs={{0,7},{1,0},{2,1},{3,2},{4,3},{5,4},{6,5},{7,6},{8,15},{9,8},{10,9... | collective-permute-start | bytes 98312 | tf_op jit(solution)/shard_map/ppermute | solution.py:702
  22.1 2.6 %copy-start.12 = (f32[64,128]{1,0:T(8,128)}, f32[64,128]{1,0:T(8,128)S(1)}, u32[]{:S(2)}) copy-start(f32[64,128]{1,0:T(8,128)S(1)} %collective-permute-done.below_hbm) | copy-start | bytes 98308
  24.7 0.6 copy-start.13
  27.1 14.8 %copy-start.14 = (f32[224,128]{1,0:T(8,128)S(1)}, f32[224,128]{1,0:T(8,128)}, u32[]{:S(2)}) copy-start(f32[224,128]{1,0:T(8,128)} %get-tuple-element.36) | copy-start | bytes 344068
  31.9 28.3 %copy-start.2 = (s32[1,1,2,96]{3,2,1,0:T(2,128)S(1)}, s32[1,1,2,96]{3,2,1,0:T(2,128)}, u32[]{:S(2)}) copy-start(s32[1,1,2,96]{3,2,1,0:T(2,128)} %param.13) | copy-start | bytes 2308
  35.0 16.5 %all-to-all-start.1 = ((f32[8,128,128]{2,1,0:T(8,128)}), f32[8,128,128]{2,1,0:T(8,128)}, u32[]{:S(2)}, u32[]{:S(2)}) async-start(f32[8,128,128]{2,1,0:T(8,128)} %get-tuple-element.34), calls=%async_computation.1 | async-start | bytes 1048576 | tf_op jit(solution)/shard_map/all_to_all | solution.py:706
  41.8 8.3 %collective-permute-start.3 = (f32[224,128]{1,0:T(8,128)S(1)}, f32[224,128]{1,0:T(8,128)S(1)}, u32[]{:S(2)}, u32[]{:S(2)}) collective-permute-start(f32[224,128]{1,0:T(8,128)S(1)} %copy-done.14), channel_id=1, source_target_pairs={{0,248},{8,0},{16,8},{24,16},{32,24},{40,32},{48,40},{56,48},{64,5... | collective-permute-start | bytes 344072 | tf_op jit(solution)/shard_map/ppermute | solution.py:702
  42.6 7.6 %collective-permute-start.2 = (f32[192,128]{1,0:T(8,128)}, f32[192,128]{1,0:T(8,128)S(1)}, u32[]{:S(2)}, u32[]{:S(2)}) collective-permute-start(f32[192,128]{1,0:T(8,128)} %get-tuple-element.35), channel_id=1, source_target_pairs={{0,8},{8,16},{16,24},{24,32},{32,40},{40,48},{48,56},{56,64},{64,7... | collective-permute-start | bytes 294920 | tf_op jit(solution)/shard_map/ppermute | solution.py:702
  50.1 1.3 %copy-start.4 = (f32[192,128]{1,0:T(8,128)}, f32[192,128]{1,0:T(8,128)S(1)}, u32[]{:S(2)}) copy-start(f32[192,128]{1,0:T(8,128)S(1)} %collective-permute-done.2.below_hbm.before_hbm.refs_8_) | copy-start | bytes 294916
  50.1 1.3 %copy-start.3 = (f32[224,128]{1,0:T(8,128)}, f32[224,128]{1,0:T(8,128)S(1)}, u32[]{:S(2)}) copy-start(f32[224,128]{1,0:T(8,128)S(1)} %collective-permute-done.3.above_hbm.after_hbm.refs_10_) | copy-start | bytes 344068
  54.4 11.6 %all-to-all-start.2 = ((f32[8,64,128]{2,1,0:T(8,128)}), f32[8,64,128]{2,1,0:T(8,128)S(1)}, u32[]{:S(2)}, u32[]{:S(2)}) async-start(f32[8,64,128]{2,1,0:T(8,128)} %get-tuple-element.37), calls=%async_computation.2 | async-start | bytes 524288 | tf_op jit(solution)/shard_map/all_to_all | solution.py:706
  68.6 11.4 %all-to-all-start.3 = ((f32[8,64,128]{2,1,0:T(8,128)}), f32[8,64,128]{2,1,0:T(8,128)S(1)}, u32[]{:S(2)}, u32[]{:S(2)}) async-start(f32[8,64,128]{2,1,0:T(8,128)} %get-tuple-element.40), calls=%async_computation.3 | async-start | bytes 524288 | tf_op jit(solution)/shard_map/all_to_all | solution.py:706
  82.2 11.5 %all-to-all-start.4 = ((f32[8,64,128]{2,1,0:T(8,128)}), f32[8,64,128]{2,1,0:T(8,128)S(1)}, u32[]{:S(2)}, u32[]{:S(2)}) async-start(f32[8,64,128]{2,1,0:T(8,128)} %get-tuple-element.49), calls=%async_computation.4 | async-start | bytes 524288 | tf_op jit(solution)/shard_map/all_to_all | solution.py:706
  96.5 3.8 %collective-permute-start.6 = (f32[184,128]{1,0:T(8,128)}, f32[184,128]{1,0:T(8,128)S(1)}, u32[]{:S(2)}, u32[]{:S(2)}) collective-permute-start(f32[184,128]{1,0:T(8,128)} %fifth.1.refs_0_), channel_id=1, source_target_pairs={{0,6},{1,7},{2,0},{3,1},{4,2},{5,3},{6,4},{7,5},{8,14},{9,15},{10,... | collective-permute-start | bytes 282632 | tf_op jit(solution)/shard_map/ppermute | solution.py:870
  97.4 5.5 %collective-permute-start.5 = (f32[184,128]{1,0:T(8,128)}, f32[184,128]{1,0:T(8,128)S(1)}, u32[]{:S(2)}, u32[]{:S(2)}) collective-permute-start(f32[184,128]{1,0:T(8,128)} %fifth.1.refs_0_), channel_id=1, source_target_pairs={{0,4},{1,5},{2,6},{3,7},{4,0},{5,1},{6,2},{7,3},{8,12},{9,13},{10,... | collective-permute-start | bytes 282632 | tf_op jit(solution)/shard_map/ppermute | solution.py:870
  98.7 6.9 %collective-permute-start.4 = (f32[184,128]{1,0:T(8,128)}, f32[184,128]{1,0:T(8,128)S(1)}, u32[]{:S(2)}, u32[]{:S(2)}) collective-permute-start(f32[184,128]{1,0:T(8,128)} %fifth.1.refs_0_), channel_id=1, source_target_pairs={{0,2},{1,3},{2,4},{3,5},{4,6},{5,7},{6,0},{7,1},{8,10},{9,11},{10,... | collective-permute-start | bytes 282632 | tf_op jit(solution)/shard_map/ppermute | solution.py:870
  98.7 7.8 %collective-permute-start.7 = (f32[184,128]{1,0:T(8,128)}, f32[184,128]{1,0:T(8,128)S(1)}, u32[]{:S(2)}, u32[]{:S(2)}) collective-permute-start(f32[184,128]{1,0:T(8,128)} %fifth.1.refs_0_), channel_id=1, source_target_pairs={{0,1},{1,0},{2,3},{3,2},{4,5},{5,4},{6,7},{7,6},{8,9},{9,8},{10,11... | collective-permute-start | bytes 282632 | tf_op jit(solution)/shard_map/ppermute | solution.py:882
  100.3 7.2 %copy-start.5 = (f32[184,128]{1,0:T(8,128)}, f32[184,128]{1,0:T(8,128)S(1)}, u32[]{:S(2)}) copy-start(f32[184,128]{1,0:T(8,128)S(1)} %collective-permute-done.6.refs_3_) | copy-start | bytes 282628
  100.3 6.2 %collective-permute-start.10 = (f32[184,128]{1,0:T(8,128)S(1)}, f32[184,128]{1,0:T(8,128)S(1)}, u32[]{:S(2)}, u32[]{:S(2)}) collective-permute-start(f32[184,128]{1,0:T(8,128)S(1)} %collective-permute-done.6.refs_3_), channel_id=1, source_target_pairs={{0,1},{1,0},{2,3},{3,2},{4,5},{5,4},{6,7},{7,6},{8,9},{9,8},{10,11... | collective-permute-start | bytes 282632 | tf_op jit(solution)/shard_map/ppermute | solution.py:882
  102.9 4.5 %copy-start.6 = (f32[184,128]{1,0:T(8,128)}, f32[184,128]{1,0:T(8,128)S(1)}, u32[]{:S(2)}) copy-start(f32[184,128]{1,0:T(8,128)S(1)} %collective-permute-done.5.refs_2_) | copy-start | bytes 282628
  102.9 3.6 %collective-permute-start.9 = (f32[184,128]{1,0:T(8,128)S(1)}, f32[184,128]{1,0:T(8,128)S(1)}, u32[]{:S(2)}, u32[]{:S(2)}) collective-permute-start(f32[184,128]{1,0:T(8,128)S(1)} %collective-permute-done.5.refs_2_), channel_id=1, source_target_pairs={{0,1},{1,0},{2,3},{3,2},{4,5},{5,4},{6,7},{7,6},{8,9},{9,8},{10,11... | collective-permute-start | bytes 282632 | tf_op jit(solution)/shard_map/ppermute | solution.py:882
  105.5 1.9 %copy-start.7 = (f32[184,128]{1,0:T(8,128)}, f32[184,128]{1,0:T(8,128)S(1)}, u32[]{:S(2)}) copy-start(f32[184,128]{1,0:T(8,128)S(1)} %collective-permute-done.4.refs_1_) | copy-start | bytes 282628
  105.5 1.9 %collective-permute-start.8 = (f32[184,128]{1,0:T(8,128)S(1)}, f32[184,128]{1,0:T(8,128)S(1)}, u32[]{:S(2)}, u32[]{:S(2)}) collective-permute-start(f32[184,128]{1,0:T(8,128)S(1)} %collective-permute-done.4.refs_1_), channel_id=1, source_target_pairs={{0,1},{1,0},{2,3},{3,2},{4,5},{5,4},{6,7},{7,6},{8,9},{9,8},{10,11... | collective-permute-start | bytes 282632 | tf_op jit(solution)/shard_map/ppermute | solution.py:882
  106.5 1.0 copy-start.8
  106.5 1.0 copy-start.9
  106.5 0.9 copy-start.10
  107.4 0.6 copy-start.11
